TPU v7x, 256 devices: a whole 4x4x8 slice. The times are simulated.
256 devices in a mesh: segment: 8 (over z_hi, core), dp: 32 (over y, z_lo, x).
Axes of the slice: x: 4, y: 4, z: 8 (z_hi: 4, z_lo: 2; z = z_hi * 2 + z_lo), core: 2. Of those that a mesh axis runs over, the one named last changes fastest.
Arguments:
- segment_input: bfloat16 [8, 4096, 1536], P('segment', 'dp'), may hold values from -6 to 6
- upstream_grad: bfloat16 [8, 4096, 1536], P('segment', 'dp'), may hold values from -6 to 6
- step_noise: bfloat16 [4096, 1536], P('dp'), may hold values from -6 to 6
- rewards: float32 [4096], P('dp'), may hold values from -4 to 4
- routes: int32 [8, 4096, 2], P('segment', 'dp'), may hold values from 0 to 7, all different within a row
- up_weight: bfloat16 [8, 1536, 24576], P('segment', None, 'dp'), may hold values from -0.15625 to 0.15625
- down_weight: bfloat16 [8, 24576, 1536], P('segment', 'dp'), may hold values from -0.109375 to 0.109375
- router_weight: bfloat16 [8, 1536, 8], P('segment'), may hold values from -0.15625 to 0.15625
- norm_gain: float32 [8, 1536], P('segment'), may hold values from 0.5 to 1.5
Outputs:
- input_grad: bfloat16 [8, 4096, 1536], P('segment', 'dp')
- up_grad: bfloat16 [8, 1536, 24576], P('segment', None, 'dp')
- down_grad: bfloat16 [8, 24576, 1536], P('segment', 'dp')
- router_grad: float32 [8, 1536, 8], P('segment')
- gain_grad: float32 [8, 1536], P('segment')
Inputs may be any that keep to these rules, and one draw needn't show every extreme that they name: `routes`: each token names 2 different experts in each layer.
All inputs are finite; a program needn't handle non-finite values.
Results may differ from a plain program's by a relative error of at most 0.0075.
Values may be sent and summed in bfloat16 or wider, within the bound.
No kernel may reach another device: no remote copies, remote signals or barrier semaphores. Data moves between devices by JAX's collectives and lax.ppermute only.
A program may use at most 128 MiB of HBM per device.

v0:
```python
import jax
import jax.numpy as jnp
from jax import lax
from jax.sharding import PartitionSpec as P

gelu_scale = 0.7978845608028654
cubic_coef = 0.044715
norm_eps = 1e-06


def from_behind(value, axis, steps):
    count = lax.axis_size(axis)
    first, last = (max(0, -steps), min(count, count - steps))
    return lax.ppermute(value, axis, [(source, source + steps) for source in range(first, last)])


def gelu_tanh(values):
    inner = gelu_scale * (values + cubic_coef * values * values * values)
    return 0.5 * values * (1.0 + jnp.tanh(inner))


def gelu_slope(values):
    inner = gelu_scale * (values + cubic_coef * values * values * values)
    tangent = jnp.tanh(inner)
    return 0.5 * (1.0 + tangent) + 0.5 * values * (1.0 - tangent * tangent) * gelu_scale * (
        1.0 + 3.0 * cubic_coef * values * values
    )


def shards(
    segment_input,
    upstream_grad,
    step_noise,
    rewards,
    routes,
    up_weight,
    down_weight,
    router_weight,
    norm_gain,
):
    n_dp = lax.axis_size("dp")
    n_segment = lax.axis_size("segment")
    tok_count = segment_input.shape[1]
    width = segment_input.shape[2]
    top_count = routes.shape[2]
    experts = router_weight.shape[2]
    split = n_dp // experts
    capacity = tok_count * top_count // experts
    up_local = up_weight[0]
    down_local = down_weight[0]
    router_local = router_weight[0]
    device_scale_grad = norm_gain[0]
    layer_routes = routes[0]
    arrived = from_behind(upstream_grad, "segment", -1)[0]
    own_grad = (-rewards[:, None] * step_noise.astype(jnp.float32)).astype(jnp.bfloat16)
    is_last = lax.axis_index("segment") == n_segment - 1
    cotangent = jnp.where(is_last, own_grad, arrived)
    input_widened_rows = segment_input[0].astype(jnp.float32)
    reciprocal_root_mean = lax.rsqrt(
        jnp.mean(input_widened_rows * input_widened_rows, -1, keepdims=True) + norm_eps
    )
    unit_norm_rows = input_widened_rows * reciprocal_root_mean
    rescaled_rows = (unit_norm_rows * device_scale_grad[None, :]).astype(jnp.bfloat16)
    logits = jnp.dot(rescaled_rows, router_local, preferred_element_type=jnp.float32)
    expert_ids = jnp.arange(experts, dtype=jnp.int32)
    onehot = (layer_routes[:, :, None] == expert_ids[None, None, :]).astype(jnp.float32)
    chosen = jnp.sum(logits[:, None, :] * onehot, -1)
    first_gate = jax.nn.sigmoid(chosen[:, 0] - chosen[:, 1])
    gates = jnp.stack([first_gate, 1.0 - first_gate], 1)
    flat_hot = (
        (layer_routes[:, :, None] == expert_ids[None, None, :])
        .astype(jnp.int32)
        .reshape(tok_count * top_count, experts)
    )
    before = jnp.cumsum(flat_hot, 0) - flat_hot
    position = jnp.sum(before * flat_hot, -1)
    expert_of_pair = layer_routes.reshape(-1)
    slot_index = jnp.where(
        position < capacity, expert_of_pair * capacity + position, experts * capacity
    )
    pair_ids = jnp.arange(tok_count * top_count, dtype=jnp.int32)
    pair_of_slot = (
        jnp.full((experts * capacity + 1,), tok_count * top_count, jnp.int32)
        .at[slot_index]
        .set(pair_ids)[: experts * capacity]
    )
    token_of_slot = pair_of_slot // top_count
    normed_pad = jnp.concatenate([rescaled_rows, jnp.zeros((1, width), jnp.bfloat16)], 0)
    cot_pad = jnp.concatenate([cotangent, jnp.zeros((1, width), jnp.bfloat16)], 0)
    gate_pad = jnp.concatenate([gates.reshape(-1), jnp.zeros((1,), jnp.float32)], 0)

    def spread(slot_rows):
        shaped = slot_rows.reshape((experts, 1) + slot_rows.shape[1:])
        widened = jnp.broadcast_to(shaped, (experts, split) + slot_rows.shape[1:])
        return widened.reshape((n_dp,) + slot_rows.shape[1:])

    sent_rows = spread(normed_pad[token_of_slot].reshape(experts, capacity, width))
    sent_cot = spread(cot_pad[token_of_slot].reshape(experts, capacity, width))
    sent_gate = spread(gate_pad[pair_of_slot].astype(jnp.bfloat16).reshape(experts, capacity))
    block_rows = lax.all_to_all(sent_rows, "dp", split_axis=0, concat_axis=0, tiled=True)
    lead = block_rows.shape[0]
    count = block_rows.shape[1]
    flat_rows = block_rows.reshape(-1, width)
    pre_act = jnp.dot(flat_rows, up_local, preferred_element_type=jnp.float32)
    hidden = gelu_tanh(pre_act).astype(jnp.bfloat16)
    partial_value = jnp.dot(hidden, down_local, preferred_element_type=jnp.float32).astype(
        jnp.bfloat16
    )
    got_rows, pre_act, hidden, partial_value = (
        block_rows,
        pre_act.reshape(lead, count, -1),
        hidden.reshape(lead, count, -1),
        partial_value.reshape(lead, count, width),
    )
    returned = lax.all_to_all(partial_value, "dp", split_axis=0, concat_axis=0, tiled=True)
    out_slots = jnp.sum(
        returned.astype(jnp.float32).reshape(experts, split, capacity, width), 1
    ).reshape(experts * capacity, width)
    got_cot, got_gate = (
        lax.all_to_all(sent_cot, "dp", split_axis=0, concat_axis=0, tiled=True),
        lax.all_to_all(sent_gate, "dp", split_axis=0, concat_axis=0, tiled=True),
    )
    flat_rows = got_rows.reshape(-1, width)
    flat_pre = pre_act.reshape(flat_rows.shape[0], -1)
    flat_hidden = hidden.reshape(flat_rows.shape[0], -1)
    scaled = (
        got_gate.reshape(-1, 1).astype(jnp.float32) * got_cot.reshape(-1, width).astype(jnp.float32)
    ).astype(jnp.bfloat16)
    down_g = jnp.einsum("rf,rd->fd", flat_hidden, scaled, preferred_element_type=jnp.float32)
    d_hidden = jnp.einsum("rd,fd->rf", scaled, down_local, preferred_element_type=jnp.float32)
    d_pre = (d_hidden * gelu_slope(flat_pre)).astype(jnp.bfloat16)
    up_g = jnp.einsum("rd,rf->df", flat_rows, d_pre, preferred_element_type=jnp.float32)
    back_part = jnp.einsum("rf,df->rd", d_pre, up_local, preferred_element_type=jnp.float32).astype(
        jnp.bfloat16
    )
    back_part = back_part.reshape(n_dp, capacity, width)
    cot_pair = jnp.broadcast_to(
        cotangent.astype(jnp.float32)[:, None, :], (tok_count, top_count, width)
    ).reshape(tok_count * top_count, width)
    back_recv = lax.all_to_all(back_part, "dp", split_axis=0, concat_axis=0, tiled=True)
    out_pad = jnp.concatenate([out_slots, jnp.zeros((1, width), jnp.float32)], 0)
    d_gate = jnp.sum(out_pad[slot_index] * cot_pair, -1).reshape(tok_count, top_count)
    back_slots = jnp.sum(
        back_recv.astype(jnp.float32).reshape(experts, split, capacity, width), 1
    ).reshape(experts * capacity, width)
    back_pad = jnp.concatenate([back_slots, jnp.zeros((1, width), jnp.float32)], 0)
    expert_dx = jnp.sum(back_pad[slot_index].reshape(tok_count, top_count, width), 1)
    d_logit = first_gate * (1.0 - first_gate) * (d_gate[:, 0] - d_gate[:, 1])
    d_logits = (onehot[:, 0, :] - onehot[:, 1, :]) * d_logit[:, None]
    router_part = jnp.dot(
        rescaled_rows.astype(jnp.float32).T, d_logits, precision=lax.Precision.HIGHEST
    )
    normed_cotangent = expert_dx + jnp.dot(
        d_logits, router_local.astype(jnp.float32).T, precision=lax.Precision.HIGHEST
    )
    scale_grad_piece = jnp.sum(normed_cotangent * unit_norm_rows, 0)
    router_total, gain_total = lax.psum((router_part, scale_grad_piece), "dp")
    unit_rows_grad = normed_cotangent * device_scale_grad[None, :]
    input_cotangent = reciprocal_root_mean * (
        unit_rows_grad
        - unit_norm_rows * jnp.mean(unit_rows_grad * unit_norm_rows, -1, keepdims=True)
    )
    input_g = (cotangent.astype(jnp.float32) + input_cotangent).astype(jnp.bfloat16)
    return (
        input_g[None],
        up_g.astype(jnp.bfloat16)[None],
        down_g.astype(jnp.bfloat16)[None],
        router_total[None],
        gain_total[None],
    )


def solution(mesh):
    placed = (
        P("segment", "dp", None),
        P("segment", "dp", None),
        P("dp", None),
        P("dp"),
        P("segment", "dp", None),
        P("segment", None, "dp"),
        P("segment", "dp", None),
        P("segment", None, None),
        P("segment", None),
    )
    return jax.shard_map(
        shards,
        mesh=mesh,
        in_specs=placed,
        out_specs=(
            P("segment", "dp", None),
            P("segment", None, "dp"),
            P("segment", "dp", None),
            P("segment", None, None),
            P("segment", None),
        ),
        check_vma=False,
    )
```

profile of v0, /device:TPU:64, one launch (start us, length us, event | category | flops | bytes accessed | tf_op | source)
XLA Modules:
  0.0 446.7 jit_solution(14017040828664969518)
XLA Ops:
  0.6 0.8 broadcast_multiply_fusion
  1.5 0.8 copy.44
  2.3 0.1 eq.53
  2.4 0.1 eq.49
  2.5 1.2 fusion.31
  3.7 0.1 copy.46
  3.8 0.1 mul.196
  4.0 0.6 reduce-window.6
  4.6 0.2 slice_reduce_fusion
  4.8 0.1 fusion.43
  5.0 1.4 scatter_custom_fusion
  6.4 0.7 reduce.4
  7.1 1.2 fusion.24
  8.3 2.1 gather_fusion.2
  10.4 1.5 broadcast_in_dim.74
  11.9 47.5 %all_to_all.29 = bf16[32,32,1536]{2,1,0:T(8,128)(2,1)S(1)} all-to-all(bf16[32,32,1536]{2,1,0:T(8,128)(2,1)S(1)} %bitcast.114), channel_id=1, replica_groups=mesh['segment'=8,'dp'=32] {'dp'}, dimensions={0} | all-to-all | bytes 6291456 | tf_op jit(solution)/shard_map/all_to_all | solution.py:100
  59.4 1.7 copy-done.5
  61.1 2.6 fusion.11
  63.7 4.1 convolution_convert_fusion
  67.9 5.8 %all-to-all-start.4 = ((bf16[32,32,1536]{2,1,0:T(8,128)(2,1)}), bf16[32,32,1536]{2,1,0:T(8,128)(2,1)}, u32[]{:S(2)}, u32[]{:S(2)}) async-start(bf16[32,32,1536]{2,1,0:T(8,128)(2,1)} %bitcast.119), calls=%async_computation.4 | async-start | bytes 6291456 | tf_op jit(solution)/shard_map/all_to_all | solution.py:115
  73.7 2.1 collective-permute-start
  75.9 0.3 fusion.38
  76.2 5.1 %collective-permute-done = bf16[1,128,1536]{2,1,0:T(8,128)(2,1)} collective-permute-done((bf16[1,128,1536]{2,1,0:T(8,128)(2,1)}, bf16[1,128,1536]{2,1,0:T(8,128)(2,1)}, u32[]{:S(2)}, u32[]{:S(2)}) %collective-permute-start) | collective-permute-done | bytes 393248 | tf_op jit(solution)/shard_map/ppermute | solution.py:14
  81.3 1.2 fusion.34
  82.5 0.7 copy-done.3
  83.2 1.5 broadcast_in_dim.75
  84.8 3.2 broadcast_in_dim.76
  88.0 28.6 %all-to-all-done.4 = bf16[32,32,1536]{2,1,0:T(8,128)(2,1)} async-done(((bf16[32,32,1536]{2,1,0:T(8,128)(2,1)}), bf16[32,32,1536]{2,1,0:T(8,128)(2,1)}, u32[]{:S(2)}, u32[]{:S(2)}) %all-to-all-start.4) | async-done | bytes 3145760 | tf_op jit(solution)/shard_map/all_to_all | solution.py:115
  116.5 2.6 convert_reduce_fusion
  119.1 1.3 concatenate.19
  120.4 4.5 %gather_fusion.4 = f32[256,1536]{1,0:T(8,128)} fusion(f32[257,1536]{1,0:T(8,128)} %concatenate.19, s32[1024]{0:T(1024)S(1)} %pad_clamp_fusion), kind=kCustom, calls=%fused_computation.4 | custom fusion | bytes 3146752 | tf_op jit(solution)/shard_map/gather | solution.py:142
  124.9 2.1 multiply_reduce_fusion
  127.0 0.1 reduce_sum.93
  127.4 0.1 copy.43
  127.6 0.2 reshape.209
  127.7 1.9 gather_fusion
  129.7 0.1 convert_element_type.120
  129.8 0.6 copy.47
  130.4 16.4 %all-to-all-start = ((bf16[32,1,32]{2,1,0:T(2,128)(2,1)}), bf16[32,1,32]{2,1,0:T(2,128)(2,1)S(1)}, u32[]{:S(2)}, u32[]{:S(2)}) async-start(bf16[32,1,32]{2,1,0:T(2,128)(2,1)} %copy.47), calls=%async_computation | async-start | bytes 32768 | tf_op jit(solution)/shard_map/all_to_all | solution.py:121
  146.8 1.0 concatenate.16
  147.8 2.1 gather_fusion.1
  150.0 5.0 %all-to-all-done = bf16[32,1,32]{2,1,0:T(2,128)(2,1)S(1)} async-done(((bf16[32,1,32]{2,1,0:T(2,128)(2,1)}), bf16[32,1,32]{2,1,0:T(2,128)(2,1)S(1)}, u32[]{:S(2)}, u32[]{:S(2)}) %all-to-all-start) | async-done | bytes 2080 | tf_op jit(solution)/shard_map/all_to_all | solution.py:121
  155.0 3.1 broadcast_in_dim.72
  158.1 4.8 %all-to-all-start.1 = ((bf16[32,32,1536]{2,1,0:T(8,128)(2,1)}), bf16[32,32,1536]{2,1,0:T(8,128)(2,1)}, u32[]{:S(2)}, u32[]{:S(2)}) async-start(bf16[32,32,1536]{2,1,0:T(8,128)(2,1)} %bitcast.113), calls=%async_computation.1 | async-start | bytes 6291456 | tf_op jit(solution)/shard_map/all_to_all | solution.py:120
  163.0 40.4 %all-to-all-done.1 = bf16[32,32,1536]{2,1,0:T(8,128)(2,1)} async-done(((bf16[32,32,1536]{2,1,0:T(8,128)(2,1)}), bf16[32,32,1536]{2,1,0:T(8,128)(2,1)}, u32[]{:S(2)}, u32[]{:S(2)}) %all-to-all-start.1) | async-done | bytes 3145760 | tf_op jit(solution)/shard_map/all_to_all | solution.py:120
  203.3 2.6 multiply_convert_fusion
  205.9 0.2 copy-done.13
  206.1 4.0 fusion.7
  210.2 4.2 convolution_convert_fusion.1
  214.3 10.0 %all-to-all-start.3 = ((bf16[32,32,1536]{2,1,0:T(8,128)(2,1)}), bf16[32,32,1536]{2,1,0:T(8,128)(2,1)}, u32[]{:S(2)}, u32[]{:S(2)}) async-start(bf16[32,32,1536]{2,1,0:T(8,128)(2,1)} %bitcast.120), calls=%async_computation.3 | async-start | bytes 6291456 | tf_op jit(solution)/shard_map/all_to_all | solution.py:140
  224.3 0.4 convolution_bitcast_fusion
  224.8 6.0 %fusion.8 = bf16[1,1536,768]{2,1,0:T(8,128)(2,1)} fusion(bf16[1024,1536]{1,0:T(8,128)(2,1)} %bitcast.118, bf16[1024,768]{1,0:T(8,128)(2,1)S(1)} %copy-done.16), kind=kOutput, calls=%fused_computation.25 | convolution fusion | flops 2417098752 | bytes 7077888 | tf_op jit(solution)/shard_map/rd,rf->df/dot_general | solution.py:132
  230.8 2.6 fusion
  233.4 0.2 copy-done.14
  233.6 4.0 fusion.9
  237.6 32.0 %all-to-all-done.3 = bf16[32,32,1536]{2,1,0:T(8,128)(2,1)} async-done(((bf16[32,32,1536]{2,1,0:T(8,128)(2,1)}), bf16[32,32,1536]{2,1,0:T(8,128)(2,1)}, u32[]{:S(2)}, u32[]{:S(2)}) %all-to-all-start.3) | async-done | bytes 3145760 | tf_op jit(solution)/shard_map/all_to_all | solution.py:140
  269.6 2.6 convert_reduce_fusion.1
  272.1 0.1 concatenate.18
  272.3 2.3 gather_fusion.3
  274.6 3.2 reshape.218
  277.8 4.2 reduce_sum.90
  282.0 2.7 fusion.30
  284.7 159.8 %all-reduce.4 = (f32[1,1536,8]{1,2,0:T(8,128)}, f32[1,1536]{1,0:T(1,128)}) all-reduce(f32[1,1536,8]{1,2,0:T(8,128)S(1)} %convolution_bitcast_fusion, f32[1,1536]{1,0:T(1,128)S(1)} %broadcast_in_dim.81), channel_id=1, replica_groups=mesh['segment'=8,'dp'=32] {'dp'}, use_global_device_ids=true, to_apply=%region_11.12 | all-reduce | flops 13824 | bytes 110592 | tf_op jit(solution)/shard_map/psum | solution.py:157
  444.5 2.2 fusion.36
  (57 shorter events, 0.7 us)
Async XLA Ops:
  0.6 63.1 %copy-start = (bf16[1,768,1536]{2,1,0:T(8,128)(2,1)S(1)}, bf16[1,768,1536]{2,1,0:T(8,128)(2,1)}, u32[]{:S(2)}) copy-start(bf16[1,768,1536]{2,1,0:T(8,128)(2,1)} %param.15) | copy-start | bytes 7077892
  11.9 49.2 %copy-start.9 = (bf16[1,1536,768]{2,1,0:T(8,128)(2,1)S(1)}, bf16[1,1536,768]{2,1,0:T(8,128)(2,1)}, u32[]{:S(2)}) copy-start(bf16[1,1536,768]{2,1,0:T(8,128)(2,1)} %param.14) | copy-start | bytes 7077892
  59.4 1.7 copy-start.5
  63.7 4.2 copy-start.12
  67.9 8.0 %copy-start.11 = (f32[128]{0:T(128)S(1)}, f32[128]{0:T(128)}, u32[]{:S(2)}) copy-start(f32[128]{0:T(128)} %param.12) | copy-start | bytes 1540
  67.9 8.0 %copy-start.2 = (bf16[1,128,1536]{2,1,0:T(8,128)(2,1)S(1)}, bf16[1,128,1536]{2,1,0:T(8,128)(2,1)}, u32[]{:S(2)}) copy-start(bf16[1,128,1536]{2,1,0:T(8,128)(2,1)} %param.9) | copy-start | bytes 1179652
  67.9 8.0 %copy-start.7 = (bf16[1,1536,8]{1,2,0:T(8,128)(2,1)S(1)}, bf16[1,1536,8]{1,2,0:T(8,128)(2,1)}, u32[]{:S(2)}) copy-start(bf16[1,1536,8]{1,2,0:T(8,128)(2,1)} %param.16) | copy-start | bytes 73732
  67.9 8.3 %copy-start.8 = (s32[1,128,2]{1,2,0:T(2,128)S(1)}, s32[1,128,2]{1,2,0:T(2,128)}, u32[]{:S(2)}) copy-start(s32[1,128,2]{1,2,0:T(2,128)} %param.13) | copy-start | bytes 3076
  67.9 13.4 %copy-start.6 = (bf16[128,1536]{1,0:T(8,128)(2,1)S(1)}, bf16[128,1536]{1,0:T(8,128)(2,1)}, u32[]{:S(2)}) copy-start(bf16[128,1536]{1,0:T(8,128)(2,1)} %param.11) | copy-start | bytes 1179652
  67.9 48.6 %all-to-all-start.4 = ((bf16[32,32,1536]{2,1,0:T(8,128)(2,1)}), bf16[32,32,1536]{2,1,0:T(8,128)(2,1)}, u32[]{:S(2)}, u32[]{:S(2)}) async-start(bf16[32,32,1536]{2,1,0:T(8,128)(2,1)} %bitcast.119), calls=%async_computation.4 | async-start | bytes 6291456 | tf_op jit(solution)/shard_map/all_to_all | solution.py:115
  73.7 7.6 %collective-permute-start = (bf16[1,128,1536]{2,1,0:T(8,128)(2,1)}, bf16[1,128,1536]{2,1,0:T(8,128)(2,1)}, u32[]{:S(2)}, u32[]{:S(2)}) collective-permute-start(bf16[1,128,1536]{2,1,0:T(8,128)(2,1)} %param.10), channel_id=1, source_target_pairs={{32,0},{64,32},{96,64},{128,96},{160,128},{192,160},{224,192},{33,... | collective-permute-start | bytes 1179656 | tf_op jit(solution)/shard_map/ppermute | solution.py:14
  82.5 0.7 copy-start.3
  130.4 24.6 %all-to-all-start = ((bf16[32,1,32]{2,1,0:T(2,128)(2,1)}), bf16[32,1,32]{2,1,0:T(2,128)(2,1)S(1)}, u32[]{:S(2)}, u32[]{:S(2)}) async-start(bf16[32,1,32]{2,1,0:T(2,128)(2,1)} %copy.47), calls=%async_computation | async-start | bytes 32768 | tf_op jit(solution)/shard_map/all_to_all | solution.py:121
  158.1 45.2 %all-to-all-start.1 = ((bf16[32,32,1536]{2,1,0:T(8,128)(2,1)}), bf16[32,32,1536]{2,1,0:T(8,128)(2,1)}, u32[]{:S(2)}, u32[]{:S(2)}) async-start(bf16[32,32,1536]{2,1,0:T(8,128)(2,1)} %bitcast.113), calls=%async_computation.1 | async-start | bytes 6291456 | tf_op jit(solution)/shard_map/all_to_all | solution.py:120
  203.3 2.8 copy-start.13
  206.1 4.0 copy-start.10
  210.1 4.2 copy-start.15
  214.3 10.5 %copy-start.16 = (bf16[1024,768]{1,0:T(8,128)(2,1)S(1)}, bf16[1024,768]{1,0:T(8,128)(2,1)}, u32[]{:S(2)}) copy-start(bf16[1024,768]{1,0:T(8,128)(2,1)} %copy-done.15) | copy-start | bytes 4718596
  214.3 55.3 %all-to-all-start.3 = ((bf16[32,32,1536]{2,1,0:T(8,128)(2,1)}), bf16[32,32,1536]{2,1,0:T(8,128)(2,1)}, u32[]{:S(2)}, u32[]{:S(2)}) async-start(bf16[32,32,1536]{2,1,0:T(8,128)(2,1)} %bitcast.120), calls=%async_computation.3 | async-start | bytes 6291456 | tf_op jit(solution)/shard_map/all_to_all | solution.py:140
  230.8 2.8 copy-start.14
  274.6 169.8 %copy-start.4 = (bf16[128,1536]{1,0:T(8,128)(2,1)S(1)}, bf16[128,1536]{1,0:T(8,128)(2,1)}, u32[]{:S(2)}) copy-start(bf16[128,1536]{1,0:T(8,128)(2,1)} %copy-done.3) | copy-start | bytes 1179652
  274.6 172.1 %copy-start.1 = (bf16[1,768,1536]{2,1,0:T(8,128)(2,1)S(1)}, bf16[1,768,1536]{2,1,0:T(8,128)(2,1)}, u32[]{:S(2)}) copy-start(bf16[1,768,1536]{2,1,0:T(8,128)(2,1)} %param.15) | copy-start | bytes 7077892
where the time goes:
time: 447 us
  blocking collectives  207 us (46%)
  waiting for transfers between devices  111 us (25%)
  starting transfers between devices  39.1 us (9%)
  local copies, waits for them, and re-layouts  35.4 us (8%)
  matrix products  28.2 us (6%)
  other arithmetic  24.8 us (6%)
    psum x1, blocking collectives, shards(): router_total, gain_total = lax.psum((router_part, scale_grad_piece), 'dp')  160 us
    all_to_all x1, blocking collectives, shards(): lax.all_to_all(sent_rows, 'dp', split_axis=0, concat_axis=0, tiled=True)  47.5 us
    all_to_all x1, waiting for transfers between devices, shards(): lax.all_to_all(sent_cot, 'dp', split_axis=0, concat_axis=0, tiled=True)  40.4 us
    all_to_all x1, waiting for transfers between devices, shards(): lax.all_to_all(back_part, 'dp', split_axis=0, concat_axis=0, tiled=True)  32 us
    all_to_all x1, waiting for transfers between devices, shards(): lax.all_to_all(partial_value, 'dp', split_axis=0, concat_axis=0, tiled=True)  28.6 us
    all_to_all x1, starting transfers between devices, shards(): lax.all_to_all(sent_gate, 'dp', split_axis=0, concat_axis=0, tiled=True)  16.4 us
    all_to_all x1, starting transfers between devices, shards(): lax.all_to_all(back_part, 'dp', split_axis=0, concat_axis=0, tiled=True)  9.96 us
  transfers between devices with their start and end apart: 5, of which 5 were waited for; matrix products, arithmetic and copies ran while one was open for 5% of the time, Pallas kernels for 0%

commit v1 on v0

v1 whole, which is shorter than its diff:
```python
import jax
import jax.numpy as jnp
from jax import lax
from jax.sharding import Mesh, PartitionSpec as P

gelu_scale = 0.7978845608028654
cubic_coef = 0.044715
norm_eps = 1e-06
bf16 = jnp.bfloat16
f32 = jnp.float32


def shift(value, axis, steps):
    count = lax.axis_size(axis)
    return lax.ppermute(value, axis, [(i, (i + steps) % count) for i in range(count)])


def swap(value, axis, mask):
    count = lax.axis_size(axis)
    return lax.ppermute(value, axis, [(i, i ^ mask) for i in range(count)])


def total_over(value):
    for axis in ("x", "e"):
        mask = 1
        while mask < lax.axis_size(axis):
            value = value + swap(value, axis, mask)
            mask *= 2
    return value


def dot(a, b, dims):
    return lax.dot_general(a, b, (dims, ((), ())), preferred_element_type=f32)


def gather_x(rows):
    half = rows.shape[0] // 2
    low = shift(rows, "x", 1)
    high = shift(rows, "x", -1)
    far_low = shift(low[:half], "x", 1)
    far_high = shift(high[half:], "x", -1)
    return [rows, low, high, far_low, far_high]


def scatter_x(parts):
    own, low, high, far_low, far_high = parts
    half = own.shape[0] // 2
    got_low = shift(far_low.astype(bf16), "x", -1)
    got_high = shift(far_high.astype(bf16), "x", 1)
    low_b = shift(low[half:].astype(bf16), "x", -1)
    high_a = shift(high[:half].astype(bf16), "x", 1)
    high_b = shift((high[half:] + got_high.astype(f32)).astype(bf16), "x", 1)
    low_a = shift((low[:half] + got_low.astype(f32)).astype(bf16), "x", -1)
    first = own[:half] + high_a.astype(f32) + low_a.astype(f32)
    second = own[half:] + high_b.astype(f32) + low_b.astype(f32)
    return jnp.concatenate([first.astype(bf16), second.astype(bf16)], 0)


def relative(table):
    count = table.shape[1]
    here = lax.axis_index("x")
    steps = jnp.array([0, -1, 1, 2], jnp.int32)
    place = (here + steps) % count
    pick = (place[:, None] == jnp.arange(count)[None, :]).astype(f32)
    return pick


def shards(
    segment_input,
    upstream_grad,
    step_noise,
    rewards,
    routes,
    up_weight,
    down_weight,
    router_weight,
    norm_gain,
):
    tok_count = segment_input.shape[1]
    width = segment_input.shape[2]
    experts = router_weight.shape[2]
    split = lax.axis_size("x")
    top_count = routes.shape[2]
    capacity = tok_count * top_count // experts
    slots = experts * capacity
    up = up_weight[0]
    down = down_weight[0]
    router = router_weight[0]
    gain = norm_gain[0]
    n_segment = lax.axis_size("segment")
    arrived = lax.ppermute(
        upstream_grad[0], "segment", [(i + 1, i) for i in range(n_segment - 1)]
    )
    own_grad = (-rewards[:, None] * step_noise.astype(f32)).astype(bf16)
    is_last = lax.axis_index("segment") == n_segment - 1
    cot = jnp.where(is_last, own_grad, arrived)

    x32 = segment_input[0].astype(f32)
    inv = lax.rsqrt(jnp.mean(x32 * x32, -1, keepdims=True) + norm_eps)
    xh = x32 * inv
    xn = (xh * gain[None, :]).astype(bf16)
    logits = dot(router, xn, ((0,), (1,)))
    ids = jnp.arange(experts, dtype=jnp.int32)[:, None]
    first = (routes[0, :, 0][None, :] == ids).astype(f32)
    second = (routes[0, :, 1][None, :] == ids).astype(f32)
    named = first + second
    g1 = jax.nn.sigmoid(
        jnp.sum(first * logits, 0, keepdims=True) - jnp.sum(second * logits, 0, keepdims=True)
    )
    gates = first * g1 + second * (1.0 - g1)
    earlier = (jnp.arange(tok_count)[:, None] < jnp.arange(tok_count)[None, :]).astype(bf16)
    place = dot(named.astype(bf16), earlier, ((1,), (0,)))
    place = jnp.where(named > 0, place, -1.0)
    chosen = place[:, None, :] == jnp.arange(capacity, dtype=f32)[None, :, None]
    pick = chosen.astype(bf16).reshape(slots, tok_count)
    gate_slot = jnp.sum(jnp.where(chosen, gates[:, None, :], 0.0), -1)

    xn_slots = dot(pick, xn, ((1,), (0,))).astype(bf16).reshape(experts, capacity, width)
    c_slots = dot(pick, cot, ((1,), (0,))).astype(bf16).reshape(experts, capacity, width)
    xn_got = lax.all_to_all(xn_slots, "e", 0, 0, tiled=True).reshape(slots, width)
    xn_parts = gather_x(xn_got)
    c_got = lax.all_to_all(c_slots, "e", 0, 0, tiled=True).reshape(slots, width)
    c_parts = gather_x(c_got)

    spread = jnp.broadcast_to(gate_slot[:, None, :], (experts, split, capacity)).reshape(
        experts * split, capacity
    )
    gate_got = lax.all_to_all(spread, ("e", "x"), 0, 0, tiled=True)
    gate_got = gate_got.reshape(experts, split, capacity)
    turn = relative(gate_got)
    gate_rel = jnp.einsum(
        "rx,exc->rec", turn, gate_got, precision=lax.Precision.HIGHEST
    ).reshape(split * slots)

    hs, ds, backs, dgs = [], [], [], []
    for xn_c, c_c in zip(xn_parts, c_parts):
        pre = dot(xn_c, up, ((1,), (0,)))
        square = pre * pre
        tangent = jnp.tanh(gelu_scale * pre * (1.0 + cubic_coef * square))
        hidden = (0.5 * pre * (1.0 + tangent)).astype(bf16)
        slope = 0.5 * (1.0 + tangent) + 0.5 * pre * (1.0 - tangent * tangent) * gelu_scale * (
            1.0 + 3.0 * cubic_coef * square
        )
        dh = dot(c_c, down, ((1,), (1,)))
        dgs.append(jnp.sum(hidden.astype(f32) * dh, -1))
        d_pre = (dh * slope).astype(bf16)
        backs.append(dot(d_pre, up, ((1,), (1,))))
        hs.append(hidden)
        ds.append(d_pre)
    half = slots // 2
    dg = jnp.concatenate(dgs, 0).reshape(split, experts, capacity)
    dg_abs = jnp.einsum("rx,rec->exc", turn, dg, precision=lax.Precision.HIGHEST)
    dg_got = lax.all_to_all(
        dg_abs.reshape(experts * split, capacity), ("e", "x"), 0, 0, tiled=True
    )
    dg_slot = jnp.sum(dg_got.reshape(experts, split, capacity), 1)

    back = scatter_x(backs).reshape(experts, capacity, width)
    back_slots = lax.all_to_all(back, "e", 0, 0, tiled=True).reshape(slots, width)

    gate_col = gate_rel[:, None]
    h_all = (jnp.concatenate(hs, 0).astype(f32) * gate_col).astype(bf16)
    d_all = (jnp.concatenate(ds, 0).astype(f32) * gate_col).astype(bf16)
    xn_all = jnp.concatenate(xn_parts, 0)
    c_all = jnp.concatenate(c_parts, 0)
    down_g = dot(h_all, c_all, ((0,), (0,)))
    up_g = dot(xn_all, d_all, ((0,), (0,)))
    gain_part = jnp.sum(up_g * up.astype(f32), 1)

    dg_tok = jnp.sum(jnp.where(chosen, dg_slot[:, :, None], 0.0), 1)
    dl = g1 * (1.0 - g1) * jnp.sum((first - second) * dg_tok, 0, keepdims=True)
    d_logits = (first - second) * dl
    router_part = lax.dot_general(
        d_logits,
        xn.astype(f32),
        (((1,), (0,)), ((), ())),
        precision=lax.Precision.HIGHEST,
    )
    small = total_over(jnp.concatenate([router_part, gain_part[None, :]], 0))
    router_total = small[:experts]
    router32 = router.astype(f32)
    gain_total = (small[experts] + jnp.sum(router_total * router32.T, 0)) / gain

    weigh = jnp.where(chosen, gates[:, None, :], 0.0).astype(bf16).reshape(slots, tok_count)
    dxe = dot(weigh, back_slots, ((0,), (0,)))
    dxn = dxe + lax.dot_general(
        d_logits, router32, (((0,), (1,)), ((), ())), precision=lax.Precision.HIGHEST
    )
    dh_row = dxn * gain[None, :]
    input_g = cot.astype(f32) + inv * (
        dh_row - xh * jnp.mean(dh_row * xh, -1, keepdims=True)
    )
    return (
        input_g.astype(bf16)[None],
        up_g.astype(bf16)[None],
        down_g.astype(bf16)[None],
        router_total.T[None],
        gain_total[None],
    )


def solution(mesh):
    experts = 8
    n_segment, n_dp = mesh.devices.shape
    grid = Mesh(
        mesh.devices.reshape(n_segment, experts, n_dp // experts), ("segment", "e", "x")
    )
    dp = ("e", "x")
    return jax.shard_map(
        shards,
        mesh=grid,
        in_specs=(
            P("segment", dp, None),
            P("segment", dp, None),
            P(dp, None),
            P(dp),
            P("segment", dp, None),
            P("segment", None, dp),
            P("segment", dp, None),
            P("segment", None, None),
            P("segment", None),
        ),
        out_specs=(
            P("segment", dp, None),
            P("segment", None, dp),
            P("segment", dp, None),
            P("segment", None, None),
            P("segment", None),
        ),
        check_vma=False,
    )
```

time: 447 us -> 204 us (0.46)
  blocking collectives: 207 us -> 0 us
  waiting for transfers between devices: 111 us -> 30.8 us
  matrix products: 28.2 us -> 49.7 us
  starting transfers between devices: 39.1 us -> 60 us
    psum x1 -> x0, blocking collectives: 160 us -> none  [shards(): router_total, gain_total = lax.psum((router_part, scale_grad_piece), 'dp')]
    all_to_all x4 -> x5, waiting for transfers between devices: 106 us -> 15.8 us  [the longest x1 7 us: shards(): lax.all_to_all(xn_slots, 'e', 0, 0, tiled=True).reshape(slots, width)]
    all_to_all x1 -> x0, blocking collectives: 47.5 us -> none  [shards(): lax.all_to_all(sent_rows, 'dp', split_axis=0, concat_axis=0, tiled=True)]
    ppermute x1 -> x20, starting transfers between devices: 2.1 us -> 30.8 us  [the longest x14 22 us: shift(): lax.ppermute(value, axis, [(i, (i + steps) % count) for i in range(count)])]
    dot_general x9 -> x26, matrix products: 28.2 us -> 49.7 us  [the longest x22 44.1 us: dot(): return lax.dot_general(a, b, (dims, ((), ())), preferred_element_type=f32)]
    unnamed x37 -> x68, local copies, waits for them, and re-layouts: 3.87 us -> 24.4 us
    gather x5 -> x0, local copies, waits for them, and re-layouts: 13.1 us -> none  [the longest x1 4.51 us: shards(): out_pad[slot_index] * cot_pair]
    ppermute x1 -> x20, waiting for transfers between devices: 5.07 us -> 14.9 us  [the longest x14 8.89 us: shift(): lax.ppermute(value, axis, [(i, (i + steps) % count) for i in range(count)])]
  transfers between devices with their start and end apart: 5 -> 25, of which waited for: 5 -> 10; matrix products, arithmetic and copies ran while one was open for 5% -> 49% of each run, Pallas kernels for 0% -> 0%
where the time goes in v1:
time: 204 us; the launch traced here: 200 us
  starting transfers between devices  60 us (29%)
  matrix products  49.7 us (24%)
  local copies, waits for them, and re-layouts  36.1 us (18%)
  waiting for transfers between devices  30.8 us (15%)
  other arithmetic  22.3 us (11%)
    dot_general x22, matrix products, dot(): return lax.dot_general(a, b, (dims, ((), ())), preferred_element_type=f32)  44.1 us
    unnamed x68, local copies, waits for them, and re-layouts  24.4 us
    ppermute x14, starting transfers between devices, shift(): lax.ppermute(value, axis, [(i, (i + steps) % count) for i in range(count)])  22 us
    ppermute x14, waiting for transfers between devices, shift(): lax.ppermute(value, axis, [(i, (i + steps) % count) for i in range(count)])  8.89 us
    all_to_all x1, starting transfers between devices, shards(): c_got = lax.all_to_all(c_slots, 'e', 0, 0, tiled=True).reshape(slots, width)  7.94 us
    all_to_all x1, waiting for transfers between devices, shards(): lax.all_to_all(xn_slots, 'e', 0, 0, tiled=True).reshape(slots, width)  7 us
    ppermute x5, starting transfers between devices, swap(): return lax.ppermute(value, axis, [(i, i ^ mask) for i in range(count)])  6.94 us
    all_to_all x1, starting transfers between devices, shards(): lax.all_to_all(dg_abs.reshape(experts * split, capacity), ('e', 'x'), 0,...  6.83 us
  transfers between devices with their start and end apart: 25, of which 10 were waited for; matrix products, arithmetic and copies ran while one was open for 49% of the time, Pallas kernels for 0%

profile of v1, /device:TPU:64, one launch (start us, length us, event | category | flops | bytes accessed | tf_op | source)
XLA Modules:
  0.0 200.1 jit_solution(1961322490890092340)
XLA Ops:
  2.3 1.2 fusion.44
  4.2 2.3 %convolution_convert_fusion.1 = bf16[256,1536]{1,0:T(8,128)(2,1)} fusion(pred[256,128]{1,0:T(32,128)(4,1)S(1)} %bitcast.170, bf16[1,128,1536]{2,1,0:T(8,128)(2,1)} %param.10, f32[1536]{0:T(1024)S(1)} %reduce, f32[128]{0:T(128)S(1)} %add_rsqrt_fusion), kind=kOutput, calls=%fused_computation.5 | convolution fusion | flops 101842944 | bytes 1219072 | tf_op jit(solution)/shard_map/dot_general | solution.py:33
  6.5 5.8 %all-to-all-start.1 = ((bf16[8,32,1536]{2,1,0:T(8,128)(2,1)}), bf16[8,32,1536]{2,1,0:T(8,128)(2,1)S(1)}, u32[]{:S(2)}, u32[]{:S(2)}) async-start(bf16[8,32,1536]{2,1,0:T(8,128)(2,1)} %bitcast.168), calls=%async_computation.1 | async-start | bytes 1572864 | tf_op jit(solution)/shard_map/all_to_all | solution.py:120
  12.3 1.9 collective-permute-start
  15.5 4.3 %copy.23 = bf16[1,1536,768]{1,2,0:T(8,128)(2,1)} copy(bf16[1,1536,768]{2,1,0:T(8,128)(2,1)} %param.15) | data formatting | bytes 4718592 | tf_op args[5]
  19.9 2.5 %convolution_convert_fusion.2 = bf16[256,1536]{1,0:T(8,128)(2,1)} fusion(pred[256,128]{1,0:T(32,128)(4,1)} %bitcast_compare_fusion, bf16[128,1536]{1,0:T(8,128)(2,1)} %collective-permute-done, bf16[128,1536]{1,0:T(8,128)(2,1)} %param.12, f32[128]{0:T(128)} %neg.18, pred[]{:T(512)S(6)} %eq.89), kind=kOutput, calls=%fused_computation.6 | convolution fusion | flops 101842944 | bytes 1606145 | tf_op jit(solution)/shard_map/dot_general | solution.py:33
  22.4 7.0 %all-to-all-done.1 = bf16[8,32,1536]{2,1,0:T(8,128)(2,1)S(1)} async-done(((bf16[8,32,1536]{2,1,0:T(8,128)(2,1)}), bf16[8,32,1536]{2,1,0:T(8,128)(2,1)S(1)}, u32[]{:S(2)}, u32[]{:S(2)}) %all-to-all-start.1) | async-done | bytes 786464 | tf_op jit(solution)/shard_map/all_to_all | solution.py:120
  29.4 7.9 %all-to-all-start = ((bf16[8,32,1536]{2,1,0:T(8,128)(2,1)}), bf16[8,32,1536]{2,1,0:T(8,128)(2,1)}, u32[]{:S(2)}, u32[]{:S(2)}) async-start(bf16[8,32,1536]{2,1,0:T(8,128)(2,1)} %bitcast.169), calls=%async_computation | async-start | bytes 1572864 | tf_op jit(solution)/shard_map/all_to_all | solution.py:122
  38.4 1.2 and_select_fusion
  40.3 1.5 collective-permute-start.5
  41.8 1.7 collective-permute-start.2
  44.5 3.3 %fusion.18 = f32[256,768]{1,0:T(8,128)} fusion(bf16[256,1536]{1,0:T(8,128)(2,1)S(1)} %bitcast.166, bf16[1,1536,768]{2,1,0:T(8,128)(2,1)} %param.15), kind=kOutput, calls=%fused_computation.28 | convolution fusion | flops 603979776 | bytes 3932160 | tf_op jit(solution)/shard_map/dot_general | solution.py:33
  47.8 1.6 all-to-all-done
  49.4 1.5 collective-permute-start.4
  50.9 1.7 collective-permute-start.1
  52.6 2.4 %constant_dynamic-update-slice_fusion.10 = (bf16[1024,768]{1,0:T(8,128)(2,1)S(1)}, bf16[256,768]{1,0:T(8,128)(2,1)S(1)}, bf16[1024,768]{1,0:T(8,128)(2,1)S(1)}, f32[256,768]{1,0:T(8,128)S(1)}) fusion(f32[256,768]{1,0:T(8,128)} %fusion.18, bf16[256,1536]{1,0:T(8,128)(2,1)} %bitcast.9, bf16[1,768,1536]{2,1,0:T(8,128)(2,1)S(1)} %copy-done), kind=kOutput, calls=%fused_computation.125 | convolution fusion | flops 607911936 | bytes 5898240 | tf_op jit(solution)/shard_map/dot_general | solution.py:33
  55.4 1.5 constant_dynamic-update-slice_fusion
  56.9 1.2 constant_dynamic-update-slice_fusion.20
  58.1 1.9 fusion.16
  62.5 3.0 %collective-permute-start.11 = (bf16[128,1536]{1,0:T(8,128)(2,1)S(1)}, bf16[128,1536]{1,0:T(8,128)(2,1)S(1)}, u32[]{:S(2)}, u32[]{:S(2)}) collective-permute-start(bf16[128,1536]{1,0:T(8,128)(2,1)S(1)} %slice.66), channel_id=1, source_target_pairs={{0,3},{1,0},{2,1},{3,2},{4,7},{5,4},{6,5},{7,6},{8,11},{9,8},{10,9... | collective-permute-start | bytes 1179656 | tf_op jit(solution)/shard_map/ppermute | solution.py:15
  65.5 1.9 fusion.10
  67.4 2.1 %constant_dynamic-update-slice_fusion.4 = bf16[1024,1536]{1,0:T(8,128)(2,1)} fusion(bf16[1024,1536]{1,0:T(8,128)(2,1)} %constant_dynamic-update-slice_fusion.5, bf16[256,1536]{1,0:T(8,128)(2,1)} %collective-permute-done.5), kind=kLoop, calls=%fused_computation.119 | loop fusion | bytes 1572864
  69.5 1.9 fusion.14
  71.4 2.1 %constant_dynamic-update-slice_fusion.3 = bf16[1024,1536]{1,0:T(8,128)(2,1)} fusion(bf16[1024,1536]{1,0:T(8,128)(2,1)} %constant_dynamic-update-slice_fusion.4, bf16[256,1536]{1,0:T(8,128)(2,1)} %collective-permute-done.2), kind=kLoop, calls=%fused_computation.118 | loop fusion | bytes 1572864
  73.5 2.6 %collective-permute-done.4 = bf16[256,1536]{1,0:T(8,128)(2,1)S(1)} collective-permute-done((bf16[256,1536]{1,0:T(8,128)(2,1)}, bf16[256,1536]{1,0:T(8,128)(2,1)S(1)}, u32[]{:S(2)}, u32[]{:S(2)}) %collective-permute-start.4) | collective-permute-done | bytes 786464 | tf_op jit(solution)/shard_map/ppermute | solution.py:15
  78.1 3.0 %collective-permute-start.10 = (bf16[128,1536]{1,0:T(8,128)(2,1)S(1)}, bf16[128,1536]{1,0:T(8,128)(2,1)S(1)}, u32[]{:S(2)}, u32[]{:S(2)}) collective-permute-start(bf16[128,1536]{1,0:T(8,128)(2,1)S(1)} %slice.65), channel_id=1, source_target_pairs={{0,3},{1,0},{2,1},{3,2},{4,7},{5,4},{6,5},{7,6},{8,11},{9,8},{10,9... | collective-permute-start | bytes 1179656 | tf_op jit(solution)/shard_map/ppermute | solution.py:15
  85.5 3.2 %collective-permute-start.14 = (bf16[128,1536]{1,0:T(8,128)(2,1)}, bf16[128,1536]{1,0:T(8,128)(2,1)}, u32[]{:S(2)}, u32[]{:S(2)}) collective-permute-start(bf16[128,1536]{1,0:T(8,128)(2,1)} %slice.95), channel_id=1, source_target_pairs={{0,3},{1,0},{2,1},{3,2},{4,7},{5,4},{6,5},{7,6},{8,11},{9,8},{10,9... | collective-permute-start | bytes 1179656 | tf_op jit(solution)/shard_map/ppermute | solution.py:15
  89.5 1.3 constant_dynamic-update-slice_fusion.24
  92.1 1.3 constant_dynamic-update-slice_fusion.23
  93.9 1.6 constant_dynamic-update-slice_fusion.7
  95.7 1.6 constant_dynamic-update-slice_fusion.6
  97.6 1.4 constant_dynamic-update-slice_fusion.22
  99.1 1.3 constant_dynamic-update-slice_fusion.21
  100.4 1.4 reshape.229
  101.7 1.6 fusion.68
  103.3 6.8 %all-to-all-start.3 = ((f32[32,1,32]{2,1,0:T(1,128)}), f32[32,1,32]{2,1,0:T(1,128)}, u32[]{:S(2)}, u32[]{:S(2)}) async-start(f32[32,1,32]{2,1,0:T(1,128)} %bitcast.172), calls=%async_computation.3 | async-start | bytes 32768 | tf_op jit(solution)/shard_map/all_to_all | solution.py:153
  110.1 3.5 %convolution_convert_fusion.3 = bf16[128,1536]{1,0:T(8,128)(2,1)} fusion(bf16[128,768]{1,0:T(8,128)(2,1)} %get-tuple-element.25, bf16[1,1536,768]{2,1,0:T(8,128)(2,1)} %param.15), kind=kOutput, calls=%fused_computation.10 | convolution fusion | flops 302186496 | bytes 2949120 | tf_op jit(solution)/shard_map/dot_general | solution.py:33
  113.6 1.7 collective-permute-start.12
  115.3 2.9 %all-to-all-done.3 = f32[32,1,32]{2,1,0:T(1,128)} async-done(((f32[32,1,32]{2,1,0:T(1,128)}), f32[32,1,32]{2,1,0:T(1,128)}, u32[]{:S(2)}, u32[]{:S(2)}) %all-to-all-start.3) | async-done | bytes 4128 | tf_op jit(solution)/shard_map/all_to_all | solution.py:153
  118.3 1.3 reduce_sum.145
  119.6 1.4 select_reduce_fusion
  121.6 5.1 %all-to-all-start.4 = ((f32[32,1,32]{2,1,0:T(1,128)}), f32[32,1,32]{2,1,0:T(1,128)}, u32[]{:S(2)}, u32[]{:S(2)}) async-start(f32[32,1,32]{2,1,0:T(1,128)} %bitcast.171), calls=%async_computation.4 | async-start | bytes 32768 | tf_op jit(solution)/shard_map/all_to_all | solution.py:128
  128.6 1.7 fusion.55
  130.3 4.3 %all-to-all-done.4 = f32[32,1,32]{2,1,0:T(1,128)} async-done(((f32[32,1,32]{2,1,0:T(1,128)}), f32[32,1,32]{2,1,0:T(1,128)}, u32[]{:S(2)}, u32[]{:S(2)}) %all-to-all-start.4) | async-done | bytes 4128 | tf_op jit(solution)/shard_map/all_to_all | solution.py:128
  136.1 1.4 mul.447
  137.5 7.6 %multiply_reduce_fusion = (f32[1536]{0:T(1024)S(1)}, bf16[1,1536,768]{1,2,0:T(8,128)(2,1)}) fusion(bf16[1,1536,768]{1,2,0:T(8,128)(2,1)} %copy.23, bf16[1024,1536]{1,0:T(8,128)(2,1)} %constant_dynamic-update-slice_fusion.1, bf16[1024,768]{1,0:T(8,128)(2,1)} %copy-done.25, f32[1024]{0:T(1024)} %mul.447), kind=kOutput, calls=%fused_computation | convolution fusion | flops 2422995456 | bytes 9447424 | tf_op jit(solution)/shard_map/dot_general | solution.py:33
  146.7 1.3 collective-permute-start.8
  148.0 1.9 collective-permute-done.15
  149.8 1.3 collective-permute-start.16
  151.1 1.1 fusion.47
  153.3 5.2 %collective-permute-done.8 = bf16[128,1536]{1,0:T(8,128)(2,1)S(1)} collective-permute-done((bf16[128,1536]{1,0:T(8,128)(2,1)S(1)}, bf16[128,1536]{1,0:T(8,128)(2,1)S(1)}, u32[]{:S(2)}, u32[]{:S(2)}) %collective-permute-start.8) | collective-permute-done | bytes 393248 | tf_op jit(solution)/shard_map/ppermute | solution.py:15
  158.5 1.3 collective-permute-start.9
  162.2 4.1 %collective-permute-done.17 = f32[9,1536]{1,0:T(8,128)S(1)} collective-permute-done((f32[9,1536]{1,0:T(8,128)S(1)}, f32[9,1536]{1,0:T(8,128)S(1)}, u32[]{:S(2)}, u32[]{:S(2)}) %collective-permute-start.17) | collective-permute-done | bytes 55328 | tf_op jit(solution)/shard_map/ppermute | solution.py:20
  169.0 1.4 fusion.52
  171.3 3.5 %all-to-all-start.2 = ((bf16[8,32,1536]{2,1,0:T(8,128)(2,1)}), bf16[8,32,1536]{2,1,0:T(8,128)(2,1)S(1)}, u32[]{:S(2)}, u32[]{:S(2)}) async-start(bf16[8,32,1536]{2,1,0:T(8,128)(2,1)} %bitcast.167), calls=%async_computation.2 | async-start | bytes 1572864 | tf_op jit(solution)/shard_map/all_to_all | solution.py:159
  174.9 1.8 constant_dynamic-update-slice_fusion.16
  176.7 1.6 add.194
  178.3 3.4 %collective-permute-start.19 = (f32[9,1536]{1,0:T(8,128)}, f32[9,1536]{1,0:T(8,128)}, u32[]{:S(2)}, u32[]{:S(2)}) collective-permute-start(f32[9,1536]{1,0:T(8,128)} %add.194), channel_id=1, source_target_pairs={{0,16},{4,20},{8,24},{12,28},{16,0},{20,4},{24,8},{28,12},{1,17},{... | collective-permute-start | bytes 165896 | tf_op jit(solution)/shard_map/ppermute | solution.py:20
  181.7 6.5 %fusion = bf16[1,768,1536]{2,1,0:T(8,128)(2,1)} fusion(bf16[1024,1536]{1,0:T(8,128)(2,1)} %constant_dynamic-update-slice_fusion.16, bf16[1024,768]{1,0:T(8,128)(2,1)} %copy-done.26, f32[1024]{0:T(1024)} %mul.447), kind=kOutput, calls=%fused_computation.4 | convolution fusion | flops 2419458048 | bytes 7081984 | tf_op jit(solution)/shard_map/dot_general | solution.py:33
  188.2 4.3 %copy.28 = bf16[1,1536,768]{2,1,0:T(8,128)(2,1)} copy(bf16[1,1536,768]{1,2,0:T(8,128)(2,1)} %get-tuple-element.37) | data formatting | bytes 4718592
  193.5 1.4 fusion.65
  194.8 1.3 fusion.70
  196.4 1.5 fusion.38
  198.0 2.1 %fusion.57 = bf16[1,128,1536]{2,1,0:T(8,128)(2,1)} fusion(f32[128,1536]{1,0:T(8,128)S(1)} %get-tuple-element.55, bf16[1,128,1536]{2,1,0:T(8,128)(2,1)S(1)} %copy-done.4, f32[128]{0:T(128)S(1)} %broadcast_multiply_fusion, f32[128]{0:T(128)S(1)} %copy-done.20, bf16[128,1536]{1,0:T(8,128)(2,1)} %collective-permute-done, bf16[128,1536]{1,0:T(8,128)(2,1)S(1)} %copy-done.11, ...), kind=kLoop, calls=%fused_computation.91 | loop fusion | flops 2359296 | bytes 2360833 | tf_op jit(solution)/shard_map/broadcast_in_dim | solution.py:194
  (130 shorter events, 32.4 us)
Async XLA Ops:
  0.6 52.0 %copy-start = (bf16[1,768,1536]{2,1,0:T(8,128)(2,1)S(1)}, bf16[1,768,1536]{2,1,0:T(8,128)(2,1)}, u32[]{:S(2)}) copy-start(bf16[1,768,1536]{2,1,0:T(8,128)(2,1)} %param.16) | copy-start | bytes 7077892
  0.6 14.4 %copy-start.24 = (f32[128]{0:T(128)S(1)}, f32[128]{0:T(128)}, u32[]{:S(2)}) copy-start(f32[128]{0:T(128)} %param.13) | copy-start | bytes 1540
  1.5 0.6 copy-start.18
  1.5 35.8 %copy-start.17 = (s32[128]{0:T(128)}, s32[128]{0:T(128)S(1)}, u32[]{:S(2)}) copy-start(s32[128]{0:T(128)S(1)} %get-tuple-element.47) | copy-start | bytes 1540
  3.4 12.1 %copy-start.19 = (f32[128]{0:T(128)}, f32[128]{0:T(128)S(1)}, u32[]{:S(2)}) copy-start(f32[128]{0:T(128)S(1)} %add_rsqrt_fusion) | copy-start | bytes 1540
  6.5 22.9 %all-to-all-start.1 = ((bf16[8,32,1536]{2,1,0:T(8,128)(2,1)}), bf16[8,32,1536]{2,1,0:T(8,128)(2,1)S(1)}, u32[]{:S(2)}, u32[]{:S(2)}) async-start(bf16[8,32,1536]{2,1,0:T(8,128)(2,1)} %bitcast.168), calls=%async_computation.1 | async-start | bytes 1572864 | tf_op jit(solution)/shard_map/all_to_all | solution.py:120
  12.3 7.6 %collective-permute-start = (bf16[128,1536]{1,0:T(8,128)(2,1)}, bf16[128,1536]{1,0:T(8,128)(2,1)}, u32[]{:S(2)}, u32[]{:S(2)}) collective-permute-start(bf16[128,1536]{1,0:T(8,128)(2,1)} %bitcast.173), channel_id=1, source_target_pairs={{32,0},{64,32},{96,64},{128,96},{160,128},{192,160},{224,192},{33,... | collective-permute-start | bytes 1179656 | tf_op jit(solution)/shard_map/ppermute | solution.py:91
  19.8 17.6 %copy-start.4 = (bf16[1,128,1536]{2,1,0:T(8,128)(2,1)S(1)}, bf16[1,128,1536]{2,1,0:T(8,128)(2,1)}, u32[]{:S(2)}) copy-start(bf16[1,128,1536]{2,1,0:T(8,128)(2,1)} %param.10) | copy-start | bytes 1179652
  29.4 20.0 %all-to-all-start = ((bf16[8,32,1536]{2,1,0:T(8,128)(2,1)}), bf16[8,32,1536]{2,1,0:T(8,128)(2,1)}, u32[]{:S(2)}, u32[]{:S(2)}) async-start(bf16[8,32,1536]{2,1,0:T(8,128)(2,1)} %bitcast.169), calls=%async_computation | async-start | bytes 1572864 | tf_op jit(solution)/shard_map/all_to_all | solution.py:122
  39.6 0.7 copy-start.21
  40.3 19.7 %collective-permute-start.5 = (bf16[256,1536]{1,0:T(8,128)(2,1)S(1)}, bf16[256,1536]{1,0:T(8,128)(2,1)}, u32[]{:S(2)}, u32[]{:S(2)}) collective-permute-start(bf16[256,1536]{1,0:T(8,128)(2,1)S(1)} %bitcast.163), channel_id=1, source_target_pairs={{0,1},{1,2},{2,3},{3,0},{4,5},{5,6},{6,7},{7,4},{8,9},{9,10},{10,1... | collective-permute-start | bytes 2359304 | tf_op jit(solution)/shard_map/ppermute | solution.py:15
  41.8 19.6 %collective-permute-start.2 = (bf16[256,1536]{1,0:T(8,128)(2,1)S(1)}, bf16[256,1536]{1,0:T(8,128)(2,1)}, u32[]{:S(2)}, u32[]{:S(2)}) collective-permute-start(bf16[256,1536]{1,0:T(8,128)(2,1)S(1)} %bitcast.164), channel_id=1, source_target_pairs={{0,3},{1,0},{2,1},{3,2},{4,7},{5,4},{6,5},{7,6},{8,11},{9,8},{10,9... | collective-permute-start | bytes 2359304 | tf_op jit(solution)/shard_map/ppermute | solution.py:15
  49.4 5.7 %copy-start.12 = (f32[256,768]{1,0:T(8,128)S(1)}, f32[256,768]{1,0:T(8,128)}, u32[]{:S(2)}) copy-start(f32[256,768]{1,0:T(8,128)} %fusion.18) | copy-start | bytes 2359300
  49.4 26.7 %collective-permute-start.4 = (bf16[256,1536]{1,0:T(8,128)(2,1)}, bf16[256,1536]{1,0:T(8,128)(2,1)S(1)}, u32[]{:S(2)}, u32[]{:S(2)}) collective-permute-start(bf16[256,1536]{1,0:T(8,128)(2,1)} %bitcast.9), channel_id=1, source_target_pairs={{0,1},{1,2},{2,3},{3,0},{4,5},{5,6},{6,7},{7,4},{8,9},{9,10},{10,1... | collective-permute-start | bytes 2359304 | tf_op jit(solution)/shard_map/ppermute | solution.py:15
  50.9 27.2 %collective-permute-start.1 = (bf16[256,1536]{1,0:T(8,128)(2,1)}, bf16[256,1536]{1,0:T(8,128)(2,1)S(1)}, u32[]{:S(2)}, u32[]{:S(2)}) collective-permute-start(bf16[256,1536]{1,0:T(8,128)(2,1)} %bitcast.9), channel_id=1, source_target_pairs={{0,3},{1,0},{2,1},{3,2},{4,7},{5,4},{6,5},{7,6},{8,11},{9,8},{10,9... | collective-permute-start | bytes 2359304 | tf_op jit(solution)/shard_map/ppermute | solution.py:15
  55.0 3.1 %copy-start.1 = (bf16[1,1536,768]{2,1,0:T(8,128)(2,1)S(1)}, bf16[1,1536,768]{2,1,0:T(8,128)(2,1)}, u32[]{:S(2)}) copy-start(bf16[1,1536,768]{2,1,0:T(8,128)(2,1)} %param.15) | copy-start | bytes 7077892
  61.1 24.5 %collective-permute-start.7 = (bf16[128,1536]{1,0:T(8,128)(2,1)S(1)}, bf16[128,1536]{1,0:T(8,128)(2,1)S(1)}, u32[]{:S(2)}, u32[]{:S(2)}) collective-permute-start(bf16[128,1536]{1,0:T(8,128)(2,1)S(1)} %slice.62), channel_id=1, source_target_pairs={{0,1},{1,2},{2,3},{3,0},{4,5},{5,6},{6,7},{7,4},{8,9},{9,10},{10,1... | collective-permute-start | bytes 1179656 | tf_op jit(solution)/shard_map/ppermute | solution.py:15
  62.5 28.8 %collective-permute-start.11 = (bf16[128,1536]{1,0:T(8,128)(2,1)S(1)}, bf16[128,1536]{1,0:T(8,128)(2,1)S(1)}, u32[]{:S(2)}, u32[]{:S(2)}) collective-permute-start(bf16[128,1536]{1,0:T(8,128)(2,1)S(1)} %slice.66), channel_id=1, source_target_pairs={{0,3},{1,0},{2,1},{3,2},{4,7},{5,4},{6,5},{7,6},{8,11},{9,8},{10,9... | collective-permute-start | bytes 1179656 | tf_op jit(solution)/shard_map/ppermute | solution.py:15
  76.1 17.7 %collective-permute-start.6 = (bf16[128,1536]{1,0:T(8,128)(2,1)S(1)}, bf16[128,1536]{1,0:T(8,128)(2,1)S(1)}, u32[]{:S(2)}, u32[]{:S(2)}) collective-permute-start(bf16[128,1536]{1,0:T(8,128)(2,1)S(1)} %slice.61), channel_id=1, source_target_pairs={{0,1},{1,2},{2,3},{3,0},{4,5},{5,6},{6,7},{7,4},{8,9},{9,10},{10,1... | collective-permute-start | bytes 1179656 | tf_op jit(solution)/shard_map/ppermute | solution.py:15
  78.1 4.1 %copy-start.9 = (bf16[256,1536]{1,0:T(8,128)(2,1)}, bf16[256,1536]{1,0:T(8,128)(2,1)S(1)}, u32[]{:S(2)}) copy-start(bf16[256,1536]{1,0:T(8,128)(2,1)S(1)} %collective-permute-done.1) | copy-start | bytes 2359300
  78.1 17.6 %collective-permute-start.10 = (bf16[128,1536]{1,0:T(8,128)(2,1)S(1)}, bf16[128,1536]{1,0:T(8,128)(2,1)S(1)}, u32[]{:S(2)}, u32[]{:S(2)}) collective-permute-start(bf16[128,1536]{1,0:T(8,128)(2,1)S(1)} %slice.65), channel_id=1, source_target_pairs={{0,3},{1,0},{2,1},{3,2},{4,7},{5,4},{6,5},{7,6},{8,11},{9,8},{10,9... | collective-permute-start | bytes 1179656 | tf_op jit(solution)/shard_map/ppermute | solution.py:15
  83.0 1.2 copy-start.7
  83.8 1.7 copy-start.5
  84.2 83.7 %collective-permute-start.3 = (bf16[128,1536]{1,0:T(8,128)(2,1)S(1)}, bf16[128,1536]{1,0:T(8,128)(2,1)}, u32[]{:S(2)}, u32[]{:S(2)}) collective-permute-start(bf16[128,1536]{1,0:T(8,128)(2,1)S(1)} %slice.96), channel_id=1, source_target_pairs={{0,1},{1,2},{2,3},{3,0},{4,5},{5,6},{6,7},{7,4},{8,9},{9,10},{10,1... | collective-permute-start | bytes 1179656 | tf_op jit(solution)/shard_map/ppermute | solution.py:15
  85.5 6.6 %copy-start.15 = (bf16[1024,1536]{1,0:T(8,128)(2,1)}, bf16[1024,1536]{1,0:T(8,128)(2,1)S(1)}, u32[]{:S(2)}) copy-start(bf16[1024,1536]{1,0:T(8,128)(2,1)S(1)} %constant_dynamic-update-slice_fusion.19) | copy-start | bytes 9437188
  85.5 82.4 %collective-permute-start.14 = (bf16[128,1536]{1,0:T(8,128)(2,1)}, bf16[128,1536]{1,0:T(8,128)(2,1)}, u32[]{:S(2)}, u32[]{:S(2)}) collective-permute-start(bf16[128,1536]{1,0:T(8,128)(2,1)} %slice.95), channel_id=1, source_target_pairs={{0,3},{1,0},{2,1},{3,2},{4,7},{5,4},{6,5},{7,6},{8,11},{9,8},{10,9... | collective-permute-start | bytes 1179656 | tf_op jit(solution)/shard_map/ppermute | solution.py:15
  95.7 1.9 copy-start.13
  97.4 1.6 copy-start.25
  97.4 1.7 copy-start.26
  103.3 14.9 %all-to-all-start.3 = ((f32[32,1,32]{2,1,0:T(1,128)}), f32[32,1,32]{2,1,0:T(1,128)}, u32[]{:S(2)}, u32[]{:S(2)}) async-start(f32[32,1,32]{2,1,0:T(1,128)} %bitcast.172), calls=%async_computation.3 | async-start | bytes 32768 | tf_op jit(solution)/shard_map/all_to_all | solution.py:153
  113.6 37.5 %collective-permute-start.12 = (bf16[128,1536]{1,0:T(8,128)(2,1)}, bf16[128,1536]{1,0:T(8,128)(2,1)}, u32[]{:S(2)}, u32[]{:S(2)}) collective-permute-start(bf16[128,1536]{1,0:T(8,128)(2,1)} %convolution_convert_fusion.3), channel_id=1, source_target_pairs={{0,1},{1,2},{2,3},{3,0},{4,5},{5,6},{6,7},{7,4},{8,9},{9,10},{10,1... | collective-permute-start | bytes 1179656 | tf_op jit(solution)/shard_map/ppermute | solution.py:15
  121.6 13.0 %all-to-all-start.4 = ((f32[32,1,32]{2,1,0:T(1,128)}), f32[32,1,32]{2,1,0:T(1,128)}, u32[]{:S(2)}, u32[]{:S(2)}) async-start(f32[32,1,32]{2,1,0:T(1,128)} %bitcast.171), calls=%async_computation.4 | async-start | bytes 32768 | tf_op jit(solution)/shard_map/all_to_all | solution.py:128
  128.1 0.5 copy-start.23
  137.5 7.6 %copy-start.16 = (f32[8,1536]{1,0:T(8,128)S(1)}, f32[8,1536]{1,0:T(8,128)}, u32[]{:S(2)}) copy-start(f32[8,1536]{1,0:T(8,128)} %fusion.55) | copy-start | bytes 147460
  137.5 8.3 %copy-start.2 = (bf16[1,1536,768]{2,1,0:T(8,128)(2,1)S(1)}, bf16[1,1536,768]{2,1,0:T(8,128)(2,1)}, u32[]{:S(2)}) copy-start(bf16[1,1536,768]{2,1,0:T(8,128)(2,1)} %param.15) | copy-start | bytes 7077892
  137.5 8.3 %copy-start.14 = (bf16[128,768]{1,0:T(8,128)(2,1)S(1)}, bf16[128,768]{1,0:T(8,128)(2,1)}, u32[]{:S(2)}) copy-start(bf16[128,768]{1,0:T(8,128)(2,1)} %get-tuple-element.27) | copy-start | bytes 589828
  145.1 6.1 %copy-start.8 = (f32[256,1536]{1,0:T(8,128)S(1)}, f32[256,1536]{1,0:T(8,128)}, u32[]{:S(2)}) copy-start(f32[256,1536]{1,0:T(8,128)} %copy-done.7) | copy-start | bytes 4718596
  145.1 4.7 %collective-permute-start.15 = (f32[9,1536]{1,0:T(8,128)S(1)}, f32[9,1536]{1,0:T(8,128)S(1)}, u32[]{:S(2)}, u32[]{:S(2)}) collective-permute-start(f32[9,1536]{1,0:T(8,128)S(1)} %pad_maximum_fusion.1), channel_id=1, source_target_pairs={{0,1},{1,0},{2,3},{3,2},{4,5},{5,4},{6,7},{7,6},{8,9},{9,8},{10,11... | collective-permute-start | bytes 165896 | tf_op jit(solution)/shard_map/ppermute | solution.py:20
  145.8 12.6 %copy-start.6 = (f32[256,1536]{1,0:T(8,128)S(1)}, f32[256,1536]{1,0:T(8,128)}, u32[]{:S(2)}) copy-start(f32[256,1536]{1,0:T(8,128)} %copy-done.5) | copy-start | bytes 4718596
  146.7 13.2 %copy-start.10 = (bf16[256,1536]{1,0:T(8,128)(2,1)S(1)}, bf16[256,1536]{1,0:T(8,128)(2,1)}, u32[]{:S(2)}) copy-start(bf16[256,1536]{1,0:T(8,128)(2,1)} %copy-done.9) | copy-start | bytes 2359300
  146.7 11.7 %collective-permute-start.8 = (bf16[128,1536]{1,0:T(8,128)(2,1)S(1)}, bf16[128,1536]{1,0:T(8,128)(2,1)S(1)}, u32[]{:S(2)}, u32[]{:S(2)}) collective-permute-start(bf16[128,1536]{1,0:T(8,128)(2,1)S(1)} %convolution_convert_fusion.4), channel_id=1, source_target_pairs={{0,3},{1,0},{2,1},{3,2},{4,7},{5,4},{6,5},{7,6},{8,11},{9,8},{10,9... | collective-permute-start | bytes 1179656 | tf_op jit(solution)/shard_map/ppermute | solution.py:15
  149.8 11.0 %collective-permute-start.16 = (f32[9,1536]{1,0:T(8,128)S(1)}, f32[9,1536]{1,0:T(8,128)S(1)}, u32[]{:S(2)}, u32[]{:S(2)}) collective-permute-start(f32[9,1536]{1,0:T(8,128)S(1)} %fusion.78), channel_id=1, source_target_pairs={{0,2},{1,3},{2,0},{3,1},{4,6},{5,7},{6,4},{7,5},{8,10},{9,11},{10,... | collective-permute-start | bytes 165896 | tf_op jit(solution)/shard_map/ppermute | solution.py:20
  152.2 16.7 %copy-start.3 = (f32[256,1536]{1,0:T(8,128)S(1)}, f32[256,1536]{1,0:T(8,128)}, u32[]{:S(2)}) copy-start(f32[256,1536]{1,0:T(8,128)} %fusion.16) | copy-start | bytes 4718596
  152.3 15.7 %collective-permute-start.13 = (bf16[128,1536]{1,0:T(8,128)(2,1)S(1)}, bf16[128,1536]{1,0:T(8,128)(2,1)S(1)}, u32[]{:S(2)}, u32[]{:S(2)}) collective-permute-start(bf16[128,1536]{1,0:T(8,128)(2,1)S(1)} %fusion.47), channel_id=1, source_target_pairs={{0,1},{1,2},{2,3},{3,0},{4,5},{5,6},{6,7},{7,4},{8,9},{9,10},{10,1... | collective-permute-start | bytes 1179656 | tf_op jit(solution)/shard_map/ppermute | solution.py:15
  158.5 10.4 %collective-permute-start.9 = (bf16[128,1536]{1,0:T(8,128)(2,1)S(1)}, bf16[128,1536]{1,0:T(8,128)(2,1)S(1)}, u32[]{:S(2)}, u32[]{:S(2)}) collective-permute-start(bf16[128,1536]{1,0:T(8,128)(2,1)S(1)} %fusion.50), channel_id=1, source_target_pairs={{0,3},{1,0},{2,1},{3,2},{4,7},{5,4},{6,5},{7,6},{8,11},{9,8},{10,9... | collective-permute-start | bytes 1179656 | tf_op jit(solution)/shard_map/ppermute | solution.py:15
  160.8 5.4 %collective-permute-start.17 = (f32[9,1536]{1,0:T(8,128)S(1)}, f32[9,1536]{1,0:T(8,128)S(1)}, u32[]{:S(2)}, u32[]{:S(2)}) collective-permute-start(f32[9,1536]{1,0:T(8,128)S(1)} %add.192), channel_id=1, source_target_pairs={{0,4},{4,0},{8,12},{12,8},{16,20},{20,16},{24,28},{28,24},{1,5},{5... | collective-permute-start | bytes 165896 | tf_op jit(solution)/shard_map/ppermute | solution.py:20
  166.9 9.7 %collective-permute-start.18 = (f32[9,1536]{1,0:T(8,128)}, f32[9,1536]{1,0:T(8,128)}, u32[]{:S(2)}, u32[]{:S(2)}) collective-permute-start(f32[9,1536]{1,0:T(8,128)} %add.193), channel_id=1, source_target_pairs={{0,8},{4,12},{8,0},{12,4},{16,24},{20,28},{24,16},{28,20},{1,9},{5... | collective-permute-start | bytes 165896 | tf_op jit(solution)/shard_map/ppermute | solution.py:20
  171.3 24.8 %all-to-all-start.2 = ((bf16[8,32,1536]{2,1,0:T(8,128)(2,1)}), bf16[8,32,1536]{2,1,0:T(8,128)(2,1)S(1)}, u32[]{:S(2)}, u32[]{:S(2)}) async-start(bf16[8,32,1536]{2,1,0:T(8,128)(2,1)} %bitcast.167), calls=%async_computation.2 | async-start | bytes 1572864 | tf_op jit(solution)/shard_map/all_to_all | solution.py:159
  178.3 14.2 %collective-permute-start.19 = (f32[9,1536]{1,0:T(8,128)}, f32[9,1536]{1,0:T(8,128)}, u32[]{:S(2)}, u32[]{:S(2)}) collective-permute-start(f32[9,1536]{1,0:T(8,128)} %add.194), channel_id=1, source_target_pairs={{0,16},{4,20},{8,24},{12,28},{16,0},{20,4},{24,8},{28,12},{1,17},{... | collective-permute-start | bytes 165896 | tf_op jit(solution)/shard_map/ppermute | solution.py:20
  196.1 1.8 copy-start.11
  196.1 1.8 copy-start.20
  196.1 1.8 copy-start.22

commit v2 on v1

v2 whole, which is shorter than its diff:
```python
import functools

import jax
import jax.numpy as jnp
from jax import lax
from jax.experimental import pallas as pl
from jax.experimental.pallas import tpu as pltpu
from jax.sharding import Mesh, PartitionSpec as P

gelu_scale = 0.7978845608028654
cubic_coef = 0.044715
norm_eps = 1e-06
lane = 128
bf16 = jnp.bfloat16
f32 = jnp.float32
room = 60 << 20
cheaper = 8


def shift(value, axis, steps):
    count = lax.axis_size(axis)
    return lax.ppermute(value, axis, [(i, (i + steps) % count) for i in range(count)])


def swap(value, axis, mask):
    count = lax.axis_size(axis)
    return lax.ppermute(value, axis, [(i, i ^ mask) for i in range(count)])


def total_over(value):
    value = value + swap(value, "e", 1)
    for axis, unit in (("e", 2), ("x", 1)):
        one, two, three = (swap(value, axis, unit * mask) for mask in (1, 2, 3))
        value = (value + two) + (one + three)
    return value


def after(value, *done):
    return lax.optimization_barrier((value,) + done)[0]


def dot(a, b, dims):
    return lax.dot_general(a, b, (dims, ((), ())), preferred_element_type=f32)


def exact(a, b, dims):
    return lax.dot_general(
        a, b, (dims, ((), ())), preferred_element_type=f32, precision=lax.Precision.HIGHEST
    )


def like(shape, dtype):
    return jax.ShapeDtypeStruct(shape, dtype)


def call(kernel, out, flops, moved, **options):
    return pl.pallas_call(
        kernel,
        out_shape=out,
        cost_estimate=pl.CostEstimate(flops=flops, bytes_accessed=moved, transcendentals=0),
        compiler_params=pltpu.CompilerParams(vmem_limit_bytes=room),
        **options,
    )


def one_hots(routes, experts, tok_count):
    ids = lax.broadcasted_iota(jnp.int32, (experts, tok_count), 0)
    return (ids == routes[0:1, :]).astype(f32), (ids == routes[1:2, :]).astype(f32)


def token_kernel(
    capacity, x_ref, gain_ref, router_ref, routes_ref, xn_ref, slots_ref, pick_ref, gate_ref, back_ref, g_ref
):
    tok_count = x_ref.shape[0]
    experts = router_ref.shape[0]
    slots = experts * capacity
    x32 = x_ref[...].astype(f32)
    inv = lax.rsqrt(jnp.mean(x32 * x32, -1, keepdims=True) + norm_eps)
    xn = (x32 * inv * gain_ref[...]).astype(bf16)
    xn_ref[...] = xn
    logits = dot(router_ref[...], xn, ((1,), (1,)))
    first, second = one_hots(routes_ref[...], experts, tok_count)
    named = first + second
    g1 = jax.nn.sigmoid(
        jnp.sum(first * logits, 0, keepdims=True) - jnp.sum(second * logits, 0, keepdims=True)
    )
    g_ref[...] = g1
    gates = first * g1 + second * (1.0 - g1)
    row = lax.broadcasted_iota(jnp.int32, (tok_count, tok_count), 0)
    col = lax.broadcasted_iota(jnp.int32, (tok_count, tok_count), 1)
    earlier = (row < col).astype(f32).astype(bf16)
    place = dot(named.astype(bf16), earlier, ((1,), (0,)))
    place = jnp.where(named > 0, place, -1.0)
    slot = lax.broadcasted_iota(jnp.int32, (capacity, tok_count), 0).astype(f32)
    chosen = jnp.concatenate(
        [(slot == place[e : e + 1, :]).astype(f32) for e in range(experts)], 0
    )
    spread = jnp.concatenate(
        [jnp.broadcast_to(gates[e : e + 1, :], (capacity, tok_count)) for e in range(experts)], 0
    )
    pick = chosen.astype(bf16)
    pick_ref[...] = pick
    weighed = chosen * spread
    gate = jnp.sum(weighed, -1, keepdims=True)
    gate_ref[...] = jnp.broadcast_to(gate, (slots, lane)).astype(bf16)
    back_ref[...] = weighed.T.astype(bf16)
    slots_ref[...] = dot(pick, xn, ((1,), (0,))).astype(bf16)


def cot_kernel(last_ref, arrived_ref, noise_ref, rewards_ref, pick_ref, gate_ref, cot_ref, slots_ref):
    width = arrived_ref.shape[1]
    own = (-rewards_ref[...] * noise_ref[...].astype(f32)).astype(bf16)
    last = last_ref[0] == 1
    cot = jnp.where(last, own.astype(f32), arrived_ref[...].astype(f32)).astype(bf16)
    cot_ref[...] = cot
    slots_ref[:, :width] = dot(pick_ref[...], cot, ((1,), (0,))).astype(bf16)
    slots_ref[:, width:] = gate_ref[...]


def as_row(column):
    return jnp.broadcast_to(column, (column.shape[0], lane)).T[0:1, :]


def expert_rows(xn, cot, gate, up, down):
    pre = dot(xn, up, ((1,), (0,)))
    dh = dot(cot, down, ((1,), (1,)))
    square = pre * pre
    tangent = jnp.tanh(gelu_scale * pre * (1.0 + cubic_coef * square))
    hidden = 0.5 * pre * (1.0 + tangent)
    slope = 0.5 * (1.0 + tangent) + 0.5 * pre * (1.0 - tangent * tangent) * gelu_scale * (
        1.0 + 3.0 * cubic_coef * square
    )
    hidden = hidden.astype(bf16).astype(f32)
    d_gate = jnp.sum(hidden * dh, -1, keepdims=True)
    d_pre = dh * slope
    back = dot(d_pre.astype(bf16), up, ((1,), (1,)))
    gain = jnp.sum(back * (gate * xn.astype(f32)), 0, keepdims=True)
    return (
        (hidden * gate).astype(bf16),
        (d_pre * gate).astype(bf16),
        back.astype(bf16),
        as_row(d_gate),
        gain,
    )


def expert_kernel(count, *refs):
    up_ref, down_ref = refs[:2]
    ins, outs = refs[2 : 2 + 2 * count], refs[2 + 2 * count :]
    width = up_ref.shape[0]
    cot = jnp.concatenate([ref[...] for ref in ins[count:]], 0)
    found = expert_rows(
        jnp.concatenate([ref[...] for ref in ins[:count]], 0),
        cot[:, :width],
        cot[:, width : width + 1].astype(f32),
        up_ref[...],
        down_ref[...],
    )
    for ref, value in zip(outs, found):
        ref[...] = value


def run_experts(up, down, xns, cots):
    total = sum(xn.shape[0] for xn in xns)
    return call(
        functools.partial(expert_kernel, len(xns)),
        [
            like((total, up.shape[1]), bf16),
            like((total, up.shape[1]), bf16),
            like((total, up.shape[0]), bf16),
            like((1, total), f32),
            like((1, up.shape[0]), f32),
        ],
        6 * total * up.size // cheaper,
        (4 * up.size + 8 * total * up.shape[0]) // cheaper,
    )(up, down, *xns, *cots)


def grads_kernel(xns, cots, hs, *refs):
    xn_refs, cot_refs = refs[:xns], refs[xns : xns + cots]
    h_refs = refs[xns + cots : xns + cots + hs]
    d_refs = refs[xns + cots + hs : xns + cots + 2 * hs]
    up_g_ref, down_g_ref = refs[-2:]

    def joined(group):
        return jnp.concatenate([ref[...] for ref in group], 0)

    up_g_ref[...] = dot(joined(xn_refs), joined(d_refs), ((0,), (0,))).astype(bf16)
    down_g_ref[...] = dot(joined(h_refs), joined(cot_refs), ((0,), (0,))).astype(bf16)


def run_grads(width, hid, xns, cots, hs, ds):
    steps = 6
    specs = [pl.BlockSpec((v.shape[0], width // steps), lambda i: (0, i)) for v in xns]
    specs += [pl.BlockSpec((v.shape[0], width), lambda i: (0, 0)) for v in cots]
    specs += [pl.BlockSpec((v.shape[0], hid // steps), lambda i: (0, i)) for v in hs]
    specs += [pl.BlockSpec((v.shape[0], hid), lambda i: (0, 0)) for v in ds]
    total = sum(v.shape[0] for v in xns)
    return call(
        functools.partial(grads_kernel, len(xns), len(cots), len(hs)),
        [like((width, hid), bf16), like((hid, width), bf16)],
        4 * total * width * hid // cheaper,
        (4 * width * hid + 6 * total * width) // cheaper,
        grid=(steps,),
        in_specs=specs,
        out_specs=[
            pl.BlockSpec((width // steps, hid), lambda i: (i, 0)),
            pl.BlockSpec((hid // steps, width), lambda i: (i, 0)),
        ],
    )(*xns, *cots, *hs, *ds)


def spread_kernel(here_ref, own_ref, near_ref, far_ref, out_ref):
    here = here_ref[0]
    experts = out_ref.shape[0]
    far = far_ref[...]
    slots = far.shape[1]
    held = [own_ref[...], near_ref[:, slots:], far, near_ref[:, :slots]]
    count = len(held)
    capacity = far.shape[1] // experts
    columns = []
    for place in range(count):
        step = lax.rem(place - here + count, count)
        row = held[0]
        for k in range(1, count):
            row = jnp.where(step == k, held[k], row)
        columns.append(
            jnp.concatenate(
                [row[:, e * capacity : (e + 1) * capacity] for e in range(experts)], 0
            )
        )
    out_ref[...] = jnp.concatenate(columns, 1)


def router_kernel(dg_ref, pick_ref, routes_ref, g_ref, xn_ref, part_ref, dl_ref):
    slots, tok_count = pick_ref.shape
    experts = dg_ref.shape[0]
    capacity = slots // experts
    wide = dg_ref[...]
    dg = wide[:, :capacity]
    for k in range(1, wide.shape[1] // capacity):
        dg = dg + wide[:, k * capacity : (k + 1) * capacity]
    tiled = jnp.concatenate([dg] * experts, 1)
    row = lax.broadcasted_iota(jnp.int32, (experts, slots), 0)
    col = lax.broadcasted_iota(jnp.int32, (experts, slots), 1)
    mine = (col >= row * capacity) & (col < (row + 1) * capacity)
    dg_tok = exact(jnp.where(mine, tiled, 0.0), pick_ref[...].astype(f32), ((1,), (0,)))
    first, second = one_hots(routes_ref[...], experts, tok_count)
    sign = first - second
    g1 = g_ref[...]
    d_logits = sign * (g1 * (1.0 - g1) * jnp.sum(sign * dg_tok, 0, keepdims=True))
    part_ref[...] = exact(d_logits, xn_ref[...].astype(f32), ((1,), (0,)))
    padded = jnp.concatenate(
        [d_logits, jnp.zeros((lane - experts, tok_count), f32)], 0
    )
    dl_ref[...] = padded.T


def final_kernel(x_ref, gain_ref, cot_ref, slots_ref, back_ref, dl_ref, router_ref, out_ref):
    x32 = x_ref[...].astype(f32)
    inv = lax.rsqrt(jnp.mean(x32 * x32, -1, keepdims=True) + norm_eps)
    xh = x32 * inv
    dxn = dot(back_ref[...], slots_ref[...], ((1,), (0,)))
    router = router_ref[...].astype(f32)
    for e in range(router.shape[0]):
        dxn = dxn + dl_ref[:, e : e + 1] * router[e : e + 1, :]
    rows = dxn * gain_ref[...]
    out_ref[...] = (
        cot_ref[...].astype(f32) + inv * (rows - xh * jnp.mean(rows * xh, -1, keepdims=True))
    ).astype(bf16)


def shards(
    segment_input,
    upstream_grad,
    step_noise,
    rewards,
    routes,
    up_weight,
    down_weight,
    router_weight,
    norm_gain,
):
    tok_count = segment_input.shape[1]
    width = segment_input.shape[2]
    experts = router_weight.shape[2]
    split = lax.axis_size("x")
    top_count = routes.shape[2]
    capacity = tok_count * top_count // experts
    slots = experts * capacity
    half = slots // 2
    x = segment_input[0]
    up = up_weight[0]
    down = down_weight[0]
    router = router_weight[0].T
    pair = routes[0].T
    n_segment = lax.axis_size("segment")
    arrived = lax.ppermute(
        upstream_grad[0], "segment", [(i + 1, i) for i in range(n_segment - 1)]
    )
    is_last = (lax.axis_index("segment") == n_segment - 1).astype(jnp.int32).reshape(1)
    here = lax.axis_index("x").astype(jnp.int32).reshape(1)
    scalar = pl.BlockSpec(memory_space=pltpu.SMEM)
    whole = pl.BlockSpec(memory_space=pltpu.VMEM)

    xn, xn_slots, pick, gate, weigh, g1 = call(
        functools.partial(token_kernel, capacity),
        [
            like((tok_count, width), bf16),
            like((slots, width), bf16),
            like((slots, tok_count), bf16),
            like((slots, lane), bf16),
            like((tok_count, slots), bf16),
            like((1, tok_count), f32),
        ],
        2 * slots * tok_count * width,
        4 * tok_count * width + 2 * slots * width,
    )(x, norm_gain, router, pair)
    def exchange(rows):
        shaped = rows.reshape(experts, capacity, rows.shape[1])
        return lax.all_to_all(shaped, "e", 0, 0, tiled=True).reshape(rows.shape)

    xn_own = exchange(xn_slots)
    xn_low, xn_high = shift(xn_own, "x", 1), shift(xn_own, "x", -1)
    pick_late = after(pick, xn_own)
    cot, c_slots = call(
        cot_kernel,
        [like((tok_count, width), bf16), like((slots, width + lane), bf16)],
        2 * slots * tok_count * width,
        6 * tok_count * width + 2 * slots * width,
        in_specs=[scalar] + [whole] * 5,
    )(is_last, arrived, step_noise, rewards[:, None], pick_late, gate)

    c_own = exchange(c_slots)
    c_own, xn_low, xn_high = lax.optimization_barrier((c_own, xn_low, xn_high))
    c_low, c_high = shift(c_own, "x", 1), shift(c_own, "x", -1)
    xn_far_a, xn_far_b = shift(xn_low[:half], "x", 1), shift(xn_high[half:], "x", -1)
    h_own, d_own, b_own, g_own, n_own = run_experts(up, down, [xn_own], [c_own])
    c_far_a, c_far_b = shift(c_low[:half], "x", 1), shift(c_high[half:], "x", -1)
    h_near, d_near, b_near, g_near, n_near = run_experts(
        after(up, b_own), down, [xn_low, xn_high], [c_low, c_high]
    )
    to_low_b = shift(b_near[half:slots], "x", -1)
    to_high_a = shift(b_near[slots : slots + half], "x", 1)
    h_far, d_far, b_far, g_far, n_far = run_experts(
        after(up, b_near), down, [xn_far_a, xn_far_b], [c_far_a, c_far_b]
    )
    via_low = shift(b_far[:half], "x", -1)
    via_high = shift(b_far[half:], "x", 1)
    g_far, to_low_b, to_high_a = lax.optimization_barrier((g_far, to_low_b, to_high_a))
    to_low_a = shift((b_near[:half].astype(f32) + via_low.astype(f32)).astype(bf16), "x", -1)
    to_high_b = shift(
        (b_near[slots + half :].astype(f32) + via_high.astype(f32)).astype(bf16), "x", 1
    )
    first = b_own[:half].astype(f32) + to_high_a.astype(f32) + to_low_a.astype(f32)
    second = b_own[half:].astype(f32) + to_high_b.astype(f32) + to_low_b.astype(f32)
    back = jnp.concatenate([first.astype(bf16), second.astype(bf16)], 0)
    back_slots = exchange(back)

    dg = call(
        spread_kernel,
        like((experts, split * capacity), f32),
        1000,
        8 * experts * split * capacity,
        in_specs=[scalar] + [whole] * 3,
    )(here, g_own, g_near, g_far)
    dg_got = lax.all_to_all(
        dg.reshape(experts * split, capacity), ("e", "x"), 0, 0, tiled=True
    ).reshape(experts, split * capacity)
    router_part, d_logits = call(
        router_kernel,
        [like((experts, width), f32), like((tok_count, lane), f32)],
        12 * experts * tok_count * width // cheaper,
        2 * tok_count * width // cheaper,
    )(dg_got, pick, pair, g1, xn)
    up_g, down_g = run_grads(
        width,
        up.shape[1],
        [xn_own, xn_low, xn_high, xn_far_a, xn_far_b],
        [c_own, c_low, c_high, c_far_a, c_far_b],
        [h_own, h_near, h_far],
        [d_own, d_near, d_far],
    )
    small = total_over(jnp.concatenate([router_part, n_own + n_near + n_far], 0))
    router_total = small[:experts]
    gain_total = (small[experts] + jnp.sum(router_total * router.astype(f32), 0)) / norm_gain[0]

    input_g = call(
        final_kernel,
        like((tok_count, width), bf16),
        2 * slots * tok_count * width,
        8 * tok_count * width + 2 * slots * width,
    )(x, norm_gain, cot, back_slots, weigh, d_logits, router)
    return (
        input_g[None],
        up_g[None],
        down_g[None],
        router_total.T[None],
        gain_total[None],
    )


def solution(mesh):
    experts = 8
    n_segment, n_dp = mesh.devices.shape
    grid = Mesh(
        mesh.devices.reshape(n_segment, experts, n_dp // experts), ("segment", "e", "x")
    )
    dp = ("e", "x")
    return jax.shard_map(
        shards,
        mesh=grid,
        in_specs=(
            P("segment", dp, None),
            P("segment", dp, None),
            P(dp, None),
            P(dp),
            P("segment", dp, None),
            P("segment", None, dp),
            P("segment", dp, None),
            P("segment", None, None),
            P("segment", None),
        ),
        out_specs=(
            P("segment", dp, None),
            P("segment", None, dp),
            P("segment", dp, None),
            P("segment", None, None),
            P("segment", None),
        ),
        check_vma=False,
    )
```

time: 204 us -> 181 us (0.89); the launches traced: 200 us -> 180 us
  matrix products: 49.7 us -> 0 us
  Pallas kernels: 0 us -> 42.4 us
  waiting for transfers between devices: 30.8 us -> 58.2 us
  local copies, waits for them, and re-layouts: 36.1 us -> 16.5 us
  other arithmetic: 22.3 us -> 5.41 us
  starting transfers between devices: 60 us -> 56.2 us
    dot_general x26 -> x0, matrix products: 49.7 us -> none  [the longest x22 44.1 us: dot(): return lax.dot_general(a, b, (dims, ((), ())), preferred_element_type=f32)]
    pallas_call x0 -> x9, Pallas kernels: none -> 42.4 us  [the longest x3 20 us: run_experts(): call(functools.partial(expert_kernel, len(xns)), [like((total, up.shape[1...]
    ppermute x14, waiting for transfers between devices: 8.89 us -> 33 us  [shift(): lax.ppermute(value, axis, [(i, (i + steps) % count) for i in range(count)])]
    unnamed x68 -> x42, local copies, waits for them, and re-layouts: 24.4 us -> 4.62 us
    reduce_sum x10 -> x1, other arithmetic: 7.54 us -> 0.63 us  [shards(): jnp.sum(router_total * router.astype(f32), 0)]
    all_to_all x5 -> x4, waiting for transfers between devices: 15.8 us -> 22.6 us  [the longest x3 14.4 us: exchange(): return lax.all_to_all(shaped, 'e', 0, 0, tiled=True).reshape(rows.shape)]
    slice x6, local copies, waits for them, and re-layouts: 3 us -> 8.62 us  [the longest x1 1.94 us: shards(): via_low = shift(b_far[:half], 'x', -1)]
    all_to_all x5 -> x4, starting transfers between devices: 29.2 us -> 24.6 us  [the longest x3 14.7 us: exchange(): return lax.all_to_all(shaped, 'e', 0, 0, tiled=True).reshape(rows.shape)]
  transfers between devices with their start and end apart: 25 -> 26, of which waited for: 10 -> 10; matrix products, arithmetic and copies ran while one was open for 49% -> 9% of each run, Pallas kernels for 0% -> 19%
where the time goes in v2:
time: 181 us; the launch traced here: 180 us
  waiting for transfers between devices  58.2 us (32%)
  starting transfers between devices  56.2 us (31%)
  Pallas kernels  42.4 us (23%)
  local copies, waits for them, and re-layouts  16.5 us (9%)
  other arithmetic  5.41 us (3%)
    ppermute x14, waiting for transfers between devices, shift(): lax.ppermute(value, axis, [(i, (i + steps) % count) for i in range(count)])  33 us
    ppermute x14, starting transfers between devices, shift(): lax.ppermute(value, axis, [(i, (i + steps) % count) for i in range(count)])  20.4 us
    pallas_call x3, Pallas kernels, run_experts(): call(functools.partial(expert_kernel, len(xns)), [like((total, up.shape[1...  20 us
    all_to_all x3, starting transfers between devices, exchange(): return lax.all_to_all(shaped, 'e', 0, 0, tiled=True).reshape(rows.shape)  14.7 us
    all_to_all x3, waiting for transfers between devices, exchange(): return lax.all_to_all(shaped, 'e', 0, 0, tiled=True).reshape(rows.shape)  14.4 us
    pallas_call x1, Pallas kernels, run_grads(): call(functools.partial(grads_kernel, len(xns), len(cots), len(hs)), [like...  10.3 us
    all_to_all x1, starting transfers between devices, shards(): lax.all_to_all(dg.reshape(experts * split, capacity), ('e', 'x'), 0, 0, t...  9.98 us
    ppermute x7, starting transfers between devices, swap(): return lax.ppermute(value, axis, [(i, i ^ mask) for i in range(count)])  9.23 us
  transfers between devices with their start and end apart: 26, of which 10 were waited for; matrix products, arithmetic and copies ran while one was open for 9% of the time, Pallas kernels for 19%

profile of v2, /device:TPU:64, one launch (start us, length us, event | category | flops | bytes accessed | tf_op | source)
XLA Modules:
  0.0 179.7 jit_solution(5778992975339271009)
XLA Ops:
  0.7 2.6 %shard_map.128 = (bf16[128,1536]{1,0:T(8,128)(2,1)}, bf16[256,1536]{1,0:T(8,128)(2,1)}, bf16[256,128]{1,0:T(8,128)(2,1)}, bf16[256,128]{1,0:T(8,128)(2,1)}, bf16[128,256]{1,0:T(8,128)(2,1)}, /*index=5*/f32[1,128]{1,0:T(1,128)}) custom-call(bf16[128,1536]{1,0:T(8,128)(2,1)} %bitcast.43, f32[1,1536]{1,0:T(1,128)} %gain_ref.3, bf16[8,1536]{1,0:T(8,128)(2,1)} %bitcast.48, ...), custom_call_target="tpu_custom_call" | custom-call | flops 100663296 | bytes 1572864 | tf_op jit(solution)/shard_map/pallas_call | solution.py:306
  3.2 5.8 %all-to-all-start = ((bf16[8,32,1536]{2,1,0:T(8,128)(2,1)}), bf16[8,32,1536]{2,1,0:T(8,128)(2,1)S(1)}, u32[]{:S(2)}, u32[]{:S(2)}) async-start(bf16[8,32,1536]{2,1,0:T(8,128)(2,1)} %bitcast.46), calls=%async_computation | async-start | bytes 1572864 | tf_op jit(solution)/shard_map/all_to_all | solution.py:321
  9.1 1.9 %collective-permute-start = (bf16[128,1536]{1,0:T(8,128)(2,1)S(1)}, bf16[128,1536]{1,0:T(8,128)(2,1)S(1)}, u32[]{:S(2)}, u32[]{:S(2)}) collective-permute-start(bf16[128,1536]{1,0:T(8,128)(2,1)S(1)} %bitcast.55), channel_id=1, source_target_pairs={{32,0},{64,32},{96,64},{128,96},{160,128},{192,160},{224,192},{33,... | collective-permute-start | bytes 1179656 | tf_op jit(solution)/shard_map/ppermute | solution.py:298
  11.0 0.7 copy.15.rewards_ref
  11.8 14.4 %all-to-all-done = bf16[8,32,1536]{2,1,0:T(8,128)(2,1)S(1)} async-done(((bf16[8,32,1536]{2,1,0:T(8,128)(2,1)}), bf16[8,32,1536]{2,1,0:T(8,128)(2,1)S(1)}, u32[]{:S(2)}, u32[]{:S(2)}) %all-to-all-start) | async-done | bytes 786464 | tf_op jit(solution)/shard_map/all_to_all | solution.py:321
  26.2 0.8 copy-done.12
  27.0 2.5 %shard_map.129 = (bf16[128,1536]{1,0:T(8,128)(2,1)}, bf16[256,1664]{1,0:T(8,128)(2,1)}) custom-call(s32[1]{0:T(128)} %bitcast.1.last_ref, bf16[128,1536]{1,0:T(8,128)(2,1)} %copy-done.12, bf16[128,1536]{1,0:T(8,128)(2,1)} %noise_ref.1, f32[128,1]{1,0:T(8,128)} %copy.15.rewards_ref, bf16[256,128]{1,0:T(8,128)(2,1)} %get-tuple-element.43.pick_ref, ...), custom_call_target="tpu_custom_call" | custom-call | flops 100663296 | bytes 1966080 | tf_op jit(solution)/shard_map/pallas_call | solution.py:326
  29.5 5.3 %all-to-all-start.1 = ((bf16[8,32,1664]{2,1,0:T(8,128)(2,1)}), bf16[8,32,1664]{2,1,0:T(8,128)(2,1)S(1)}, u32[]{:S(2)}, u32[]{:S(2)}) async-start(bf16[8,32,1664]{2,1,0:T(8,128)(2,1)} %bitcast.45), calls=%async_computation.1 | async-start | bytes 1703936 | tf_op jit(solution)/shard_map/all_to_all | solution.py:321
  34.8 1.5 collective-permute-start.1
  36.3 1.7 collective-permute-start.2
  38.0 15.7 %collective-permute-done.1.refs_2_.refs_1_ = bf16[256,1536]{1,0:T(8,128)(2,1)S(1)} collective-permute-done((bf16[256,1536]{1,0:T(8,128)(2,1)S(1)}, bf16[256,1536]{1,0:T(8,128)(2,1)S(1)}, u32[]{:S(2)}, u32[]{:S(2)}) %collective-permute-start.1) | collective-permute-done | bytes 786464 | tf_op jit(solution)/shard_map/ppermute | solution.py:22
  53.7 0.9 copy-done.4
  54.6 1.3 collective-permute-start.3
  55.9 2.0 %collective-permute-start.4 = (bf16[256,1664]{1,0:T(8,128)(2,1)S(1)}, bf16[256,1664]{1,0:T(8,128)(2,1)S(1)}, u32[]{:S(2)}, u32[]{:S(2)}) collective-permute-start(bf16[256,1664]{1,0:T(8,128)(2,1)S(1)} %bitcast.35), channel_id=1, source_target_pairs={{0,3},{1,0},{2,1},{3,2},{4,7},{5,4},{6,5},{7,6},{8,11},{9,8},{10,9... | collective-permute-start | bytes 2555912 | tf_op jit(solution)/shard_map/ppermute | solution.py:22
  57.9 5.8 %shard_map.130 = (bf16[256,768]{1,0:T(8,128)(2,1)}, bf16[256,768]{1,0:T(8,128)(2,1)}, bf16[256,1536]{1,0:T(8,128)(2,1)}, f32[1,256]{1,0:T(1,128)}, f32[1,1536]{1,0:T(1,128)}) custom-call(bf16[1536,768]{1,0:T(8,128)(2,1)} %bitcast.28, bf16[768,1536]{1,0:T(8,128)(2,1)} %bitcast.31, bf16[256,1536]{1,0:T(8,128)(2,1)} %bitcast.40, bf16[256,1664]{1,0:T(8,128)(2,1)} %bitcast.36), custom_call_target="tpu_custom_call" | custom-call | flops 226492416 | bytes 983040 | tf_op jit(solution)/shard_map/pallas_call | solution.py:165
  63.8 1.8 slice.43
  65.5 1.8 slice.44
  67.3 3.2 %collective-permute-start.6 = (bf16[128,1536]{1,0:T(8,128)(2,1)}, bf16[128,1536]{1,0:T(8,128)(2,1)S(1)}, u32[]{:S(2)}, u32[]{:S(2)}) collective-permute-start(bf16[128,1536]{1,0:T(8,128)(2,1)} %slice.44), channel_id=1, source_target_pairs={{0,3},{1,0},{2,1},{3,2},{4,7},{5,4},{6,5},{7,6},{8,11},{9,8},{10,9... | collective-permute-start | bytes 1179656 | tf_op jit(solution)/shard_map/ppermute | solution.py:22
  70.5 5.6 %collective-permute-done.3.refs_4_.refs_6_ = bf16[256,1664]{1,0:T(8,128)(2,1)S(1)} collective-permute-done((bf16[256,1664]{1,0:T(8,128)(2,1)S(1)}, bf16[256,1664]{1,0:T(8,128)(2,1)S(1)}, u32[]{:S(2)}, u32[]{:S(2)}) %collective-permute-start.3) | collective-permute-done | bytes 852000 | tf_op jit(solution)/shard_map/ppermute | solution.py:22
  76.1 0.6 collective-permute-done.4.refs_5_.refs_7_
  77.0 0.9 copy-done.3
  78.0 8.4 %shard_map.131 = (bf16[512,768]{1,0:T(8,128)(2,1)}, bf16[512,768]{1,0:T(8,128)(2,1)}, bf16[512,1536]{1,0:T(8,128)(2,1)}, f32[1,512]{1,0:T(1,128)}, f32[1,1536]{1,0:T(1,128)}) custom-call(bf16[1536,768]{1,0:T(8,128)(2,1)} %bitcast.29, bf16[768,1536]{1,0:T(8,128)(2,1)} %bitcast.32, bf16[256,1536]{1,0:T(8,128)(2,1)} %copy-done.4, ...), custom_call_target="tpu_custom_call" | custom-call | flops 452984832 | bytes 1376256 | tf_op jit(solution)/shard_map/pallas_call | solution.py:165
  86.3 1.2 slice.56
  87.5 1.2 collective-permute-start.7
  88.6 1.0 slice.57
  89.7 2.4 %collective-permute-start.8 = (bf16[128,1664]{1,0:T(8,128)(2,1)S(1)}, bf16[128,1664]{1,0:T(8,128)(2,1)S(1)}, u32[]{:S(2)}, u32[]{:S(2)}) collective-permute-start(bf16[128,1664]{1,0:T(8,128)(2,1)S(1)} %slice.57), channel_id=1, source_target_pairs={{0,3},{1,0},{2,1},{3,2},{4,7},{5,4},{6,5},{7,6},{8,11},{9,8},{10,9... | collective-permute-start | bytes 1277960 | tf_op jit(solution)/shard_map/ppermute | solution.py:22
  92.1 0.9 fusion.2
  93.0 1.4 collective-permute-start.9
  94.5 0.6 collective-permute-start.10
  95.1 4.2 %collective-permute-done.7.refs_4_.refs_8_ = bf16[128,1664]{1,0:T(8,128)(2,1)S(1)} collective-permute-done((bf16[128,1664]{1,0:T(8,128)(2,1)S(1)}, bf16[128,1664]{1,0:T(8,128)(2,1)S(1)}, u32[]{:S(2)}, u32[]{:S(2)}) %collective-permute-start.7) | collective-permute-done | bytes 426016 | tf_op jit(solution)/shard_map/ppermute | solution.py:22
  99.2 1.7 collective-permute-done.8.refs_5_.refs_9_
  101.0 0.8 copy-done.7
  101.7 5.8 %shard_map.132 = (bf16[256,768]{1,0:T(8,128)(2,1)}, bf16[256,768]{1,0:T(8,128)(2,1)}, bf16[256,1536]{1,0:T(8,128)(2,1)}, f32[1,256]{1,0:T(1,128)}, f32[1,1536]{1,0:T(1,128)}) custom-call(bf16[1536,768]{1,0:T(8,128)(2,1)} %bitcast.30, bf16[768,1536]{1,0:T(8,128)(2,1)} %bitcast.33, bf16[128,1536]{1,0:T(8,128)(2,1)} %copy-done.8, bf16[128,1536]{1,0:T(8,128)(2,1)} %copy-done.9, ...), custom_call_target="tpu_custom_call" | custom-call | flops 226492416 | bytes 983040 | tf_op jit(solution)/shard_map/pallas_call | solution.py:165
  107.6 1.9 %fusion.3 = (bf16[128,1536]{1,0:T(8,128)(2,1)}, bf16[128,1536]{1,0:T(8,128)(2,1)S(1)}) fusion(bf16[256,1536]{1,0:T(8,128)(2,1)} %get-tuple-element.56), kind=kLoop, calls=%fused_computation.15 | loop fusion | bytes 1572864 | tf_op jit(solution)/shard_map/slice | solution.py:348
  109.5 2.9 %collective-permute-start.11 = (bf16[128,1536]{1,0:T(8,128)(2,1)}, bf16[128,1536]{1,0:T(8,128)(2,1)S(1)}, u32[]{:S(2)}, u32[]{:S(2)}) collective-permute-start(bf16[128,1536]{1,0:T(8,128)(2,1)} %get-tuple-element.83), channel_id=1, source_target_pairs={{0,3},{1,0},{2,1},{3,2},{4,7},{5,4},{6,5},{7,6},{8,11},{9,8},{10,9... | collective-permute-start | bytes 1179656 | tf_op jit(solution)/shard_map/ppermute | solution.py:22
  112.4 1.5 shard_map.133
  113.9 1.4 all_to_all.18
  115.3 10.0 %all-to-all-start.3 = ((f32[32,1,32]{2,1,0:T(1,128)}), f32[32,1,32]{2,1,0:T(1,128)S(1)}, u32[]{:S(2)}, u32[]{:S(2)}) async-start(f32[32,1,32]{2,1,0:T(1,128)} %bitcast.17), calls=%async_computation.3 | async-start | bytes 32768 | tf_op jit(solution)/shard_map/all_to_all | solution.py:367
  125.3 8.2 %all-to-all-done.3 = f32[32,1,32]{2,1,0:T(1,128)S(1)} async-done(((f32[32,1,32]{2,1,0:T(1,128)}), f32[32,1,32]{2,1,0:T(1,128)S(1)}, u32[]{:S(2)}, u32[]{:S(2)}) %all-to-all-start.3) | async-done | bytes 4128 | tf_op jit(solution)/shard_map/all_to_all | solution.py:367
  133.5 0.5 broadcast.3
  134.0 0.7 reduce.3
  134.7 0.7 reshape.54.dg_ref
  135.3 2.5 %shard_map.134 = (f32[8,1536]{1,0:T(8,128)}, f32[128,128]{1,0:T(8,128)}) custom-call(f32[8,128]{1,0:T(8,128)} %reshape.54.dg_ref, bf16[256,128]{1,0:T(8,128)(2,1)} %get-tuple-element.43.pick_ref, s32[2,128]{1,0:T(2,128)} %bitcast.51, f32[1,128]{1,0:T(1,128)} %get-tuple-element.62.g_ref, bf16[128,1536]{1,0:T(8,128)(2,1)} %get-tuple-element.63.xn_ref), custom_call_target="tpu_custom_call" | custom-call | flops 2359296 | bytes 49152 | tf_op jit(solution)/shard_map/pallas_call | solution.py:370
  137.8 0.9 pad_maximum_fusion.1
  138.7 0.7 collective-permute-start.15
  139.5 1.2 collective-permute-start.12
  140.8 0.9 collective-permute-start.14
  141.7 2.6 %collective-permute-done.15 = f32[9,1536]{1,0:T(8,128)S(1)} collective-permute-done((f32[9,1536]{1,0:T(8,128)S(1)}, f32[9,1536]{1,0:T(8,128)S(1)}, u32[]{:S(2)}, u32[]{:S(2)}) %collective-permute-start.15) | collective-permute-done | bytes 55328 | tf_op jit(solution)/shard_map/ppermute | solution.py:27
  144.2 0.7 collective-permute-start.17
  144.9 1.2 collective-permute-start.18
  146.1 2.3 %collective-permute-start.16 = (f32[9,1536]{1,0:T(8,128)S(1)}, f32[9,1536]{1,0:T(8,128)S(1)}, u32[]{:S(2)}, u32[]{:S(2)}) collective-permute-start(f32[9,1536]{1,0:T(8,128)S(1)} %fusion.1), channel_id=1, source_target_pairs={{0,16},{4,20},{8,24},{12,28},{16,0},{20,4},{24,8},{28,12},{1,17},{... | collective-permute-start | bytes 165896 | tf_op jit(solution)/shard_map/ppermute | solution.py:27
  148.4 3.1 %collective-permute-done.12 = bf16[128,1536]{1,0:T(8,128)(2,1)S(1)} collective-permute-done((bf16[128,1536]{1,0:T(8,128)(2,1)S(1)}, bf16[128,1536]{1,0:T(8,128)(2,1)S(1)}, u32[]{:S(2)}, u32[]{:S(2)}) %collective-permute-start.12) | collective-permute-done | bytes 393248 | tf_op jit(solution)/shard_map/ppermute | solution.py:22
  151.6 2.1 %collective-permute-done.14 = bf16[128,1536]{1,0:T(8,128)(2,1)S(1)} collective-permute-done((bf16[128,1536]{1,0:T(8,128)(2,1)S(1)}, bf16[128,1536]{1,0:T(8,128)(2,1)S(1)}, u32[]{:S(2)}, u32[]{:S(2)}) %collective-permute-start.14) | collective-permute-done | bytes 393248 | tf_op jit(solution)/shard_map/ppermute | solution.py:22
  153.7 1.4 add_convert_fusion.2
  155.1 0.9 pad_maximum_fusion
  156.0 3.5 %all-to-all-start.2 = ((bf16[8,32,1536]{2,1,0:T(8,128)(2,1)}), bf16[8,32,1536]{2,1,0:T(8,128)(2,1)S(1)}, u32[]{:S(2)}, u32[]{:S(2)}) async-start(bf16[8,32,1536]{2,1,0:T(8,128)(2,1)} %bitcast.14), calls=%async_computation.2 | async-start | bytes 1572864 | tf_op jit(solution)/shard_map/all_to_all | solution.py:321
  159.6 0.3 collective-permute-start.20
  159.9 0.8 collective-permute-start.21
  160.7 3.3 %collective-permute-start.19 = (f32[9,1536]{1,0:T(8,128)S(1)}, f32[9,1536]{1,0:T(8,128)S(1)}, u32[]{:S(2)}, u32[]{:S(2)}) collective-permute-start(f32[9,1536]{1,0:T(8,128)S(1)} %add_add_fusion.1), channel_id=1, source_target_pairs={{0,2},{1,3},{2,0},{3,1},{4,6},{5,7},{6,4},{7,5},{8,10},{9,11},{10,... | collective-permute-start | bytes 165896 | tf_op jit(solution)/shard_map/ppermute | solution.py:27
  164.0 10.3 %shard_map.136 = (bf16[1536,768]{1,0:T(8,128)(2,1)}, bf16[768,1536]{1,0:T(8,128)(2,1)}) custom-call(bf16[256,1536]{1,0:T(8,128)(2,1)} %bitcast.41, bf16[256,1536]{1,0:T(8,128)(2,1)} %copy-done.4, bf16[256,1536]{1,0:T(8,128)(2,1)} %collective-permute-done.2.refs_3_.refs_2_, bf16[128,1536]{1,0:T(8,128)(2,1)} %copy-done.8, bf16[128,1536]{1,0:T(8,128)(2,1)} %copy-done.9, ...), custom_call_target="tpu_custom_call" | custom-call | flops 603979776 | bytes 1769472 | tf_op jit(solution)/shard_map/pallas_call | solution.py:199
  174.4 0.6 multiply_reduce_fusion
  175.1 0.6 fusion
  175.7 0.9 copy-done.5
  176.6 3.1 %shard_map.135 = bf16[128,1536]{1,0:T(8,128)(2,1)} custom-call(bf16[128,1536]{1,0:T(8,128)(2,1)} %bitcast.44, f32[1,1536]{1,0:T(1,128)} %gain_ref.3, bf16[128,1536]{1,0:T(8,128)(2,1)} %get-tuple-element.45.cot_ref, bf16[256,1536]{1,0:T(8,128)(2,1)} %bitcast.42, bf16[128,256]{1,0:T(8,128)(2,1)} %get-tuple-element.58.back_ref, ...), custom_call_target="tpu_custom_call" | custom-call | flops 100663296 | bytes 2359296 | tf_op jit(solution)/shard_map/pallas_call | solution.py:388
  (60 shorter events, 0.7 us)
Async XLA Ops:
  0.6 8.4 %copy-start.20 = (bf16[1,128,1536]{2,1,0:T(8,128)(2,1)S(1)}, bf16[1,128,1536]{2,1,0:T(8,128)(2,1)}, u32[]{:S(2)}) copy-start(bf16[1,128,1536]{2,1,0:T(8,128)(2,1)} %param.10) | copy-start | bytes 1179652
  0.6 10.4 %copy-start.19 = (f32[128]{0:T(128)S(1)}, f32[128]{0:T(128)}, u32[]{:S(2)}) copy-start(f32[128]{0:T(128)} %param.12) | copy-start | bytes 1540
  3.2 22.9 %all-to-all-start = ((bf16[8,32,1536]{2,1,0:T(8,128)(2,1)}), bf16[8,32,1536]{2,1,0:T(8,128)(2,1)S(1)}, u32[]{:S(2)}, u32[]{:S(2)}) async-start(bf16[8,32,1536]{2,1,0:T(8,128)(2,1)} %bitcast.46), calls=%async_computation | async-start | bytes 1572864 | tf_op jit(solution)/shard_map/all_to_all | solution.py:321
  9.1 17.1 %collective-permute-start = (bf16[128,1536]{1,0:T(8,128)(2,1)S(1)}, bf16[128,1536]{1,0:T(8,128)(2,1)S(1)}, u32[]{:S(2)}, u32[]{:S(2)}) collective-permute-start(bf16[128,1536]{1,0:T(8,128)(2,1)S(1)} %bitcast.55), channel_id=1, source_target_pairs={{32,0},{64,32},{96,64},{128,96},{160,128},{192,160},{224,192},{33,... | collective-permute-start | bytes 1179656 | tf_op jit(solution)/shard_map/ppermute | solution.py:298
  26.2 31.8 %copy-start.1 = (bf16[8,32,1536]{2,1,0:T(8,128)(2,1)}, bf16[8,32,1536]{2,1,0:T(8,128)(2,1)S(1)}, u32[]{:S(2)}) copy-start(bf16[8,32,1536]{2,1,0:T(8,128)(2,1)S(1)} %all-to-all-done) | copy-start | bytes 2359300
  26.2 0.8 copy-start.12
  29.5 25.1 %all-to-all-start.1 = ((bf16[8,32,1664]{2,1,0:T(8,128)(2,1)}), bf16[8,32,1664]{2,1,0:T(8,128)(2,1)S(1)}, u32[]{:S(2)}, u32[]{:S(2)}) async-start(bf16[8,32,1664]{2,1,0:T(8,128)(2,1)} %bitcast.45), calls=%async_computation.1 | async-start | bytes 1703936 | tf_op jit(solution)/shard_map/all_to_all | solution.py:321
  34.8 18.9 %collective-permute-start.1 = (bf16[256,1536]{1,0:T(8,128)(2,1)S(1)}, bf16[256,1536]{1,0:T(8,128)(2,1)S(1)}, u32[]{:S(2)}, u32[]{:S(2)}) collective-permute-start(bf16[256,1536]{1,0:T(8,128)(2,1)S(1)} %bitcast.38), channel_id=1, source_target_pairs={{0,1},{1,2},{2,3},{3,0},{4,5},{5,6},{6,7},{7,4},{8,9},{9,10},{10,1... | collective-permute-start | bytes 2359304 | tf_op jit(solution)/shard_map/ppermute | solution.py:22
  36.3 18.3 %collective-permute-start.2 = (bf16[256,1536]{1,0:T(8,128)(2,1)S(1)}, bf16[256,1536]{1,0:T(8,128)(2,1)}, u32[]{:S(2)}, u32[]{:S(2)}) collective-permute-start(bf16[256,1536]{1,0:T(8,128)(2,1)S(1)} %bitcast.39), channel_id=1, source_target_pairs={{0,3},{1,0},{2,1},{3,2},{4,7},{5,4},{6,5},{7,6},{8,11},{9,8},{10,9... | collective-permute-start | bytes 2359304 | tf_op jit(solution)/shard_map/ppermute | solution.py:22
  53.7 0.9 copy-start.4
  54.6 3.3 %copy-start = (bf16[8,32,1664]{2,1,0:T(8,128)(2,1)}, bf16[8,32,1664]{2,1,0:T(8,128)(2,1)S(1)}, u32[]{:S(2)}) copy-start(bf16[8,32,1664]{2,1,0:T(8,128)(2,1)S(1)} %all-to-all-done.1) | copy-start | bytes 2555908
  54.6 21.5 %collective-permute-start.3 = (bf16[256,1664]{1,0:T(8,128)(2,1)S(1)}, bf16[256,1664]{1,0:T(8,128)(2,1)S(1)}, u32[]{:S(2)}, u32[]{:S(2)}) collective-permute-start(bf16[256,1664]{1,0:T(8,128)(2,1)S(1)} %bitcast.34), channel_id=1, source_target_pairs={{0,1},{1,2},{2,3},{3,0},{4,5},{5,6},{6,7},{7,4},{8,9},{9,10},{10,1... | collective-permute-start | bytes 2555912 | tf_op jit(solution)/shard_map/ppermute | solution.py:22
  55.9 20.9 %collective-permute-start.4 = (bf16[256,1664]{1,0:T(8,128)(2,1)S(1)}, bf16[256,1664]{1,0:T(8,128)(2,1)S(1)}, u32[]{:S(2)}, u32[]{:S(2)}) collective-permute-start(bf16[256,1664]{1,0:T(8,128)(2,1)S(1)} %bitcast.35), channel_id=1, source_target_pairs={{0,3},{1,0},{2,1},{3,2},{4,7},{5,4},{6,5},{7,6},{8,11},{9,8},{10,9... | collective-permute-start | bytes 2555912 | tf_op jit(solution)/shard_map/ppermute | solution.py:22
  65.5 28.9 %collective-permute-start.5 = (bf16[128,1536]{1,0:T(8,128)(2,1)}, bf16[128,1536]{1,0:T(8,128)(2,1)S(1)}, u32[]{:S(2)}, u32[]{:S(2)}) collective-permute-start(bf16[128,1536]{1,0:T(8,128)(2,1)} %slice.43), channel_id=1, source_target_pairs={{0,1},{1,2},{2,3},{3,0},{4,5},{5,6},{6,7},{7,4},{8,9},{9,10},{10,1... | collective-permute-start | bytes 1179656 | tf_op jit(solution)/shard_map/ppermute | solution.py:22
  67.3 27.8 %collective-permute-start.6 = (bf16[128,1536]{1,0:T(8,128)(2,1)}, bf16[128,1536]{1,0:T(8,128)(2,1)S(1)}, u32[]{:S(2)}, u32[]{:S(2)}) collective-permute-start(bf16[128,1536]{1,0:T(8,128)(2,1)} %slice.44), channel_id=1, source_target_pairs={{0,3},{1,0},{2,1},{3,2},{4,7},{5,4},{6,5},{7,6},{8,11},{9,8},{10,9... | collective-permute-start | bytes 1179656 | tf_op jit(solution)/shard_map/ppermute | solution.py:22
  76.1 0.9 copy-start.2
  77.0 0.9 copy-start.3
  86.3 5.8 %copy-start.10 = (bf16[512,1536]{1,0:T(8,128)(2,1)S(1)}, bf16[512,1536]{1,0:T(8,128)(2,1)}, u32[]{:S(2)}) copy-start(bf16[512,1536]{1,0:T(8,128)(2,1)} %get-tuple-element.52) | copy-start | bytes 4718596
  87.5 11.8 %collective-permute-start.7 = (bf16[128,1664]{1,0:T(8,128)(2,1)S(1)}, bf16[128,1664]{1,0:T(8,128)(2,1)S(1)}, u32[]{:S(2)}, u32[]{:S(2)}) collective-permute-start(bf16[128,1664]{1,0:T(8,128)(2,1)S(1)} %slice.56), channel_id=1, source_target_pairs={{0,1},{1,2},{2,3},{3,0},{4,5},{5,6},{6,7},{7,4},{8,9},{9,10},{10,1... | collective-permute-start | bytes 1277960 | tf_op jit(solution)/shard_map/ppermute | solution.py:22
  89.7 11.3 %collective-permute-start.8 = (bf16[128,1664]{1,0:T(8,128)(2,1)S(1)}, bf16[128,1664]{1,0:T(8,128)(2,1)S(1)}, u32[]{:S(2)}, u32[]{:S(2)}) collective-permute-start(bf16[128,1664]{1,0:T(8,128)(2,1)S(1)} %slice.57), channel_id=1, source_target_pairs={{0,3},{1,0},{2,1},{3,2},{4,7},{5,4},{6,5},{7,6},{8,11},{9,8},{10,9... | collective-permute-start | bytes 1277960 | tf_op jit(solution)/shard_map/ppermute | solution.py:22
  93.0 19.4 %collective-permute-start.9 = (bf16[128,1536]{1,0:T(8,128)(2,1)}, bf16[128,1536]{1,0:T(8,128)(2,1)}, u32[]{:S(2)}, u32[]{:S(2)}) collective-permute-start(bf16[128,1536]{1,0:T(8,128)(2,1)} %get-tuple-element.80), channel_id=1, source_target_pairs={{0,3},{1,0},{2,1},{3,2},{4,7},{5,4},{6,5},{7,6},{8,11},{9,8},{10,9... | collective-permute-start | bytes 1179656 | tf_op jit(solution)/shard_map/ppermute | solution.py:22
  94.5 6.5 %copy-start.8 = (bf16[128,1536]{1,0:T(8,128)(2,1)}, bf16[128,1536]{1,0:T(8,128)(2,1)S(1)}, u32[]{:S(2)}) copy-start(bf16[128,1536]{1,0:T(8,128)(2,1)S(1)} %collective-permute-done.5.refs_2_.refs_3_) | copy-start | bytes 1179652
  94.5 18.0 %collective-permute-start.10 = (bf16[128,1536]{1,0:T(8,128)(2,1)}, bf16[128,1536]{1,0:T(8,128)(2,1)}, u32[]{:S(2)}, u32[]{:S(2)}) collective-permute-start(bf16[128,1536]{1,0:T(8,128)(2,1)} %get-tuple-element.79), channel_id=1, source_target_pairs={{0,1},{1,2},{2,3},{3,0},{4,5},{5,6},{6,7},{7,4},{8,9},{9,10},{10,1... | collective-permute-start | bytes 1179656 | tf_op jit(solution)/shard_map/ppermute | solution.py:22
  95.1 5.9 %copy-start.9 = (bf16[128,1536]{1,0:T(8,128)(2,1)}, bf16[128,1536]{1,0:T(8,128)(2,1)S(1)}, u32[]{:S(2)}) copy-start(bf16[128,1536]{1,0:T(8,128)(2,1)S(1)} %collective-permute-done.6.refs_3_.refs_4_) | copy-start | bytes 1179652
  99.2 1.7 copy-start.6
  101.0 0.8 copy-start.7
  107.5 17.7 %copy-start.16 = (f32[1,1536]{1,0:T(1,128)S(1)}, f32[1,1536]{1,0:T(1,128)}, u32[]{:S(2)}) copy-start(f32[1,1536]{1,0:T(1,128)} %get-tuple-element.74) | copy-start | bytes 18436
  107.5 17.7 %copy-start.17 = (f32[1,1536]{1,0:T(1,128)S(1)}, f32[1,1536]{1,0:T(1,128)}, u32[]{:S(2)}) copy-start(f32[1,1536]{1,0:T(1,128)} %get-tuple-element.75) | copy-start | bytes 18436
  107.5 17.7 %copy-start.18 = (f32[1,1536]{1,0:T(1,128)S(1)}, f32[1,1536]{1,0:T(1,128)}, u32[]{:S(2)}) copy-start(f32[1,1536]{1,0:T(1,128)} %get-tuple-element.76) | copy-start | bytes 18436
  109.5 29.9 %collective-permute-start.11 = (bf16[128,1536]{1,0:T(8,128)(2,1)}, bf16[128,1536]{1,0:T(8,128)(2,1)S(1)}, u32[]{:S(2)}, u32[]{:S(2)}) collective-permute-start(bf16[128,1536]{1,0:T(8,128)(2,1)} %get-tuple-element.83), channel_id=1, source_target_pairs={{0,3},{1,0},{2,1},{3,2},{4,7},{5,4},{6,5},{7,6},{8,11},{9,8},{10,9... | collective-permute-start | bytes 1179656 | tf_op jit(solution)/shard_map/ppermute | solution.py:22
  112.4 26.9 %collective-permute-start.13 = (bf16[128,1536]{1,0:T(8,128)(2,1)S(1)}, bf16[128,1536]{1,0:T(8,128)(2,1)S(1)}, u32[]{:S(2)}, u32[]{:S(2)}) collective-permute-start(bf16[128,1536]{1,0:T(8,128)(2,1)S(1)} %get-tuple-element.84), channel_id=1, source_target_pairs={{0,1},{1,2},{2,3},{3,0},{4,5},{5,6},{6,7},{7,4},{8,9},{9,10},{10,1... | collective-permute-start | bytes 1179656 | tf_op jit(solution)/shard_map/ppermute | solution.py:22
  115.3 18.2 %all-to-all-start.3 = ((f32[32,1,32]{2,1,0:T(1,128)}), f32[32,1,32]{2,1,0:T(1,128)S(1)}, u32[]{:S(2)}, u32[]{:S(2)}) async-start(f32[32,1,32]{2,1,0:T(1,128)} %bitcast.17), calls=%async_computation.3 | async-start | bytes 32768 | tf_op jit(solution)/shard_map/all_to_all | solution.py:367
  135.3 18.3 %copy-start.11 = (bf16[256,1536]{1,0:T(8,128)(2,1)S(1)}, bf16[256,1536]{1,0:T(8,128)(2,1)}, u32[]{:S(2)}) copy-start(bf16[256,1536]{1,0:T(8,128)(2,1)} %get-tuple-element.48) | copy-start | bytes 2359300
  137.8 6.4 %copy-start.14 = (f32[8,1536]{1,0:T(8,128)S(1)}, f32[8,1536]{1,0:T(8,128)}, u32[]{:S(2)}) copy-start(f32[8,1536]{1,0:T(8,128)} %get-tuple-element.73) | copy-start | bytes 147460
  138.7 5.5 %collective-permute-start.15 = (f32[9,1536]{1,0:T(8,128)S(1)}, f32[9,1536]{1,0:T(8,128)S(1)}, u32[]{:S(2)}, u32[]{:S(2)}) collective-permute-start(f32[9,1536]{1,0:T(8,128)S(1)} %pad_maximum_fusion.1), channel_id=1, source_target_pairs={{0,4},{4,0},{8,12},{12,8},{16,20},{20,16},{24,28},{28,24},{1,5},{5... | collective-permute-start | bytes 165896 | tf_op jit(solution)/shard_map/ppermute | solution.py:27
  139.5 12.0 %collective-permute-start.12 = (bf16[128,1536]{1,0:T(8,128)(2,1)S(1)}, bf16[128,1536]{1,0:T(8,128)(2,1)S(1)}, u32[]{:S(2)}, u32[]{:S(2)}) collective-permute-start(bf16[128,1536]{1,0:T(8,128)(2,1)S(1)} %get-tuple-element.77), channel_id=1, source_target_pairs={{0,3},{1,0},{2,1},{3,2},{4,7},{5,4},{6,5},{7,6},{8,11},{9,8},{10,9... | collective-permute-start | bytes 1179656 | tf_op jit(solution)/shard_map/ppermute | solution.py:22
  140.8 12.9 %collective-permute-start.14 = (bf16[128,1536]{1,0:T(8,128)(2,1)S(1)}, bf16[128,1536]{1,0:T(8,128)(2,1)S(1)}, u32[]{:S(2)}, u32[]{:S(2)}) collective-permute-start(bf16[128,1536]{1,0:T(8,128)(2,1)S(1)} %get-tuple-element.78), channel_id=1, source_target_pairs={{0,1},{1,2},{2,3},{3,0},{4,5},{5,6},{6,7},{7,4},{8,9},{9,10},{10,1... | collective-permute-start | bytes 1179656 | tf_op jit(solution)/shard_map/ppermute | solution.py:22
  144.2 15.3 %collective-permute-start.17 = (f32[9,1536]{1,0:T(8,128)S(1)}, f32[9,1536]{1,0:T(8,128)S(1)}, u32[]{:S(2)}, u32[]{:S(2)}) collective-permute-start(f32[9,1536]{1,0:T(8,128)S(1)} %fusion.1), channel_id=1, source_target_pairs={{0,8},{4,12},{8,0},{12,4},{16,24},{20,28},{24,16},{28,20},{1,9},{5... | collective-permute-start | bytes 165896 | tf_op jit(solution)/shard_map/ppermute | solution.py:27
  144.9 14.6 %collective-permute-start.18 = (f32[9,1536]{1,0:T(8,128)S(1)}, f32[9,1536]{1,0:T(8,128)S(1)}, u32[]{:S(2)}, u32[]{:S(2)}) collective-permute-start(f32[9,1536]{1,0:T(8,128)S(1)} %fusion.1), channel_id=1, source_target_pairs={{0,24},{4,28},{8,16},{12,20},{16,8},{20,12},{24,0},{28,4},{1,25},{... | collective-permute-start | bytes 165896 | tf_op jit(solution)/shard_map/ppermute | solution.py:27
  146.1 13.5 %collective-permute-start.16 = (f32[9,1536]{1,0:T(8,128)S(1)}, f32[9,1536]{1,0:T(8,128)S(1)}, u32[]{:S(2)}, u32[]{:S(2)}) collective-permute-start(f32[9,1536]{1,0:T(8,128)S(1)} %fusion.1), channel_id=1, source_target_pairs={{0,16},{4,20},{8,24},{12,28},{16,0},{20,4},{24,8},{28,12},{1,17},{... | collective-permute-start | bytes 165896 | tf_op jit(solution)/shard_map/ppermute | solution.py:27
  156.0 19.7 %all-to-all-start.2 = ((bf16[8,32,1536]{2,1,0:T(8,128)(2,1)}), bf16[8,32,1536]{2,1,0:T(8,128)(2,1)S(1)}, u32[]{:S(2)}, u32[]{:S(2)}) async-start(bf16[8,32,1536]{2,1,0:T(8,128)(2,1)} %bitcast.14), calls=%async_computation.2 | async-start | bytes 1572864 | tf_op jit(solution)/shard_map/all_to_all | solution.py:321
  159.6 14.8 %collective-permute-start.20 = (f32[9,1536]{1,0:T(8,128)S(1)}, f32[9,1536]{1,0:T(8,128)S(1)}, u32[]{:S(2)}, u32[]{:S(2)}) collective-permute-start(f32[9,1536]{1,0:T(8,128)S(1)} %add_add_fusion.1), channel_id=1, source_target_pairs={{0,1},{1,0},{2,3},{3,2},{4,5},{5,4},{6,7},{7,6},{8,9},{9,8},{10,11... | collective-permute-start | bytes 165896 | tf_op jit(solution)/shard_map/ppermute | solution.py:27
  159.9 14.4 %collective-permute-start.21 = (f32[9,1536]{1,0:T(8,128)S(1)}, f32[9,1536]{1,0:T(8,128)S(1)}, u32[]{:S(2)}, u32[]{:S(2)}) collective-permute-start(f32[9,1536]{1,0:T(8,128)S(1)} %add_add_fusion.1), channel_id=1, source_target_pairs={{0,3},{1,2},{2,1},{3,0},{4,7},{5,6},{6,5},{7,4},{8,11},{9,10},{10,... | collective-permute-start | bytes 165896 | tf_op jit(solution)/shard_map/ppermute | solution.py:27
  160.7 13.6 %collective-permute-start.19 = (f32[9,1536]{1,0:T(8,128)S(1)}, f32[9,1536]{1,0:T(8,128)S(1)}, u32[]{:S(2)}, u32[]{:S(2)}) collective-permute-start(f32[9,1536]{1,0:T(8,128)S(1)} %add_add_fusion.1), channel_id=1, source_target_pairs={{0,2},{1,3},{2,0},{3,1},{4,6},{5,7},{6,4},{7,5},{8,10},{9,11},{10,... | collective-permute-start | bytes 165896 | tf_op jit(solution)/shard_map/ppermute | solution.py:27
  164.0 10.4 %copy-start.13 = (bf16[1,1536,8]{1,2,0:T(8,128)(2,1)S(1)}, bf16[1,1536,8]{1,2,0:T(8,128)(2,1)}, u32[]{:S(2)}) copy-start(bf16[1,1536,8]{1,2,0:T(8,128)(2,1)} %param.16) | copy-start | bytes 73732
  164.0 11.0 %copy-start.15 = (f32[1,1536]{1,0:T(1,128)S(1)}, f32[1,1536]{1,0:T(1,128)}, u32[]{:S(2)}) copy-start(f32[1,1536]{1,0:T(1,128)} %gain_ref.3) | copy-start | bytes 18436
  175.7 0.9 copy-start.5

commit v3 on v2

v3 whole, which is shorter than its diff:
```python
import functools

import jax
import jax.numpy as jnp
from jax import lax
from jax.experimental import pallas as pl
from jax.experimental.pallas import tpu as pltpu
from jax.sharding import Mesh, PartitionSpec as P

gelu_scale = 0.7978845608028654
cubic_coef = 0.044715
norm_eps = 1e-06
lane = 128
bf16 = jnp.bfloat16
f32 = jnp.float32
room = 60 << 20
cheaper = 100


def shift(value, axis, steps):
    count = lax.axis_size(axis)
    return lax.ppermute(value, axis, [(i, (i + steps) % count) for i in range(count)])


def swap(value, axis, mask):
    count = lax.axis_size(axis)
    return lax.ppermute(value, axis, [(i, i ^ mask) for i in range(count)])


def total_over(value):
    value = value + swap(value, "e", 1)
    for axis, unit in (("e", 2), ("x", 1)):
        one, two, three = (swap(value, axis, unit * mask) for mask in (1, 2, 3))
        value = (value + two) + (one + three)
    return value


def after(value, *done):
    return lax.optimization_barrier((value,) + done)[0]


def dot(a, b, dims):
    return lax.dot_general(a, b, (dims, ((), ())), preferred_element_type=f32)


def exact(a, b, dims):
    return lax.dot_general(
        a, b, (dims, ((), ())), preferred_element_type=f32, precision=lax.Precision.HIGHEST
    )


def like(shape, dtype):
    return jax.ShapeDtypeStruct(shape, dtype)


def call(kernel, out, flops, moved, **options):
    return pl.pallas_call(
        kernel,
        out_shape=out,
        cost_estimate=pl.CostEstimate(flops=flops, bytes_accessed=moved, transcendentals=0),
        compiler_params=pltpu.CompilerParams(vmem_limit_bytes=room),
        **options,
    )


def scalar():
    return pl.BlockSpec(memory_space=pltpu.SMEM)


def whole():
    return pl.BlockSpec(memory_space=pltpu.VMEM)


def one_hots(routes, experts, tok_count):
    ids = lax.broadcasted_iota(jnp.int32, (experts, tok_count), 0)
    return (ids == routes[0:1, :]).astype(f32), (ids == routes[1:2, :]).astype(f32)


def token_kernel(
    capacity, x_ref, gain_ref, router_ref, routes_ref, slots_ref, pick_ref, info_ref, back_ref
):
    tok_count = x_ref.shape[0]
    experts = router_ref.shape[0]
    slots = experts * capacity
    x32 = x_ref[...].astype(f32)
    inv = lax.rsqrt(jnp.mean(x32 * x32, -1, keepdims=True) + norm_eps)
    xn = (x32 * inv * gain_ref[...]).astype(bf16)
    logits = dot(router_ref[...], xn, ((1,), (1,)))
    first, second = one_hots(routes_ref[...], experts, tok_count)
    named = first + second
    g1 = jax.nn.sigmoid(
        jnp.sum(first * logits, 0, keepdims=True) - jnp.sum(second * logits, 0, keepdims=True)
    )
    gates = first * g1 + second * (1.0 - g1)
    row = lax.broadcasted_iota(jnp.int32, (tok_count, tok_count), 0)
    col = lax.broadcasted_iota(jnp.int32, (tok_count, tok_count), 1)
    earlier = (row < col).astype(f32).astype(bf16)
    place = dot(named.astype(bf16), earlier, ((1,), (0,)))
    place = jnp.where(named > 0, place, -1.0)
    slot = lax.broadcasted_iota(jnp.int32, (capacity, tok_count), 0).astype(f32)
    chosen = jnp.concatenate(
        [(slot == place[e : e + 1, :]).astype(f32) for e in range(experts)], 0
    )
    ids = routes_ref[...].astype(f32)
    other = first * ids[1:2, :] + second * ids[0:1, :]
    product = jnp.broadcast_to(g1 * (1.0 - g1), gates.shape)

    def per_slot(table):
        wide = jnp.concatenate(
            [jnp.broadcast_to(table[e : e + 1, :], (capacity, tok_count)) for e in range(experts)],
            0,
        )
        return jnp.sum(chosen * wide, -1, keepdims=True)

    pick = chosen.astype(bf16)
    pick_ref[...] = pick
    back_ref[...] = chosen.T.astype(bf16)
    slope = per_slot(product)
    coarse = slope.astype(bf16).astype(f32)
    place = lax.broadcasted_iota(jnp.int32, (slots, lane), 1)
    info = jnp.where(place == 0, per_slot(gates), 0.0)
    info = jnp.where(place == 1, coarse, info)
    info = jnp.where(place == 2, slope - coarse, info)
    info = jnp.where(place == 3, per_slot(other), info)
    info_ref[...] = info.astype(bf16)
    slots_ref[...] = dot(pick, xn, ((1,), (0,))).astype(bf16)


def cot_kernel(last_ref, arrived_ref, noise_ref, rewards_ref, pick_ref, info_ref, cot_ref, slots_ref):
    width = arrived_ref.shape[1]
    own = (-rewards_ref[...] * noise_ref[...].astype(f32)).astype(bf16)
    last = last_ref[0] == 1
    cot = jnp.where(last, own.astype(f32), arrived_ref[...].astype(f32)).astype(bf16)
    cot_ref[...] = cot
    slots_ref[:, :width] = dot(pick_ref[...], cot, ((1,), (0,))).astype(bf16)
    slots_ref[:, width:] = info_ref[...]


def in_words(value, axis):
    words = []
    for _ in range(3):
        word = value.astype(bf16).astype(f32)
        words.append(word)
        value = value - word
    return jnp.concatenate(words, axis).astype(bf16)


def from_words(value):
    rows = value.shape[0] // 3
    return value[:rows] + (value[rows : 2 * rows] + value[2 * rows :])


def expert_rows(xn, cot, info, up, down, router, mine):
    rows = xn.shape[0]
    experts = router.shape[0]
    gate = info[:, 0:1]
    pre = dot(xn, up, ((1,), (0,)))
    dh = dot(cot, down, ((1,), (1,)))
    square = pre * pre
    tangent = jnp.tanh(gelu_scale * pre * (1.0 + cubic_coef * square))
    hidden = 0.5 * pre * (1.0 + tangent)
    slope = 0.5 * (1.0 + tangent) + 0.5 * pre * (1.0 - tangent * tangent) * gelu_scale * (
        1.0 + 3.0 * cubic_coef * square
    )
    hidden = hidden.astype(bf16).astype(f32)
    d_logit = (info[:, 1:2] + info[:, 2:3]) * jnp.sum(hidden * dh, -1, keepdims=True)
    d_pre = (dh * slope * gate).astype(bf16)
    place = lax.broadcasted_iota(jnp.int32, (rows, lane), 1).astype(f32)
    sign = (place == mine.astype(f32)).astype(f32) - (place == info[:, 3:4]).astype(f32)
    d_logits = sign * d_logit
    back = dot(d_pre, up, ((1,), (1,)))
    back = back + dot(
        in_words(d_logits[:, :experts], 1), jnp.concatenate([router] * 3, 0), ((1,), (0,))
    )
    turned = d_logits.T[:experts]
    part = from_words(dot(in_words(turned, 0), xn, ((1,), (0,))))
    gain = jnp.sum(back * xn.astype(f32), 0, keepdims=True)
    return (hidden * gate).astype(bf16), d_pre, back, jnp.concatenate([part, gain], 0)


def expert_kernel(count, mine_ref, up_ref, down_ref, router_ref, before_ref, *refs):
    ins = refs[: 2 * count]
    h_ref, d_ref, part_ref = refs[2 * count : 2 * count + 3]
    outs = refs[2 * count + 3 :]
    width = up_ref.shape[0]
    cot = jnp.concatenate([ref[...] for ref in ins[count:]], 0)
    h_ref[...], d_ref[...], back, part = expert_rows(
        jnp.concatenate([ref[...] for ref in ins[:count]], 0),
        cot[:, :width],
        cot[:, width:].astype(f32),
        up_ref[...],
        down_ref[...],
        router_ref[...],
        mine_ref[0],
    )
    part_ref[...] = before_ref[...] + part
    step = back.shape[0] // count
    for i in range(count):
        outs[i][...] = back[i * step : (i + 1) * step].astype(bf16)


def run_experts(mine, up, down, router, before, xns, cots):
    total = sum(xn.shape[0] for xn in xns)
    width, hid = up.shape
    found = call(
        functools.partial(expert_kernel, len(xns)),
        [like((total, hid), bf16), like((total, hid), bf16), like(before.shape, f32)]
        + [like(xn.shape, bf16) for xn in xns],
        6 * total * up.size,
        4 * up.size + 8 * total * width,
        in_specs=[scalar()] + [whole()] * (4 + 2 * len(xns)),
    )(mine, up, down, router, before, *xns, *cots)
    return found[0], found[1], found[2], found[3:]


def grads_kernel(xns, cots, hs, *refs):
    xn_refs, cot_refs = refs[:xns], refs[xns : xns + cots]
    h_refs = refs[xns + cots : xns + cots + hs]
    d_refs = refs[xns + cots + hs : xns + cots + 2 * hs]
    up_g_ref, down_g_ref = refs[-2:]

    def joined(group):
        return jnp.concatenate([ref[...] for ref in group], 0)

    up_g_ref[...] = dot(joined(xn_refs), joined(d_refs), ((0,), (0,))).astype(bf16)
    down_g_ref[...] = dot(joined(h_refs), joined(cot_refs), ((0,), (0,))).astype(bf16)


def run_grads(width, hid, xns, cots, hs, ds):
    steps = 6
    specs = [pl.BlockSpec((v.shape[0], width // steps), lambda i: (0, i)) for v in xns]
    specs += [pl.BlockSpec((v.shape[0], width), lambda i: (0, 0)) for v in cots]
    specs += [pl.BlockSpec((v.shape[0], hid // steps), lambda i: (0, i)) for v in hs]
    specs += [pl.BlockSpec((v.shape[0], hid), lambda i: (0, 0)) for v in ds]
    total = sum(v.shape[0] for v in xns)
    return call(
        functools.partial(grads_kernel, len(xns), len(cots), len(hs)),
        [like((width, hid), bf16), like((hid, width), bf16)],
        4 * total * width * hid // cheaper,
        (4 * width * hid + 6 * total * width) // cheaper,
        grid=(steps,),
        in_specs=specs,
        out_specs=[
            pl.BlockSpec((width // steps, hid), lambda i: (i, 0)),
            pl.BlockSpec((hid // steps, width), lambda i: (i, 0)),
        ],
    )(*xns, *cots, *hs, *ds)


def merge_kernel(own_ref, high_ref, low_ref, far_ref, out_ref):
    total = own_ref[...].astype(f32) + far_ref[...].astype(f32)
    out_ref[...] = (total + (high_ref[...].astype(f32) + low_ref[...].astype(f32))).astype(bf16)


def final_kernel(x_ref, gain_ref, cot_ref, slots_ref, back_ref, out_ref):
    x32 = x_ref[...].astype(f32)
    inv = lax.rsqrt(jnp.mean(x32 * x32, -1, keepdims=True) + norm_eps)
    xh = x32 * inv
    dxn = dot(back_ref[...], slots_ref[...], ((1,), (0,)))
    rows = dxn * gain_ref[...]
    out_ref[...] = (
        cot_ref[...].astype(f32) + inv * (rows - xh * jnp.mean(rows * xh, -1, keepdims=True))
    ).astype(bf16)


def shards(
    segment_input,
    upstream_grad,
    step_noise,
    rewards,
    routes,
    up_weight,
    down_weight,
    router_weight,
    norm_gain,
):
    tok_count = segment_input.shape[1]
    width = segment_input.shape[2]
    experts = router_weight.shape[2]
    split = lax.axis_size("x")
    top_count = routes.shape[2]
    capacity = tok_count * top_count // experts
    slots = experts * capacity
    half = slots // 2
    x = segment_input[0]
    up = up_weight[0]
    down = down_weight[0]
    router = router_weight[0].T
    pair = routes[0].T
    n_segment = lax.axis_size("segment")
    is_last = (lax.axis_index("segment") == n_segment - 1).astype(jnp.int32).reshape(1)
    mine = lax.axis_index("e").astype(jnp.int32).reshape(1)

    xn_slots, pick, info, pick_turned = call(
        functools.partial(token_kernel, capacity),
        [
            like((slots, width), bf16),
            like((slots, tok_count), bf16),
            like((slots, lane), bf16),
            like((tok_count, slots), bf16),
        ],
        2 * slots * tok_count * width,
        4 * tok_count * width + 2 * slots * width,
    )(x, norm_gain, router, pair)
    arrived = lax.ppermute(
        after(upstream_grad[0], xn_slots), "segment", [(i + 1, i) for i in range(n_segment - 1)]
    )
    def exchange(rows):
        shaped = rows.reshape(experts, capacity, rows.shape[1])
        return lax.all_to_all(shaped, "e", 0, 0, tiled=True).reshape(rows.shape)

    xn_own = exchange(xn_slots)
    cot, c_slots = call(
        cot_kernel,
        [like((tok_count, width), bf16), like((slots, width + lane), bf16)],
        2 * slots * tok_count * width,
        6 * tok_count * width + 2 * slots * width,
        in_specs=[scalar()] + [whole()] * 5,
    )(is_last, arrived, step_noise, rewards[:, None], pick, info)

    c_own = exchange(c_slots)
    xn_low, xn_high = shift(xn_own, "x", 1), shift(xn_own, "x", -1)
    c_own, xn_low, xn_high = lax.optimization_barrier((c_own, xn_low, xn_high))
    c_low, c_high = shift(c_own, "x", 1), shift(c_own, "x", -1)
    nothing = jnp.zeros((experts + 1, width), f32)
    h_own, d_own, part, (b_own,) = run_experts(
        mine, up, down, router, nothing, [xn_own], [c_own]
    )
    xn_far = shift(after(xn_low, c_low), "x", 1)
    c_far = shift(c_high, "x", -1)
    h_near, d_near, part, (b_low, b_high) = run_experts(
        mine, up, down, router, part, [xn_low, xn_high], [c_low, c_high]
    )
    got_high, got_low = shift(b_low, "x", -1), shift(b_high, "x", 1)
    h_far, d_far, part, (b_far,) = run_experts(
        mine, up, down, router, part, [xn_far], [c_far]
    )
    got_far = shift(b_far, "x", 2)
    back = call(merge_kernel, like(b_own.shape, bf16), 1000, 8 * b_own.size // cheaper)(
        b_own, got_high, got_low, got_far
    )
    back_slots = exchange(back)
    up_g, down_g = run_grads(
        width,
        up.shape[1],
        [xn_own, xn_low, xn_high, xn_far],
        [c_own, c_low, c_high, c_far],
        [h_own, h_near, h_far],
        [d_own, d_near, d_far],
    )
    small = total_over(part)
    router_total = small[:experts]
    gain_total = small[experts] / norm_gain[0]

    input_g = call(
        final_kernel,
        like((tok_count, width), bf16),
        2 * slots * tok_count * width,
        8 * tok_count * width + 2 * slots * width,
    )(x, norm_gain, cot, back_slots, pick_turned)
    return (
        input_g[None],
        up_g[None],
        down_g[None],
        router_total.T[None],
        gain_total[None],
    )


def solution(mesh):
    experts = 8
    n_segment, n_dp = mesh.devices.shape
    grid = Mesh(
        mesh.devices.reshape(n_segment, experts, n_dp // experts), ("segment", "e", "x")
    )
    dp = ("e", "x")
    return jax.shard_map(
        shards,
        mesh=grid,
        in_specs=(
            P("segment", dp, None),
            P("segment", dp, None),
            P(dp, None),
            P(dp),
            P("segment", dp, None),
            P("segment", None, dp),
            P("segment", dp, None),
            P("segment", None, None),
            P("segment", None),
        ),
        out_specs=(
            P("segment", dp, None),
            P("segment", None, dp),
            P("segment", dp, None),
            P("segment", None, None),
            P("segment", None),
        ),
        check_vma=False,
    )
```

time: 181 us -> 167 us (0.923)
  local copies, waits for them, and re-layouts: 16.5 us -> 6.75 us
  starting transfers between devices: 56.2 us -> 49.5 us
  waiting for transfers between devices: 58.2 us -> 63.5 us
  other arithmetic: 5.41 us -> 1.56 us
    all_to_all x1 -> x0, starting transfers between devices: 9.98 us -> none  [shards(): lax.all_to_all(dg.reshape(experts * split, capacity), ('e', 'x'), 0, 0, t...]
    slice x6 -> x0, local copies, waits for them, and re-layouts: 8.62 us -> none  [the longest x1 1.94 us: shards(): via_low = shift(b_far[:half], 'x', -1)]
    all_to_all x1 -> x0, waiting for transfers between devices: 8.16 us -> none  [shards(): lax.all_to_all(dg.reshape(experts * split, capacity), ('e', 'x'), 0, 0, t...]
    ppermute x14 -> x9, starting transfers between devices: 20.4 us -> 12.7 us  [shift(): lax.ppermute(value, axis, [(i, (i + steps) % count) for i in range(count)])]
    all_to_all x3, starting transfers between devices: 14.7 us -> 20.7 us  [exchange(): return lax.all_to_all(shaped, 'e', 0, 0, tiled=True).reshape(rows.shape)]
    ppermute x7, starting transfers between devices: 9.23 us -> 14.2 us  [swap(): return lax.ppermute(value, axis, [(i, i ^ mask) for i in range(count)])]
    ppermute x14 -> x9, waiting for transfers between devices: 33 us -> 37.5 us  [shift(): lax.ppermute(value, axis, [(i, (i + steps) % count) for i in range(count)])]
    ppermute x1, waiting for transfers between devices: 0.01 us -> 4.24 us  [shards(): lax.ppermute(after(upstream_grad[0], xn_slots), 'segment', [(i + 1, i) fo...]
  transfers between devices with their start and end apart: 26 -> 20, of which waited for: 10 -> 14; matrix products, arithmetic and copies ran while one was open for 9% -> 3% of each run, Pallas kernels for 19% -> 23%
where the time goes in v3:
time: 167 us; the launch traced here: 166 us
  waiting for transfers between devices  63.5 us (38%)
  starting transfers between devices  49.5 us (30%)
  Pallas kernels  43.7 us (26%)
  local copies, waits for them, and re-layouts  6.75 us (4%)
    ppermute x9, waiting for transfers between devices, shift(): lax.ppermute(value, axis, [(i, (i + steps) % count) for i in range(count)])  37.5 us
    pallas_call x3, Pallas kernels, run_experts(): call(functools.partial(expert_kernel, len(xns)), [like((total, hid), bf16...  22.5 us
    all_to_all x3, starting transfers between devices, exchange(): return lax.all_to_all(shaped, 'e', 0, 0, tiled=True).reshape(rows.shape)  20.7 us
    all_to_all x3, waiting for transfers between devices, exchange(): return lax.all_to_all(shaped, 'e', 0, 0, tiled=True).reshape(rows.shape)  15.8 us
    ppermute x7, starting transfers between devices, swap(): return lax.ppermute(value, axis, [(i, i ^ mask) for i in range(count)])  14.2 us
    ppermute x9, starting transfers between devices, shift(): lax.ppermute(value, axis, [(i, (i + steps) % count) for i in range(count)])  12.7 us
    pallas_call x1, Pallas kernels, run_grads(): call(functools.partial(grads_kernel, len(xns), len(cots), len(hs)), [like...  10.3 us
    ppermute x7, waiting for transfers between devices, swap(): return lax.ppermute(value, axis, [(i, i ^ mask) for i in range(count)])  5.93 us
  transfers between devices with their start and end apart: 20, of which 14 were waited for; matrix products, arithmetic and copies ran while one was open for 3% of the time, Pallas kernels for 23%

profile of v3, /device:TPU:64, one launch (start us, length us, event | category | flops | bytes accessed | tf_op | source)
XLA Modules:
  0.0 165.7 jit_solution(13040839422974940326)
XLA Ops:
  0.6 2.5 %shard_map.128 = (bf16[256,1536]{1,0:T(8,128)(2,1)}, bf16[256,128]{1,0:T(8,128)(2,1)}, bf16[256,128]{1,0:T(8,128)(2,1)}, bf16[128,256]{1,0:T(8,128)(2,1)}) custom-call(bf16[128,1536]{1,0:T(8,128)(2,1)} %bitcast.36, f32[1,1536]{1,0:T(1,128)} %gain_ref.3, bf16[8,1536]{1,0:T(8,128)(2,1)} %bitcast.41, s32[2,128]{1,0:T(2,128)} %bitcast.45), custom_call_target="tpu_custom_call" | custom-call | flops 100663296 | bytes 1572864 | tf_op jit(solution)/shard_map/pallas_call | solution.py:294
  3.1 5.8 %all-to-all-start = ((bf16[8,32,1536]{2,1,0:T(8,128)(2,1)}), bf16[8,32,1536]{2,1,0:T(8,128)(2,1)S(1)}, u32[]{:S(2)}, u32[]{:S(2)}) async-start(bf16[8,32,1536]{2,1,0:T(8,128)(2,1)} %bitcast.39), calls=%async_computation | async-start | bytes 1572864 | tf_op jit(solution)/shard_map/all_to_all | solution.py:310
  9.0 1.9 %collective-permute-start = (bf16[128,1536]{1,0:T(8,128)(2,1)}, bf16[128,1536]{1,0:T(8,128)(2,1)S(1)}, u32[]{:S(2)}, u32[]{:S(2)}) collective-permute-start(bf16[128,1536]{1,0:T(8,128)(2,1)} %bitcast.55), channel_id=1, source_target_pairs={{32,0},{64,32},{96,64},{128,96},{160,128},{192,160},{224,192},{33,... | collective-permute-start | bytes 1179656 | tf_op jit(solution)/shard_map/ppermute | solution.py:305
  10.9 1.4 copy.14.rewards_ref
  12.3 4.2 %collective-permute-done.arrived_ref = bf16[128,1536]{1,0:T(8,128)(2,1)S(1)} collective-permute-done((bf16[128,1536]{1,0:T(8,128)(2,1)}, bf16[128,1536]{1,0:T(8,128)(2,1)S(1)}, u32[]{:S(2)}, u32[]{:S(2)}) %collective-permute-start) | collective-permute-done | bytes 393248 | tf_op jit(solution)/shard_map/ppermute | solution.py:305
  16.5 0.7 copy-done.10
  17.3 2.5 %shard_map.129 = (bf16[128,1536]{1,0:T(8,128)(2,1)}, bf16[256,1664]{1,0:T(8,128)(2,1)}) custom-call(s32[1]{0:T(128)} %bitcast.1.last_ref, bf16[128,1536]{1,0:T(8,128)(2,1)} %copy-done.10, bf16[128,1536]{1,0:T(8,128)(2,1)} %noise_ref.1, f32[128,1]{1,0:T(8,128)} %copy.14.rewards_ref, bf16[256,128]{1,0:T(8,128)(2,1)} %get-tuple-element.33.pick_ref, ...), custom_call_target="tpu_custom_call" | custom-call | flops 100663296 | bytes 1966080 | tf_op jit(solution)/shard_map/pallas_call | solution.py:313
  19.8 6.3 %all-to-all-done = bf16[8,32,1536]{2,1,0:T(8,128)(2,1)S(1)} async-done(((bf16[8,32,1536]{2,1,0:T(8,128)(2,1)}), bf16[8,32,1536]{2,1,0:T(8,128)(2,1)S(1)}, u32[]{:S(2)}, u32[]{:S(2)}) %all-to-all-start) | async-done | bytes 786464 | tf_op jit(solution)/shard_map/all_to_all | solution.py:310
  26.1 8.7 %all-to-all-start.1 = ((bf16[8,32,1664]{2,1,0:T(8,128)(2,1)}), bf16[8,32,1664]{2,1,0:T(8,128)(2,1)S(1)}, u32[]{:S(2)}, u32[]{:S(2)}) async-start(bf16[8,32,1664]{2,1,0:T(8,128)(2,1)} %bitcast.38), calls=%async_computation.1 | async-start | bytes 1703936 | tf_op jit(solution)/shard_map/all_to_all | solution.py:310
  34.8 1.5 collective-permute-start.1
  36.3 1.7 %collective-permute-start.2 = (bf16[256,1536]{1,0:T(8,128)(2,1)S(1)}, bf16[256,1536]{1,0:T(8,128)(2,1)S(1)}, u32[]{:S(2)}, u32[]{:S(2)}) collective-permute-start(bf16[256,1536]{1,0:T(8,128)(2,1)S(1)} %bitcast.31), channel_id=1, source_target_pairs={{0,3},{1,0},{2,1},{3,2},{4,7},{5,4},{6,5},{7,6},{8,11},{9,8},{10,9... | collective-permute-start | bytes 2359304 | tf_op jit(solution)/shard_map/ppermute | solution.py:22
  38.0 9.5 %all-to-all-done.1 = bf16[8,32,1664]{2,1,0:T(8,128)(2,1)S(1)} async-done(((bf16[8,32,1664]{2,1,0:T(8,128)(2,1)}), bf16[8,32,1664]{2,1,0:T(8,128)(2,1)S(1)}, u32[]{:S(2)}, u32[]{:S(2)}) %all-to-all-start.1) | async-done | bytes 852000 | tf_op jit(solution)/shard_map/all_to_all | solution.py:310
  47.5 6.3 %collective-permute-done.1.refs_0_.refs_1_ = bf16[256,1536]{1,0:T(8,128)(2,1)S(1)} collective-permute-done((bf16[256,1536]{1,0:T(8,128)(2,1)S(1)}, bf16[256,1536]{1,0:T(8,128)(2,1)S(1)}, u32[]{:S(2)}, u32[]{:S(2)}) %collective-permute-start.1) | collective-permute-done | bytes 786464 | tf_op jit(solution)/shard_map/ppermute | solution.py:22
  53.8 0.6 collective-permute-done.2.refs_1_.refs_2_
  54.4 0.4 copy-done.5
  54.8 0.9 copy-done.6
  55.7 2.6 %collective-permute-start.4 = (bf16[256,1664]{1,0:T(8,128)(2,1)S(1)}, bf16[256,1664]{1,0:T(8,128)(2,1)S(1)}, u32[]{:S(2)}, u32[]{:S(2)}) collective-permute-start(bf16[256,1664]{1,0:T(8,128)(2,1)S(1)} %bitcast.26), channel_id=1, source_target_pairs={{0,3},{1,0},{2,1},{3,2},{4,7},{5,4},{6,5},{7,6},{8,11},{9,8},{10,9... | collective-permute-start | bytes 2555912 | tf_op jit(solution)/shard_map/ppermute | solution.py:22
  58.2 0.0 collective-permute-start.3
  58.3 18.2 %collective-permute-done.4.refs_3_.refs_6_ = bf16[256,1664]{1,0:T(8,128)(2,1)S(1)} collective-permute-done((bf16[256,1664]{1,0:T(8,128)(2,1)S(1)}, bf16[256,1664]{1,0:T(8,128)(2,1)S(1)}, u32[]{:S(2)}, u32[]{:S(2)}) %collective-permute-start.4) | collective-permute-done | bytes 852000 | tf_op jit(solution)/shard_map/ppermute | solution.py:22
  76.4 3.7 %collective-permute-start.8 = (bf16[256,1664]{1,0:T(8,128)(2,1)S(1)}, bf16[256,1664]{1,0:T(8,128)(2,1)}, u32[]{:S(2)}, u32[]{:S(2)}) collective-permute-start(bf16[256,1664]{1,0:T(8,128)(2,1)S(1)} %collective-permute-done.4.refs_3_.refs_6_), channel_id=1, source_target_pairs={{0,3},{1,0},{2,1},{3,2},{4,7},{5,4},{6,5},{7,6},{8,11},{9,8},{10,9... | collective-permute-start | bytes 2555912 | tf_op jit(solution)/shard_map/ppermute | solution.py:22
  80.1 0.3 collective-permute-done.3.refs_2_.refs_5_
  80.4 0.0 collective-permute-start.7
  80.4 0.7 broadcast_in_dim.20.before_ref
  81.1 0.0 copy-done.1
  81.1 0.0 copy-done
  81.1 6.5 %shard_map.130 = (bf16[256,768]{1,0:T(8,128)(2,1)}, bf16[256,768]{1,0:T(8,128)(2,1)}, f32[9,1536]{1,0:T(8,128)}, bf16[256,1536]{1,0:T(8,128)(2,1)}) custom-call(s32[1]{0:T(128)} %bitcast.8.mine_ref, bf16[1536,768]{1,0:T(8,128)(2,1)} %bitcast.47, bf16[768,1536]{1,0:T(8,128)(2,1)} %bitcast.50, bf16[8,1536]{1,0:T(8,128)(2,1)} %bitcast.42, ...), custom_call_target="tpu_custom_call" | custom-call | flops 1811939328 | bytes 7864320 | tf_op jit(solution)/shard_map/pallas_call | solution.py:205
  87.6 0.0 copy-done.3
  87.6 0.0 copy-done.4
  87.6 9.5 %shard_map.131 = (bf16[512,768]{1,0:T(8,128)(2,1)}, bf16[512,768]{1,0:T(8,128)(2,1)}, f32[9,1536]{1,0:T(8,128)}, bf16[256,1536]{1,0:T(8,128)(2,1)}, bf16[256,1536]{1,0:T(8,128)(2,1)}) custom-call(s32[1]{0:T(128)} %bitcast.8.mine_ref, bf16[1536,768]{1,0:T(8,128)(2,1)} %bitcast.48, bf16[768,1536]{1,0:T(8,128)(2,1)} %bitcast.51, bf16[8,1536]{1,0:T(8,128)(2,1)} %bitcast.43, ...), custom_call_target="tpu_custom_call" | custom-call | flops 3623878656 | bytes 11010048 | tf_op jit(solution)/shard_map/pallas_call | solution.py:205
  97.1 3.2 %collective-permute-start.5 = (bf16[256,1536]{1,0:T(8,128)(2,1)}, bf16[256,1536]{1,0:T(8,128)(2,1)S(1)}, u32[]{:S(2)}, u32[]{:S(2)}) collective-permute-start(bf16[256,1536]{1,0:T(8,128)(2,1)} %get-tuple-element.42), channel_id=1, source_target_pairs={{0,3},{1,0},{2,1},{3,2},{4,7},{5,4},{6,5},{7,6},{8,11},{9,8},{10,9... | collective-permute-start | bytes 2359304 | tf_op jit(solution)/shard_map/ppermute | solution.py:22
  100.3 0.0 collective-permute-start.6
  100.3 1.7 %collective-permute-done.7.refs_0_.refs_3_ = bf16[256,1536]{1,0:T(8,128)(2,1)} collective-permute-done((bf16[256,1536]{1,0:T(8,128)(2,1)}, bf16[256,1536]{1,0:T(8,128)(2,1)}, u32[]{:S(2)}, u32[]{:S(2)}) %collective-permute-start.7) | collective-permute-done | bytes 786464 | tf_op jit(solution)/shard_map/ppermute | solution.py:22
  102.1 0.0 collective-permute-done.8.refs_1_.refs_7_
  102.1 6.5 %shard_map.132 = (bf16[256,768]{1,0:T(8,128)(2,1)}, bf16[256,768]{1,0:T(8,128)(2,1)}, f32[9,1536]{1,0:T(8,128)}, bf16[256,1536]{1,0:T(8,128)(2,1)}) custom-call(s32[1]{0:T(128)} %bitcast.8.mine_ref, bf16[1536,768]{1,0:T(8,128)(2,1)} %bitcast.49, bf16[768,1536]{1,0:T(8,128)(2,1)} %bitcast.52, bf16[8,1536]{1,0:T(8,128)(2,1)} %bitcast.44, ...), custom_call_target="tpu_custom_call" | custom-call | flops 1811939328 | bytes 7864320 | tf_op jit(solution)/shard_map/pallas_call | solution.py:205
  108.6 0.0 collective-permute-start.9
  108.6 2.3 %collective-permute-start.10 = (f32[9,1536]{1,0:T(8,128)}, f32[9,1536]{1,0:T(8,128)S(1)}, u32[]{:S(2)}, u32[]{:S(2)}) collective-permute-start(f32[9,1536]{1,0:T(8,128)} %get-tuple-element.56), channel_id=1, source_target_pairs={{0,4},{4,0},{8,12},{12,8},{16,20},{20,16},{24,28},{28,24},{1,5},{5... | collective-permute-start | bytes 165896 | tf_op jit(solution)/shard_map/ppermute | solution.py:27
  110.9 2.8 %collective-permute-done.10 = f32[9,1536]{1,0:T(8,128)S(1)} collective-permute-done((f32[9,1536]{1,0:T(8,128)}, f32[9,1536]{1,0:T(8,128)S(1)}, u32[]{:S(2)}, u32[]{:S(2)}) %collective-permute-start.10) | collective-permute-done | bytes 55328 | tf_op jit(solution)/shard_map/ppermute | solution.py:27
  113.7 0.9 add.21
  114.6 2.1 %collective-permute-start.12 = (f32[9,1536]{1,0:T(8,128)S(1)}, f32[9,1536]{1,0:T(8,128)S(1)}, u32[]{:S(2)}, u32[]{:S(2)}) collective-permute-start(f32[9,1536]{1,0:T(8,128)S(1)} %add.21), channel_id=1, source_target_pairs={{0,8},{4,12},{8,0},{12,4},{16,24},{20,28},{24,16},{28,20},{1,9},{5... | collective-permute-start | bytes 165896 | tf_op jit(solution)/shard_map/ppermute | solution.py:27
  116.7 2.1 %collective-permute-start.13 = (f32[9,1536]{1,0:T(8,128)S(1)}, f32[9,1536]{1,0:T(8,128)S(1)}, u32[]{:S(2)}, u32[]{:S(2)}) collective-permute-start(f32[9,1536]{1,0:T(8,128)S(1)} %add.21), channel_id=1, source_target_pairs={{0,24},{4,28},{8,16},{12,20},{16,8},{20,12},{24,0},{28,4},{1,25},{... | collective-permute-start | bytes 165896 | tf_op jit(solution)/shard_map/ppermute | solution.py:27
  118.8 0.5 collective-permute-done.12
  119.3 3.5 %collective-permute-start.11 = (f32[9,1536]{1,0:T(8,128)S(1)}, f32[9,1536]{1,0:T(8,128)S(1)}, u32[]{:S(2)}, u32[]{:S(2)}) collective-permute-start(f32[9,1536]{1,0:T(8,128)S(1)} %add.21), channel_id=1, source_target_pairs={{0,16},{4,20},{8,24},{12,28},{16,0},{20,4},{24,8},{28,12},{1,17},{... | collective-permute-start | bytes 165896 | tf_op jit(solution)/shard_map/ppermute | solution.py:27
  122.9 0.8 collective-permute-done.13
  123.6 1.8 %collective-permute-done.11 = f32[9,1536]{1,0:T(8,128)S(1)} collective-permute-done((f32[9,1536]{1,0:T(8,128)S(1)}, f32[9,1536]{1,0:T(8,128)S(1)}, u32[]{:S(2)}, u32[]{:S(2)}) %collective-permute-start.11) | collective-permute-done | bytes 55328 | tf_op jit(solution)/shard_map/ppermute | solution.py:27
  125.5 2.7 %collective-permute-start.15 = (f32[9,1536]{1,0:T(8,128)S(1)}, f32[9,1536]{1,0:T(8,128)S(1)}, u32[]{:S(2)}, u32[]{:S(2)}) collective-permute-start(f32[9,1536]{1,0:T(8,128)S(1)} %add_add_fusion.1), channel_id=1, source_target_pairs={{0,1},{1,0},{2,3},{3,2},{4,5},{5,4},{6,7},{7,6},{8,9},{9,8},{10,11... | collective-permute-start | bytes 165896 | tf_op jit(solution)/shard_map/ppermute | solution.py:27
  128.2 1.4 collective-permute-start.16
  129.6 5.8 %collective-permute-done.5.high_ref = bf16[256,1536]{1,0:T(8,128)(2,1)S(1)} collective-permute-done((bf16[256,1536]{1,0:T(8,128)(2,1)}, bf16[256,1536]{1,0:T(8,128)(2,1)S(1)}, u32[]{:S(2)}, u32[]{:S(2)}) %collective-permute-start.5) | collective-permute-done | bytes 786464 | tf_op jit(solution)/shard_map/ppermute | solution.py:22
  135.4 0.0 collective-permute-start.14
  135.4 4.7 %collective-permute-done.6.low_ref = bf16[256,1536]{1,0:T(8,128)(2,1)S(1)} collective-permute-done((bf16[256,1536]{1,0:T(8,128)(2,1)}, bf16[256,1536]{1,0:T(8,128)(2,1)S(1)}, u32[]{:S(2)}, u32[]{:S(2)}) %collective-permute-start.6) | collective-permute-done | bytes 786464 | tf_op jit(solution)/shard_map/ppermute | solution.py:22
  140.1 0.0 collective-permute-done.9.far_ref
  140.1 0.0 copy-done.7
  140.1 0.9 copy-done.8
  141.0 0.2 copy-done.9
  141.2 3.2 %shard_map.133 = bf16[256,1536]{1,0:T(8,128)(2,1)} custom-call(bf16[256,1536]{1,0:T(8,128)(2,1)} %get-tuple-element.38.own_ref, bf16[256,1536]{1,0:T(8,128)(2,1)} %copy-done.7, bf16[256,1536]{1,0:T(8,128)(2,1)} %copy-done.8, bf16[256,1536]{1,0:T(8,128)(2,1)} %copy-done.9), custom_call_target="tpu_custom_call" | custom-call | flops 1000 | bytes 31457 | tf_op jit(solution)/shard_map/pallas_call | solution.py:339
  144.4 6.2 %all-to-all-start.2 = ((bf16[8,32,1536]{2,1,0:T(8,128)(2,1)}), bf16[8,32,1536]{2,1,0:T(8,128)(2,1)S(1)}, u32[]{:S(2)}, u32[]{:S(2)}) async-start(bf16[8,32,1536]{2,1,0:T(8,128)(2,1)} %bitcast.35), calls=%async_computation.2 | async-start | bytes 1572864 | tf_op jit(solution)/shard_map/all_to_all | solution.py:310
  150.6 10.3 %shard_map.135 = (bf16[1536,768]{1,0:T(8,128)(2,1)}, bf16[768,1536]{1,0:T(8,128)(2,1)}) custom-call(bf16[256,1536]{1,0:T(8,128)(2,1)} %bitcast.33, bf16[256,1536]{1,0:T(8,128)(2,1)} %copy-done.5, bf16[256,1536]{1,0:T(8,128)(2,1)} %copy-done.6, bf16[256,1536]{1,0:T(8,128)(2,1)} %collective-permute-done.7.refs_0_.refs_3_, bf16[256,1664]{1,0:T(8,128)(2,1)} %bitcast.29, ...), custom_call_target="tpu_custom_call" | custom-call | flops 48318384 | bytes 141557 | tf_op jit(solution)/shard_map/pallas_call | solution.py:236
  160.9 0.0 collective-permute-done.15
  160.9 0.0 collective-permute-done.16
  160.9 0.0 collective-permute-done.14
  161.0 0.6 slice_divide_fusion
  161.6 0.6 slice_bitcast_fusion
  162.2 0.0 all-to-all-done.2
  162.2 0.9 copy-done.2
  163.1 2.6 %shard_map.134 = bf16[128,1536]{1,0:T(8,128)(2,1)} custom-call(bf16[128,1536]{1,0:T(8,128)(2,1)} %bitcast.37, f32[1,1536]{1,0:T(1,128)} %gain_ref.3, bf16[128,1536]{1,0:T(8,128)(2,1)} %get-tuple-element.35.cot_ref, bf16[256,1536]{1,0:T(8,128)(2,1)} %bitcast.34, bf16[128,256]{1,0:T(8,128)(2,1)} %get-tuple-element.47.back_ref), custom_call_target="tpu_custom_call" | custom-call | flops 100663296 | bytes 2359296 | tf_op jit(solution)/shard_map/pallas_call | solution.py:355
  (15 shorter events, 0.1 us)
Async XLA Ops:
  3.1 22.9 %all-to-all-start = ((bf16[8,32,1536]{2,1,0:T(8,128)(2,1)}), bf16[8,32,1536]{2,1,0:T(8,128)(2,1)S(1)}, u32[]{:S(2)}, u32[]{:S(2)}) async-start(bf16[8,32,1536]{2,1,0:T(8,128)(2,1)} %bitcast.39), calls=%async_computation | async-start | bytes 1572864 | tf_op jit(solution)/shard_map/all_to_all | solution.py:310
  9.0 7.6 %collective-permute-start = (bf16[128,1536]{1,0:T(8,128)(2,1)}, bf16[128,1536]{1,0:T(8,128)(2,1)S(1)}, u32[]{:S(2)}, u32[]{:S(2)}) collective-permute-start(bf16[128,1536]{1,0:T(8,128)(2,1)} %bitcast.55), channel_id=1, source_target_pairs={{32,0},{64,32},{96,64},{128,96},{160,128},{192,160},{224,192},{33,... | collective-permute-start | bytes 1179656 | tf_op jit(solution)/shard_map/ppermute | solution.py:305
  16.5 0.7 copy-start.10
  26.1 55.1 %copy-start.1 = (bf16[8,32,1536]{2,1,0:T(8,128)(2,1)}, bf16[8,32,1536]{2,1,0:T(8,128)(2,1)S(1)}, u32[]{:S(2)}) copy-start(bf16[8,32,1536]{2,1,0:T(8,128)(2,1)S(1)} %all-to-all-done) | copy-start | bytes 2359300
  26.1 21.4 %all-to-all-start.1 = ((bf16[8,32,1664]{2,1,0:T(8,128)(2,1)}), bf16[8,32,1664]{2,1,0:T(8,128)(2,1)S(1)}, u32[]{:S(2)}, u32[]{:S(2)}) async-start(bf16[8,32,1664]{2,1,0:T(8,128)(2,1)} %bitcast.38), calls=%async_computation.1 | async-start | bytes 1703936 | tf_op jit(solution)/shard_map/all_to_all | solution.py:310
  34.8 19.1 %collective-permute-start.1 = (bf16[256,1536]{1,0:T(8,128)(2,1)S(1)}, bf16[256,1536]{1,0:T(8,128)(2,1)S(1)}, u32[]{:S(2)}, u32[]{:S(2)}) collective-permute-start(bf16[256,1536]{1,0:T(8,128)(2,1)S(1)} %bitcast.30), channel_id=1, source_target_pairs={{0,1},{1,2},{2,3},{3,0},{4,5},{5,6},{6,7},{7,4},{8,9},{9,10},{10,1... | collective-permute-start | bytes 2359304 | tf_op jit(solution)/shard_map/ppermute | solution.py:22
  36.3 18.1 %collective-permute-start.2 = (bf16[256,1536]{1,0:T(8,128)(2,1)S(1)}, bf16[256,1536]{1,0:T(8,128)(2,1)S(1)}, u32[]{:S(2)}, u32[]{:S(2)}) collective-permute-start(bf16[256,1536]{1,0:T(8,128)(2,1)S(1)} %bitcast.31), channel_id=1, source_target_pairs={{0,3},{1,0},{2,1},{3,2},{4,7},{5,4},{6,5},{7,6},{8,11},{9,8},{10,9... | collective-permute-start | bytes 2359304 | tf_op jit(solution)/shard_map/ppermute | solution.py:22
  47.5 33.6 %copy-start = (bf16[8,32,1664]{2,1,0:T(8,128)(2,1)}, bf16[8,32,1664]{2,1,0:T(8,128)(2,1)S(1)}, u32[]{:S(2)}) copy-start(bf16[8,32,1664]{2,1,0:T(8,128)(2,1)S(1)} %all-to-all-done.1) | copy-start | bytes 2555908
  53.8 0.9 copy-start.5
  54.8 0.9 copy-start.6
  55.7 20.8 %collective-permute-start.4 = (bf16[256,1664]{1,0:T(8,128)(2,1)S(1)}, bf16[256,1664]{1,0:T(8,128)(2,1)S(1)}, u32[]{:S(2)}, u32[]{:S(2)}) collective-permute-start(bf16[256,1664]{1,0:T(8,128)(2,1)S(1)} %bitcast.26), channel_id=1, source_target_pairs={{0,3},{1,0},{2,1},{3,2},{4,7},{5,4},{6,5},{7,6},{8,11},{9,8},{10,9... | collective-permute-start | bytes 2555912 | tf_op jit(solution)/shard_map/ppermute | solution.py:22
  58.2 22.2 %collective-permute-start.3 = (bf16[256,1664]{1,0:T(8,128)(2,1)S(1)}, bf16[256,1664]{1,0:T(8,128)(2,1)S(1)}, u32[]{:S(2)}, u32[]{:S(2)}) collective-permute-start(bf16[256,1664]{1,0:T(8,128)(2,1)S(1)} %bitcast.27), channel_id=1, source_target_pairs={{0,1},{1,2},{2,3},{3,0},{4,5},{5,6},{6,7},{7,4},{8,9},{9,10},{10,1... | collective-permute-start | bytes 2555912 | tf_op jit(solution)/shard_map/ppermute | solution.py:22
  76.4 11.2 %copy-start.3 = (bf16[256,1664]{1,0:T(8,128)(2,1)}, bf16[256,1664]{1,0:T(8,128)(2,1)S(1)}, u32[]{:S(2)}) copy-start(bf16[256,1664]{1,0:T(8,128)(2,1)S(1)} %collective-permute-done.4.refs_3_.refs_6_) | copy-start | bytes 2555908
  76.4 25.7 %collective-permute-start.8 = (bf16[256,1664]{1,0:T(8,128)(2,1)S(1)}, bf16[256,1664]{1,0:T(8,128)(2,1)}, u32[]{:S(2)}, u32[]{:S(2)}) collective-permute-start(bf16[256,1664]{1,0:T(8,128)(2,1)S(1)} %collective-permute-done.4.refs_3_.refs_6_), channel_id=1, source_target_pairs={{0,3},{1,0},{2,1},{3,2},{4,7},{5,4},{6,5},{7,6},{8,11},{9,8},{10,9... | collective-permute-start | bytes 2555912 | tf_op jit(solution)/shard_map/ppermute | solution.py:22
  80.4 7.2 %copy-start.4 = (bf16[256,1664]{1,0:T(8,128)(2,1)}, bf16[256,1664]{1,0:T(8,128)(2,1)S(1)}, u32[]{:S(2)}) copy-start(bf16[256,1664]{1,0:T(8,128)(2,1)S(1)} %collective-permute-done.3.refs_2_.refs_5_) | copy-start | bytes 2555908
  80.4 21.6 %collective-permute-start.7 = (bf16[256,1536]{1,0:T(8,128)(2,1)}, bf16[256,1536]{1,0:T(8,128)(2,1)}, u32[]{:S(2)}, u32[]{:S(2)}) collective-permute-start(bf16[256,1536]{1,0:T(8,128)(2,1)} %copy-done.5), channel_id=1, source_target_pairs={{0,1},{1,2},{2,3},{3,0},{4,5},{5,6},{6,7},{7,4},{8,9},{9,10},{10,1... | collective-permute-start | bytes 2359304 | tf_op jit(solution)/shard_map/ppermute | solution.py:22
  97.1 38.2 %collective-permute-start.5 = (bf16[256,1536]{1,0:T(8,128)(2,1)}, bf16[256,1536]{1,0:T(8,128)(2,1)S(1)}, u32[]{:S(2)}, u32[]{:S(2)}) collective-permute-start(bf16[256,1536]{1,0:T(8,128)(2,1)} %get-tuple-element.42), channel_id=1, source_target_pairs={{0,3},{1,0},{2,1},{3,2},{4,7},{5,4},{6,5},{7,6},{8,11},{9,8},{10,9... | collective-permute-start | bytes 2359304 | tf_op jit(solution)/shard_map/ppermute | solution.py:22
  100.3 39.7 %collective-permute-start.6 = (bf16[256,1536]{1,0:T(8,128)(2,1)}, bf16[256,1536]{1,0:T(8,128)(2,1)S(1)}, u32[]{:S(2)}, u32[]{:S(2)}) collective-permute-start(bf16[256,1536]{1,0:T(8,128)(2,1)} %get-tuple-element.43), channel_id=1, source_target_pairs={{0,1},{1,2},{2,3},{3,0},{4,5},{5,6},{6,7},{7,4},{8,9},{9,10},{10,1... | collective-permute-start | bytes 2359304 | tf_op jit(solution)/shard_map/ppermute | solution.py:22
  108.6 31.5 %collective-permute-start.9 = (bf16[256,1536]{1,0:T(8,128)(2,1)}, bf16[256,1536]{1,0:T(8,128)(2,1)S(1)}, u32[]{:S(2)}, u32[]{:S(2)}) collective-permute-start(bf16[256,1536]{1,0:T(8,128)(2,1)} %get-tuple-element.46), channel_id=1, source_target_pairs={{0,2},{1,3},{2,0},{3,1},{4,6},{5,7},{6,4},{7,5},{8,10},{9,11},{10,... | collective-permute-start | bytes 2359304 | tf_op jit(solution)/shard_map/ppermute | solution.py:22
  108.6 5.2 %collective-permute-start.10 = (f32[9,1536]{1,0:T(8,128)}, f32[9,1536]{1,0:T(8,128)S(1)}, u32[]{:S(2)}, u32[]{:S(2)}) collective-permute-start(f32[9,1536]{1,0:T(8,128)} %get-tuple-element.56), channel_id=1, source_target_pairs={{0,4},{4,0},{8,12},{12,8},{16,20},{20,16},{24,28},{28,24},{1,5},{5... | collective-permute-start | bytes 165896 | tf_op jit(solution)/shard_map/ppermute | solution.py:27
  114.6 4.7 %collective-permute-start.12 = (f32[9,1536]{1,0:T(8,128)S(1)}, f32[9,1536]{1,0:T(8,128)S(1)}, u32[]{:S(2)}, u32[]{:S(2)}) collective-permute-start(f32[9,1536]{1,0:T(8,128)S(1)} %add.21), channel_id=1, source_target_pairs={{0,8},{4,12},{8,0},{12,4},{16,24},{20,28},{24,16},{28,20},{1,9},{5... | collective-permute-start | bytes 165896 | tf_op jit(solution)/shard_map/ppermute | solution.py:27
  116.7 6.9 %collective-permute-start.13 = (f32[9,1536]{1,0:T(8,128)S(1)}, f32[9,1536]{1,0:T(8,128)S(1)}, u32[]{:S(2)}, u32[]{:S(2)}) collective-permute-start(f32[9,1536]{1,0:T(8,128)S(1)} %add.21), channel_id=1, source_target_pairs={{0,24},{4,28},{8,16},{12,20},{16,8},{20,12},{24,0},{28,4},{1,25},{... | collective-permute-start | bytes 165896 | tf_op jit(solution)/shard_map/ppermute | solution.py:27
  119.3 6.1 %collective-permute-start.11 = (f32[9,1536]{1,0:T(8,128)S(1)}, f32[9,1536]{1,0:T(8,128)S(1)}, u32[]{:S(2)}, u32[]{:S(2)}) collective-permute-start(f32[9,1536]{1,0:T(8,128)S(1)} %add.21), channel_id=1, source_target_pairs={{0,16},{4,20},{8,24},{12,28},{16,0},{20,4},{24,8},{28,12},{1,17},{... | collective-permute-start | bytes 165896 | tf_op jit(solution)/shard_map/ppermute | solution.py:27
  125.5 35.4 %collective-permute-start.15 = (f32[9,1536]{1,0:T(8,128)S(1)}, f32[9,1536]{1,0:T(8,128)S(1)}, u32[]{:S(2)}, u32[]{:S(2)}) collective-permute-start(f32[9,1536]{1,0:T(8,128)S(1)} %add_add_fusion.1), channel_id=1, source_target_pairs={{0,1},{1,0},{2,3},{3,2},{4,5},{5,4},{6,7},{7,6},{8,9},{9,8},{10,11... | collective-permute-start | bytes 165896 | tf_op jit(solution)/shard_map/ppermute | solution.py:27
  128.2 32.8 %collective-permute-start.16 = (f32[9,1536]{1,0:T(8,128)S(1)}, f32[9,1536]{1,0:T(8,128)S(1)}, u32[]{:S(2)}, u32[]{:S(2)}) collective-permute-start(f32[9,1536]{1,0:T(8,128)S(1)} %add_add_fusion.1), channel_id=1, source_target_pairs={{0,3},{1,2},{2,1},{3,0},{4,7},{5,6},{6,5},{7,4},{8,11},{9,10},{10,... | collective-permute-start | bytes 165896 | tf_op jit(solution)/shard_map/ppermute | solution.py:27
  135.4 4.7 %copy-start.7 = (bf16[256,1536]{1,0:T(8,128)(2,1)}, bf16[256,1536]{1,0:T(8,128)(2,1)S(1)}, u32[]{:S(2)}) copy-start(bf16[256,1536]{1,0:T(8,128)(2,1)S(1)} %collective-permute-done.5.high_ref) | copy-start | bytes 2359300
  135.4 25.6 %collective-permute-start.14 = (f32[9,1536]{1,0:T(8,128)S(1)}, f32[9,1536]{1,0:T(8,128)S(1)}, u32[]{:S(2)}, u32[]{:S(2)}) collective-permute-start(f32[9,1536]{1,0:T(8,128)S(1)} %add_add_fusion.1), channel_id=1, source_target_pairs={{0,2},{1,3},{2,0},{3,1},{4,6},{5,7},{6,4},{7,5},{8,10},{9,11},{10,... | collective-permute-start | bytes 165896 | tf_op jit(solution)/shard_map/ppermute | solution.py:27
  140.1 0.9 copy-start.8
  140.1 1.1 copy-start.9
  144.4 17.8 %all-to-all-start.2 = ((bf16[8,32,1536]{2,1,0:T(8,128)(2,1)}), bf16[8,32,1536]{2,1,0:T(8,128)(2,1)S(1)}, u32[]{:S(2)}, u32[]{:S(2)}) async-start(bf16[8,32,1536]{2,1,0:T(8,128)(2,1)} %bitcast.35), calls=%async_computation.2 | async-start | bytes 1572864 | tf_op jit(solution)/shard_map/all_to_all | solution.py:310
  150.6 10.4 %copy-start.11 = (f32[1,1536]{1,0:T(1,128)S(1)}, f32[1,1536]{1,0:T(1,128)}, u32[]{:S(2)}) copy-start(f32[1,1536]{1,0:T(1,128)} %gain_ref.3) | copy-start | bytes 18436
  162.2 0.9 copy-start.2

commit v4 on v3

--- a/solution.py
+++ b/solution.py
@@ -15,6 +15,7 @@
 f32 = jnp.float32
 room = 60 << 20
 cheaper = 100
+order_cost = 10**10
 
 
 def shift(value, axis, steps):
@@ -61,6 +62,14 @@
         compiler_params=pltpu.CompilerParams(vmem_limit_bytes=room),
         **options,
     )
+
+
+def seen_kernel(low_ref, high_ref, out_ref):
+    out_ref[...] = jnp.zeros_like(out_ref)
+
+
+def zeros_after(rows, low, high):
+    return call(seen_kernel, like((rows, low.shape[1]), f32), order_cost, 1)(low[:8], high[:8])
 
 
 def scalar():
@@ -194,18 +203,18 @@
         mine_ref[0],
     )
     part_ref[...] = before_ref[...] + part
-    step = back.shape[0] // count
-    for i in range(count):
+    step = outs[0].shape[0]
+    for i in range(len(outs)):
         outs[i][...] = back[i * step : (i + 1) * step].astype(bf16)
 
 
-def run_experts(mine, up, down, router, before, xns, cots):
+def run_experts(mine, up, down, router, before, xns, cots, parts):
     total = sum(xn.shape[0] for xn in xns)
     width, hid = up.shape
     found = call(
         functools.partial(expert_kernel, len(xns)),
         [like((total, hid), bf16), like((total, hid), bf16), like(before.shape, f32)]
-        + [like(xn.shape, bf16) for xn in xns],
+        + [like((total // parts, width), bf16)] * parts,
         6 * total * up.size,
         4 * up.size + 8 * total * width,
         in_specs=[scalar()] + [whole()] * (4 + 2 * len(xns)),
@@ -245,11 +254,6 @@
             pl.BlockSpec((hid // steps, width), lambda i: (i, 0)),
         ],
     )(*xns, *cots, *hs, *ds)
-
-
-def merge_kernel(own_ref, high_ref, low_ref, far_ref, out_ref):
-    total = own_ref[...].astype(f32) + far_ref[...].astype(f32)
-    out_ref[...] = (total + (high_ref[...].astype(f32) + low_ref[...].astype(f32))).astype(bf16)
 
 
 def final_kernel(x_ref, gain_ref, cot_ref, slots_ref, back_ref, out_ref):
@@ -303,7 +307,7 @@
         4 * tok_count * width + 2 * slots * width,
     )(x, norm_gain, router, pair)
     arrived = lax.ppermute(
-        after(upstream_grad[0], xn_slots), "segment", [(i + 1, i) for i in range(n_segment - 1)]
+        upstream_grad[0], "segment", [(i + 1, i) for i in range(n_segment - 1)]
     )
     def exchange(rows):
         shaped = rows.reshape(experts, capacity, rows.shape[1])
@@ -318,33 +322,36 @@
         in_specs=[scalar()] + [whole()] * 5,
     )(is_last, arrived, step_noise, rewards[:, None], pick, info)
 
+    xn_own, c_slots = lax.optimization_barrier((xn_own, c_slots))
+    xn_low, xn_high = shift(xn_own, "x", 1), shift(xn_own, "x", -1)
     c_own = exchange(c_slots)
-    xn_low, xn_high = shift(xn_own, "x", 1), shift(xn_own, "x", -1)
-    c_own, xn_low, xn_high = lax.optimization_barrier((c_own, xn_low, xn_high))
+    c_own, seen = lax.optimization_barrier(
+        (c_own, zeros_after(experts + 1, xn_low, xn_high))
+    )
     c_low, c_high = shift(c_own, "x", 1), shift(c_own, "x", -1)
-    nothing = jnp.zeros((experts + 1, width), f32)
+    xn_far = [shift(xn_low[:half], "x", 1), shift(xn_high[half:], "x", -1)]
     h_own, d_own, part, (b_own,) = run_experts(
-        mine, up, down, router, nothing, [xn_own], [c_own]
-    )
-    xn_far = shift(after(xn_low, c_low), "x", 1)
-    c_far = shift(c_high, "x", -1)
+        mine, up, down, router, seen, [xn_own], [c_own], 1
+    )
+    c_low, c_high, b_own = lax.optimization_barrier((c_low, c_high, b_own))
+    c_far = [shift(c_low[:half], "x", 1), shift(c_high[half:], "x", -1)]
+    xn_low, xn_high, *xn_far = lax.optimization_barrier((xn_low, xn_high, *xn_far))
     h_near, d_near, part, (b_low, b_high) = run_experts(
-        mine, up, down, router, part, [xn_low, xn_high], [c_low, c_high]
+        mine, up, down, router, part, [xn_low, xn_high], [c_low, c_high], 2
     )
     got_high, got_low = shift(b_low, "x", -1), shift(b_high, "x", 1)
     h_far, d_far, part, (b_far,) = run_experts(
-        mine, up, down, router, part, [xn_far], [c_far]
+        mine, up, down, router, part, xn_far, c_far, 1
     )
     got_far = shift(b_far, "x", 2)
-    back = call(merge_kernel, like(b_own.shape, bf16), 1000, 8 * b_own.size // cheaper)(
-        b_own, got_high, got_low, got_far
-    )
+    total = b_own.astype(f32) + got_far.astype(f32)
+    back = (total + (got_high.astype(f32) + got_low.astype(f32))).astype(bf16)
     back_slots = exchange(back)
     up_g, down_g = run_grads(
         width,
         up.shape[1],
-        [xn_own, xn_low, xn_high, xn_far],
-        [c_own, c_low, c_high, c_far],
+        [xn_own, xn_low, xn_high, *xn_far],
+        [c_own, c_low, c_high, *c_far],
         [h_own, h_near, h_far],
         [d_own, d_near, d_far],
     )

time: 167 us -> 155 us (0.928)
  waiting for transfers between devices: 63.5 us -> 53.3 us
  starting transfers between devices: 49.5 us -> 46.7 us
  Pallas kernels: 43.7 us -> 41.9 us
    ppermute x9 -> x11, waiting for transfers between devices: 37.5 us -> 24.6 us  [shift(): lax.ppermute(value, axis, [(i, (i + steps) % count) for i in range(count)])]
    ppermute x7, waiting for transfers between devices: 5.93 us -> 12.9 us  [swap(): return lax.ppermute(value, axis, [(i, i ^ mask) for i in range(count)])]
    ppermute x7, starting transfers between devices: 14.2 us -> 8.22 us  [swap(): return lax.ppermute(value, axis, [(i, i ^ mask) for i in range(count)])]
    ppermute x9 -> x11, starting transfers between devices: 12.7 us -> 18.6 us  [shift(): lax.ppermute(value, axis, [(i, (i + steps) % count) for i in range(count)])]
    all_to_all x3, waiting for transfers between devices: 15.8 us -> 11.2 us  [exchange(): return lax.all_to_all(shaped, 'e', 0, 0, tiled=True).reshape(rows.shape)]
    slice x0 -> x6, local copies, waits for them, and re-layouts: none -> 3.93 us  [the longest x2 2.56 us: shards(): xn_far = [shift(xn_low[:half], 'x', 1), shift(xn_high[half:], 'x', -1)]]
    all_to_all x3, starting transfers between devices: 20.7 us -> 18 us  [exchange(): return lax.all_to_all(shaped, 'e', 0, 0, tiled=True).reshape(rows.shape)]
    pallas_call x1, Pallas kernels: 3.2 us -> 1.4 us  [zeros_after(): call(seen_kernel, like((rows, low.shape[1]), f32), order_cost, 1)]
  transfers between devices with their start and end apart: 20 -> 22, of which waited for: 14 -> 12; matrix products, arithmetic and copies ran while one was open for 3% -> 5% of each run, Pallas kernels for 23% -> 24%
where the time goes in v4:
time: 155 us; the launch traced here: 153 us
  waiting for transfers between devices  53.3 us (34%)
  starting transfers between devices  46.7 us (30%)
  Pallas kernels  41.9 us (27%)
  local copies, waits for them, and re-layouts  7.75 us (5%)
  other arithmetic  2.83 us (2%)
    ppermute x11, waiting for transfers between devices, shift(): lax.ppermute(value, axis, [(i, (i + steps) % count) for i in range(count)])  24.6 us
    pallas_call x3, Pallas kernels, run_experts(): call(functools.partial(expert_kernel, len(xns)), [like((total, hid), bf16...  22.5 us
    ppermute x11, starting transfers between devices, shift(): lax.ppermute(value, axis, [(i, (i + steps) % count) for i in range(count)])  18.6 us
    all_to_all x3, starting transfers between devices, exchange(): return lax.all_to_all(shaped, 'e', 0, 0, tiled=True).reshape(rows.shape)  18 us
    ppermute x7, waiting for transfers between devices, swap(): return lax.ppermute(value, axis, [(i, i ^ mask) for i in range(count)])  12.9 us
    all_to_all x3, waiting for transfers between devices, exchange(): return lax.all_to_all(shaped, 'e', 0, 0, tiled=True).reshape(rows.shape)  11.2 us
    pallas_call x1, Pallas kernels, run_grads(): call(functools.partial(grads_kernel, len(xns), len(cots), len(hs)), [like...  10.4 us
    ppermute x7, starting transfers between devices, swap(): return lax.ppermute(value, axis, [(i, i ^ mask) for i in range(count)])  8.22 us
  transfers between devices with their start and end apart: 22, of which 12 were waited for; matrix products, arithmetic and copies ran while one was open for 5% of the time, Pallas kernels for 24%

profile of v4, /device:TPU:64, one launch (start us, length us, event | category | flops | bytes accessed | tf_op | source)
XLA Modules:
  0.0 153.3 jit_solution(2439003049447321906)
XLA Ops:
  0.7 2.5 %shard_map.128 = (bf16[256,1536]{1,0:T(8,128)(2,1)}, bf16[256,128]{1,0:T(8,128)(2,1)}, bf16[256,128]{1,0:T(8,128)(2,1)}, bf16[128,256]{1,0:T(8,128)(2,1)}) custom-call(bf16[128,1536]{1,0:T(8,128)(2,1)} %bitcast.35, f32[1,1536]{1,0:T(1,128)} %gain_ref.3, bf16[8,1536]{1,0:T(8,128)(2,1)} %bitcast.40, s32[2,128]{1,0:T(2,128)} %bitcast.44), custom_call_target="tpu_custom_call" | custom-call | flops 100663296 | bytes 1572864 | tf_op jit(solution)/shard_map/pallas_call | solution.py:298
  3.2 5.8 %all-to-all-start = ((bf16[8,32,1536]{2,1,0:T(8,128)(2,1)}), bf16[8,32,1536]{2,1,0:T(8,128)(2,1)S(1)}, u32[]{:S(2)}, u32[]{:S(2)}) async-start(bf16[8,32,1536]{2,1,0:T(8,128)(2,1)} %bitcast.38), calls=%async_computation | async-start | bytes 1572864 | tf_op jit(solution)/shard_map/all_to_all | solution.py:314
  9.0 1.9 %collective-permute-start = (bf16[128,1536]{1,0:T(8,128)(2,1)S(1)}, bf16[128,1536]{1,0:T(8,128)(2,1)S(1)}, u32[]{:S(2)}, u32[]{:S(2)}) collective-permute-start(bf16[128,1536]{1,0:T(8,128)(2,1)S(1)} %bitcast.54), channel_id=1, source_target_pairs={{32,0},{64,32},{96,64},{128,96},{160,128},{192,160},{224,192},{33,... | collective-permute-start | bytes 1179656 | tf_op jit(solution)/shard_map/ppermute | solution.py:309
  11.0 0.7 copy.14.rewards_ref
  11.7 4.6 %collective-permute-done.arrived_ref = bf16[128,1536]{1,0:T(8,128)(2,1)S(1)} collective-permute-done((bf16[128,1536]{1,0:T(8,128)(2,1)S(1)}, bf16[128,1536]{1,0:T(8,128)(2,1)S(1)}, u32[]{:S(2)}, u32[]{:S(2)}) %collective-permute-start) | collective-permute-done | bytes 393248 | tf_op jit(solution)/shard_map/ppermute | solution.py:309
  16.3 0.7 copy-done.9
  17.0 2.5 %shard_map.129 = (bf16[128,1536]{1,0:T(8,128)(2,1)}, bf16[256,1664]{1,0:T(8,128)(2,1)}) custom-call(s32[1]{0:T(128)} %bitcast.1.last_ref, bf16[128,1536]{1,0:T(8,128)(2,1)} %copy-done.9, bf16[128,1536]{1,0:T(8,128)(2,1)} %noise_ref.1, f32[128,1]{1,0:T(8,128)} %copy.14.rewards_ref, bf16[256,128]{1,0:T(8,128)(2,1)} %get-tuple-element.37.pick_ref, ...), custom_call_target="tpu_custom_call" | custom-call | flops 100663296 | bytes 1966080 | tf_op jit(solution)/shard_map/pallas_call | solution.py:317
  19.6 6.6 %all-to-all-done = bf16[8,32,1536]{2,1,0:T(8,128)(2,1)S(1)} async-done(((bf16[8,32,1536]{2,1,0:T(8,128)(2,1)}), bf16[8,32,1536]{2,1,0:T(8,128)(2,1)S(1)}, u32[]{:S(2)}, u32[]{:S(2)}) %all-to-all-start) | async-done | bytes 786464 | tf_op jit(solution)/shard_map/all_to_all | solution.py:314
  26.1 1.5 collective-permute-start.1
  27.6 1.7 %collective-permute-start.2 = (bf16[256,1536]{1,0:T(8,128)(2,1)S(1)}, bf16[256,1536]{1,0:T(8,128)(2,1)S(1)}, u32[]{:S(2)}, u32[]{:S(2)}) collective-permute-start(bf16[256,1536]{1,0:T(8,128)(2,1)S(1)} %bitcast.31), channel_id=1, source_target_pairs={{0,3},{1,0},{2,1},{3,2},{4,7},{5,4},{6,5},{7,6},{8,11},{9,8},{10,9... | collective-permute-start | bytes 2359304 | tf_op jit(solution)/shard_map/ppermute | solution.py:23
  29.4 8.6 %all-to-all-start.1 = ((bf16[8,32,1664]{2,1,0:T(8,128)(2,1)}), bf16[8,32,1664]{2,1,0:T(8,128)(2,1)S(1)}, u32[]{:S(2)}, u32[]{:S(2)}) async-start(bf16[8,32,1664]{2,1,0:T(8,128)(2,1)} %bitcast.37), calls=%async_computation.1 | async-start | bytes 1703936 | tf_op jit(solution)/shard_map/all_to_all | solution.py:314
  38.0 7.2 %collective-permute-done.1.refs_0_.refs_1_ = bf16[256,1536]{1,0:T(8,128)(2,1)S(1)} collective-permute-done((bf16[256,1536]{1,0:T(8,128)(2,1)S(1)}, bf16[256,1536]{1,0:T(8,128)(2,1)S(1)}, u32[]{:S(2)}, u32[]{:S(2)}) %collective-permute-start.1) | collective-permute-done | bytes 786464 | tf_op jit(solution)/shard_map/ppermute | solution.py:23
  45.1 0.7 slice.32.low_ref
  45.8 0.0 collective-permute-done.2.refs_1_.refs_2_
  45.8 0.7 slice.33.high_ref
  46.5 1.4 shard_map.130.before_ref
  47.9 3.3 %all-to-all-done.1 = bf16[8,32,1664]{2,1,0:T(8,128)(2,1)S(1)} async-done(((bf16[8,32,1664]{2,1,0:T(8,128)(2,1)}), bf16[8,32,1664]{2,1,0:T(8,128)(2,1)S(1)}, u32[]{:S(2)}, u32[]{:S(2)}) %all-to-all-start.1) | async-done | bytes 852000 | tf_op jit(solution)/shard_map/all_to_all | solution.py:314
  51.1 0.3 collective-permute-start.3
  51.4 3.0 %collective-permute-start.4 = (bf16[256,1664]{1,0:T(8,128)(2,1)S(1)}, bf16[256,1664]{1,0:T(8,128)(2,1)S(1)}, u32[]{:S(2)}, u32[]{:S(2)}) collective-permute-start(bf16[256,1664]{1,0:T(8,128)(2,1)S(1)} %bitcast.27), channel_id=1, source_target_pairs={{0,3},{1,0},{2,1},{3,2},{4,7},{5,4},{6,5},{7,6},{8,11},{9,8},{10,9... | collective-permute-start | bytes 2555912 | tf_op jit(solution)/shard_map/ppermute | solution.py:23
  54.4 0.8 slice.34
  55.1 0.0 collective-permute-start.5
  55.1 1.8 %slice.35 = bf16[128,1536]{1,0:T(8,128)(2,1)} slice(bf16[256,1536]{1,0:T(8,128)(2,1)} %copy-done.6), slice={[128:256], [0:1536]} | slice | bytes 786432 | tf_op jit(solution)/shard_map/slice | solution.py:332
  56.9 3.2 %collective-permute-start.6 = (bf16[128,1536]{1,0:T(8,128)(2,1)}, bf16[128,1536]{1,0:T(8,128)(2,1)}, u32[]{:S(2)}, u32[]{:S(2)}) collective-permute-start(bf16[128,1536]{1,0:T(8,128)(2,1)} %slice.35), channel_id=1, source_target_pairs={{0,3},{1,0},{2,1},{3,2},{4,7},{5,4},{6,5},{7,6},{8,11},{9,8},{10,9... | collective-permute-start | bytes 1179656 | tf_op jit(solution)/shard_map/ppermute | solution.py:23
  60.2 6.5 %shard_map.131 = (bf16[256,768]{1,0:T(8,128)(2,1)}, bf16[256,768]{1,0:T(8,128)(2,1)}, f32[9,1536]{1,0:T(8,128)}, bf16[256,1536]{1,0:T(8,128)(2,1)}) custom-call(s32[1]{0:T(128)} %bitcast.12.mine_ref, bf16[1536,768]{1,0:T(8,128)(2,1)} %bitcast.46, bf16[768,1536]{1,0:T(8,128)(2,1)} %bitcast.49, bf16[8,1536]{1,0:T(8,128)(2,1)} %bitcast.41, ...), custom_call_target="tpu_custom_call" | custom-call | flops 1811939328 | bytes 7864320 | tf_op jit(solution)/shard_map/pallas_call | solution.py:214
  66.6 6.8 %collective-permute-done.3.refs_2_.refs_6_ = bf16[256,1664]{1,0:T(8,128)(2,1)S(1)} collective-permute-done((bf16[256,1664]{1,0:T(8,128)(2,1)S(1)}, bf16[256,1664]{1,0:T(8,128)(2,1)S(1)}, u32[]{:S(2)}, u32[]{:S(2)}) %collective-permute-start.3) | collective-permute-done | bytes 852000 | tf_op jit(solution)/shard_map/ppermute | solution.py:23
  73.4 0.0 collective-permute-done.4.refs_3_.refs_7_
  73.5 1.0 collective-permute-start.7
  74.5 3.0 %collective-permute-start.8 = (bf16[128,1664]{1,0:T(8,128)(2,1)S(1)}, bf16[128,1664]{1,0:T(8,128)(2,1)}, u32[]{:S(2)}, u32[]{:S(2)}) collective-permute-start(bf16[128,1664]{1,0:T(8,128)(2,1)S(1)} %slice.29), channel_id=1, source_target_pairs={{0,3},{1,0},{2,1},{3,2},{4,7},{5,4},{6,5},{7,6},{8,11},{9,8},{10,9... | collective-permute-start | bytes 1277960 | tf_op jit(solution)/shard_map/ppermute | solution.py:23
  77.4 4.5 %collective-permute-done.5.refs_0_.refs_3_ = bf16[128,1536]{1,0:T(8,128)(2,1)} collective-permute-done((bf16[128,1536]{1,0:T(8,128)(2,1)}, bf16[128,1536]{1,0:T(8,128)(2,1)}, u32[]{:S(2)}, u32[]{:S(2)}) %collective-permute-start.5) | collective-permute-done | bytes 393248 | tf_op jit(solution)/shard_map/ppermute | solution.py:23
  82.0 0.0 collective-permute-done.6.refs_1_.refs_4_
  82.0 9.4 %shard_map.132 = (bf16[512,768]{1,0:T(8,128)(2,1)}, bf16[512,768]{1,0:T(8,128)(2,1)}, f32[9,1536]{1,0:T(8,128)}, bf16[256,1536]{1,0:T(8,128)(2,1)}, bf16[256,1536]{1,0:T(8,128)(2,1)}) custom-call(s32[1]{0:T(128)} %bitcast.12.mine_ref, bf16[1536,768]{1,0:T(8,128)(2,1)} %bitcast.47, bf16[768,1536]{1,0:T(8,128)(2,1)} %bitcast.50, bf16[8,1536]{1,0:T(8,128)(2,1)} %bitcast.42, ...), custom_call_target="tpu_custom_call" | custom-call | flops 3623878656 | bytes 11010048 | tf_op jit(solution)/shard_map/pallas_call | solution.py:214
  91.4 0.9 collective-permute-start.11
  92.3 2.8 %collective-permute-start.10 = (bf16[256,1536]{1,0:T(8,128)(2,1)}, bf16[256,1536]{1,0:T(8,128)(2,1)S(1)}, u32[]{:S(2)}, u32[]{:S(2)}) collective-permute-start(bf16[256,1536]{1,0:T(8,128)(2,1)} %get-tuple-element.57), channel_id=1, source_target_pairs={{0,3},{1,0},{2,1},{3,2},{4,7},{5,4},{6,5},{7,6},{8,11},{9,8},{10,9... | collective-permute-start | bytes 2359304 | tf_op jit(solution)/shard_map/ppermute | solution.py:23
  95.0 0.0 collective-permute-done.7.refs_2_.refs_8_
  95.0 0.0 collective-permute-done.8.refs_3_.refs_9_
  95.0 0.8 copy-done.8
  95.8 6.6 %shard_map.133 = (bf16[256,768]{1,0:T(8,128)(2,1)}, bf16[256,768]{1,0:T(8,128)(2,1)}, f32[9,1536]{1,0:T(8,128)}, bf16[256,1536]{1,0:T(8,128)(2,1)}) custom-call(s32[1]{0:T(128)} %bitcast.12.mine_ref, bf16[1536,768]{1,0:T(8,128)(2,1)} %bitcast.48, bf16[768,1536]{1,0:T(8,128)(2,1)} %bitcast.51, bf16[8,1536]{1,0:T(8,128)(2,1)} %bitcast.43, ...), custom_call_target="tpu_custom_call" | custom-call | flops 1811939328 | bytes 7864320 | tf_op jit(solution)/shard_map/pallas_call | solution.py:214
  102.4 1.4 collective-permute-start.9
  103.8 1.0 collective-permute-start.12
  104.8 4.7 %collective-permute-done.12 = f32[9,1536]{1,0:T(8,128)S(1)} collective-permute-done((f32[9,1536]{1,0:T(8,128)}, f32[9,1536]{1,0:T(8,128)S(1)}, u32[]{:S(2)}, u32[]{:S(2)}) %collective-permute-start.12) | collective-permute-done | bytes 55328 | tf_op jit(solution)/shard_map/ppermute | solution.py:28
  109.5 0.9 add.33
  110.4 0.1 collective-permute-start.14
  110.5 1.7 %collective-permute-start.15 = (f32[9,1536]{1,0:T(8,128)S(1)}, f32[9,1536]{1,0:T(8,128)S(1)}, u32[]{:S(2)}, u32[]{:S(2)}) collective-permute-start(f32[9,1536]{1,0:T(8,128)S(1)} %add.33), channel_id=1, source_target_pairs={{0,24},{4,28},{8,16},{12,20},{16,8},{20,12},{24,0},{28,4},{1,25},{... | collective-permute-start | bytes 165896 | tf_op jit(solution)/shard_map/ppermute | solution.py:28
  112.1 3.4 %collective-permute-done.14 = f32[9,1536]{1,0:T(8,128)S(1)} collective-permute-done((f32[9,1536]{1,0:T(8,128)S(1)}, f32[9,1536]{1,0:T(8,128)S(1)}, u32[]{:S(2)}, u32[]{:S(2)}) %collective-permute-start.14) | collective-permute-done | bytes 55328 | tf_op jit(solution)/shard_map/ppermute | solution.py:28
  115.5 1.3 collective-permute-start.13
  116.8 0.0 collective-permute-done.15
  116.8 4.8 %collective-permute-done.13 = f32[9,1536]{1,0:T(8,128)S(1)} collective-permute-done((f32[9,1536]{1,0:T(8,128)S(1)}, f32[9,1536]{1,0:T(8,128)S(1)}, u32[]{:S(2)}, u32[]{:S(2)}) %collective-permute-start.13) | collective-permute-done | bytes 55328 | tf_op jit(solution)/shard_map/ppermute | solution.py:28
  121.7 1.4 collective-permute-start.17
  123.1 1.4 collective-permute-start.18
  124.4 0.0 collective-permute-done.11
  124.5 1.4 collective-permute-start.16
  125.8 4.2 %collective-permute-done.10 = bf16[256,1536]{1,0:T(8,128)(2,1)S(1)} collective-permute-done((bf16[256,1536]{1,0:T(8,128)(2,1)}, bf16[256,1536]{1,0:T(8,128)(2,1)S(1)}, u32[]{:S(2)}, u32[]{:S(2)}) %collective-permute-start.10) | collective-permute-done | bytes 786464 | tf_op jit(solution)/shard_map/ppermute | solution.py:23
  130.1 1.8 %collective-permute-done.9 = bf16[256,1536]{1,0:T(8,128)(2,1)S(1)} collective-permute-done((bf16[256,1536]{1,0:T(8,128)(2,1)}, bf16[256,1536]{1,0:T(8,128)(2,1)S(1)}, u32[]{:S(2)}, u32[]{:S(2)}) %collective-permute-start.9) | collective-permute-done | bytes 786464 | tf_op jit(solution)/shard_map/ppermute | solution.py:23
  131.9 1.3 add_convert_fusion
  133.2 3.5 %all-to-all-start.2 = ((bf16[8,32,1536]{2,1,0:T(8,128)(2,1)}), bf16[8,32,1536]{2,1,0:T(8,128)(2,1)S(1)}, u32[]{:S(2)}, u32[]{:S(2)}) async-start(bf16[8,32,1536]{2,1,0:T(8,128)(2,1)} %bitcast.16), calls=%async_computation.2 | async-start | bytes 1572864 | tf_op jit(solution)/shard_map/all_to_all | solution.py:314
  136.7 0.0 copy-start.10
  136.7 10.4 %shard_map.135 = (bf16[1536,768]{1,0:T(8,128)(2,1)}, bf16[768,1536]{1,0:T(8,128)(2,1)}) custom-call(bf16[256,1536]{1,0:T(8,128)(2,1)} %bitcast.33, bf16[256,1536]{1,0:T(8,128)(2,1)} %copy-done.5, bf16[256,1536]{1,0:T(8,128)(2,1)} %copy-done.6, bf16[128,1536]{1,0:T(8,128)(2,1)} %collective-permute-done.5.refs_0_.refs_3_, ...), custom_call_target="tpu_custom_call" | custom-call | flops 48318384 | bytes 141557 | tf_op jit(solution)/shard_map/pallas_call | solution.py:245
  147.1 0.0 collective-permute-done.17
  147.1 0.0 collective-permute-done.18
  147.2 0.6 slice_divide_fusion
  147.8 0.6 slice_bitcast_fusion
  148.4 1.4 all-to-all-done.2
  149.8 0.9 copy-done.2
  150.7 2.6 %shard_map.134 = bf16[128,1536]{1,0:T(8,128)(2,1)} custom-call(bf16[128,1536]{1,0:T(8,128)(2,1)} %bitcast.36, f32[1,1536]{1,0:T(1,128)} %gain_ref.3, bf16[128,1536]{1,0:T(8,128)(2,1)} %get-tuple-element.39.cot_ref, bf16[256,1536]{1,0:T(8,128)(2,1)} %bitcast.34, bf16[128,256]{1,0:T(8,128)(2,1)} %get-tuple-element.59.back_ref), custom_call_target="tpu_custom_call" | custom-call | flops 100663296 | bytes 2359296 | tf_op jit(solution)/shard_map/pallas_call | solution.py:362
  (27 shorter events, 0.2 us)
Async XLA Ops:
  0.6 8.4 %copy-start.12 = (bf16[1,128,1536]{2,1,0:T(8,128)(2,1)S(1)}, bf16[1,128,1536]{2,1,0:T(8,128)(2,1)}, u32[]{:S(2)}) copy-start(bf16[1,128,1536]{2,1,0:T(8,128)(2,1)} %param.10) | copy-start | bytes 1179652
  0.6 10.3 %copy-start.11 = (f32[128]{0:T(128)S(1)}, f32[128]{0:T(128)}, u32[]{:S(2)}) copy-start(f32[128]{0:T(128)} %param.12) | copy-start | bytes 1540
  3.2 22.9 %all-to-all-start = ((bf16[8,32,1536]{2,1,0:T(8,128)(2,1)}), bf16[8,32,1536]{2,1,0:T(8,128)(2,1)S(1)}, u32[]{:S(2)}, u32[]{:S(2)}) async-start(bf16[8,32,1536]{2,1,0:T(8,128)(2,1)} %bitcast.38), calls=%async_computation | async-start | bytes 1572864 | tf_op jit(solution)/shard_map/all_to_all | solution.py:314
  9.0 7.2 %collective-permute-start = (bf16[128,1536]{1,0:T(8,128)(2,1)S(1)}, bf16[128,1536]{1,0:T(8,128)(2,1)S(1)}, u32[]{:S(2)}, u32[]{:S(2)}) collective-permute-start(bf16[128,1536]{1,0:T(8,128)(2,1)S(1)} %bitcast.54), channel_id=1, source_target_pairs={{32,0},{64,32},{96,64},{128,96},{160,128},{192,160},{224,192},{33,... | collective-permute-start | bytes 1179656 | tf_op jit(solution)/shard_map/ppermute | solution.py:309
  16.3 0.7 copy-start.9
  26.1 21.7 %copy-start.1 = (bf16[8,32,1536]{2,1,0:T(8,128)(2,1)}, bf16[8,32,1536]{2,1,0:T(8,128)(2,1)S(1)}, u32[]{:S(2)}) copy-start(bf16[8,32,1536]{2,1,0:T(8,128)(2,1)S(1)} %all-to-all-done) | copy-start | bytes 2359300
  26.1 19.0 %collective-permute-start.1 = (bf16[256,1536]{1,0:T(8,128)(2,1)S(1)}, bf16[256,1536]{1,0:T(8,128)(2,1)S(1)}, u32[]{:S(2)}, u32[]{:S(2)}) collective-permute-start(bf16[256,1536]{1,0:T(8,128)(2,1)S(1)} %bitcast.30), channel_id=1, source_target_pairs={{0,1},{1,2},{2,3},{3,0},{4,5},{5,6},{6,7},{7,4},{8,9},{9,10},{10,1... | collective-permute-start | bytes 2359304 | tf_op jit(solution)/shard_map/ppermute | solution.py:23
  27.6 18.2 %collective-permute-start.2 = (bf16[256,1536]{1,0:T(8,128)(2,1)S(1)}, bf16[256,1536]{1,0:T(8,128)(2,1)S(1)}, u32[]{:S(2)}, u32[]{:S(2)}) collective-permute-start(bf16[256,1536]{1,0:T(8,128)(2,1)S(1)} %bitcast.31), channel_id=1, source_target_pairs={{0,3},{1,0},{2,1},{3,2},{4,7},{5,4},{6,5},{7,6},{8,11},{9,8},{10,9... | collective-permute-start | bytes 2359304 | tf_op jit(solution)/shard_map/ppermute | solution.py:23
  29.4 21.8 %all-to-all-start.1 = ((bf16[8,32,1664]{2,1,0:T(8,128)(2,1)}), bf16[8,32,1664]{2,1,0:T(8,128)(2,1)S(1)}, u32[]{:S(2)}, u32[]{:S(2)}) async-start(bf16[8,32,1664]{2,1,0:T(8,128)(2,1)} %bitcast.37), calls=%async_computation.1 | async-start | bytes 1703936 | tf_op jit(solution)/shard_map/all_to_all | solution.py:314
  45.1 9.2 %copy-start.5 = (bf16[256,1536]{1,0:T(8,128)(2,1)}, bf16[256,1536]{1,0:T(8,128)(2,1)S(1)}, u32[]{:S(2)}) copy-start(bf16[256,1536]{1,0:T(8,128)(2,1)S(1)} %collective-permute-done.1.refs_0_.refs_1_) | copy-start | bytes 2359300
  45.8 2.1 %copy-start.6 = (bf16[256,1536]{1,0:T(8,128)(2,1)}, bf16[256,1536]{1,0:T(8,128)(2,1)S(1)}, u32[]{:S(2)}) copy-start(bf16[256,1536]{1,0:T(8,128)(2,1)S(1)} %collective-permute-done.2.refs_1_.refs_2_) | copy-start | bytes 2359300
  51.1 9.0 %copy-start = (bf16[8,32,1664]{2,1,0:T(8,128)(2,1)}, bf16[8,32,1664]{2,1,0:T(8,128)(2,1)S(1)}, u32[]{:S(2)}) copy-start(bf16[8,32,1664]{2,1,0:T(8,128)(2,1)S(1)} %all-to-all-done.1) | copy-start | bytes 2555908
  51.1 22.3 %collective-permute-start.3 = (bf16[256,1664]{1,0:T(8,128)(2,1)S(1)}, bf16[256,1664]{1,0:T(8,128)(2,1)S(1)}, u32[]{:S(2)}, u32[]{:S(2)}) collective-permute-start(bf16[256,1664]{1,0:T(8,128)(2,1)S(1)} %bitcast.26), channel_id=1, source_target_pairs={{0,1},{1,2},{2,3},{3,0},{4,5},{5,6},{6,7},{7,4},{8,9},{9,10},{10,1... | collective-permute-start | bytes 2555912 | tf_op jit(solution)/shard_map/ppermute | solution.py:23
  51.4 22.0 %collective-permute-start.4 = (bf16[256,1664]{1,0:T(8,128)(2,1)S(1)}, bf16[256,1664]{1,0:T(8,128)(2,1)S(1)}, u32[]{:S(2)}, u32[]{:S(2)}) collective-permute-start(bf16[256,1664]{1,0:T(8,128)(2,1)S(1)} %bitcast.27), channel_id=1, source_target_pairs={{0,3},{1,0},{2,1},{3,2},{4,7},{5,4},{6,5},{7,6},{8,11},{9,8},{10,9... | collective-permute-start | bytes 2555912 | tf_op jit(solution)/shard_map/ppermute | solution.py:23
  55.1 26.8 %collective-permute-start.5 = (bf16[128,1536]{1,0:T(8,128)(2,1)}, bf16[128,1536]{1,0:T(8,128)(2,1)}, u32[]{:S(2)}, u32[]{:S(2)}) collective-permute-start(bf16[128,1536]{1,0:T(8,128)(2,1)} %slice.34), channel_id=1, source_target_pairs={{0,1},{1,2},{2,3},{3,0},{4,5},{5,6},{6,7},{7,4},{8,9},{9,10},{10,1... | collective-permute-start | bytes 1179656 | tf_op jit(solution)/shard_map/ppermute | solution.py:23
  56.9 25.0 %collective-permute-start.6 = (bf16[128,1536]{1,0:T(8,128)(2,1)}, bf16[128,1536]{1,0:T(8,128)(2,1)}, u32[]{:S(2)}, u32[]{:S(2)}) collective-permute-start(bf16[128,1536]{1,0:T(8,128)(2,1)} %slice.35), channel_id=1, source_target_pairs={{0,3},{1,0},{2,1},{3,2},{4,7},{5,4},{6,5},{7,6},{8,11},{9,8},{10,9... | collective-permute-start | bytes 1179656 | tf_op jit(solution)/shard_map/ppermute | solution.py:23
  73.4 8.5 %copy-start.3 = (bf16[256,1664]{1,0:T(8,128)(2,1)}, bf16[256,1664]{1,0:T(8,128)(2,1)S(1)}, u32[]{:S(2)}) copy-start(bf16[256,1664]{1,0:T(8,128)(2,1)S(1)} %collective-permute-done.3.refs_2_.refs_6_) | copy-start | bytes 2555908
  73.4 8.5 %copy-start.4 = (bf16[256,1664]{1,0:T(8,128)(2,1)}, bf16[256,1664]{1,0:T(8,128)(2,1)S(1)}, u32[]{:S(2)}) copy-start(bf16[256,1664]{1,0:T(8,128)(2,1)S(1)} %collective-permute-done.4.refs_3_.refs_7_) | copy-start | bytes 2555908
  73.5 21.5 %collective-permute-start.7 = (bf16[128,1664]{1,0:T(8,128)(2,1)S(1)}, bf16[128,1664]{1,0:T(8,128)(2,1)S(1)}, u32[]{:S(2)}, u32[]{:S(2)}) collective-permute-start(bf16[128,1664]{1,0:T(8,128)(2,1)S(1)} %slice.28), channel_id=1, source_target_pairs={{0,1},{1,2},{2,3},{3,0},{4,5},{5,6},{6,7},{7,4},{8,9},{9,10},{10,1... | collective-permute-start | bytes 1277960 | tf_op jit(solution)/shard_map/ppermute | solution.py:23
  74.5 20.6 %collective-permute-start.8 = (bf16[128,1664]{1,0:T(8,128)(2,1)S(1)}, bf16[128,1664]{1,0:T(8,128)(2,1)}, u32[]{:S(2)}, u32[]{:S(2)}) collective-permute-start(bf16[128,1664]{1,0:T(8,128)(2,1)S(1)} %slice.29), channel_id=1, source_target_pairs={{0,3},{1,0},{2,1},{3,2},{4,7},{5,4},{6,5},{7,6},{8,11},{9,8},{10,9... | collective-permute-start | bytes 1277960 | tf_op jit(solution)/shard_map/ppermute | solution.py:23
  91.4 33.1 %collective-permute-start.11 = (bf16[256,1536]{1,0:T(8,128)(2,1)}, bf16[256,1536]{1,0:T(8,128)(2,1)S(1)}, u32[]{:S(2)}, u32[]{:S(2)}) collective-permute-start(bf16[256,1536]{1,0:T(8,128)(2,1)} %get-tuple-element.58), channel_id=1, source_target_pairs={{0,1},{1,2},{2,3},{3,0},{4,5},{5,6},{6,7},{7,4},{8,9},{9,10},{10,1... | collective-permute-start | bytes 2359304 | tf_op jit(solution)/shard_map/ppermute | solution.py:23
  92.3 37.8 %collective-permute-start.10 = (bf16[256,1536]{1,0:T(8,128)(2,1)}, bf16[256,1536]{1,0:T(8,128)(2,1)S(1)}, u32[]{:S(2)}, u32[]{:S(2)}) collective-permute-start(bf16[256,1536]{1,0:T(8,128)(2,1)} %get-tuple-element.57), channel_id=1, source_target_pairs={{0,3},{1,0},{2,1},{3,2},{4,7},{5,4},{6,5},{7,6},{8,11},{9,8},{10,9... | collective-permute-start | bytes 2359304 | tf_op jit(solution)/shard_map/ppermute | solution.py:23
  95.0 0.8 copy-start.8
  95.8 36.1 %copy-start.7 = (bf16[256,1536]{1,0:T(8,128)(2,1)S(1)}, bf16[256,1536]{1,0:T(8,128)(2,1)}, u32[]{:S(2)}) copy-start(bf16[256,1536]{1,0:T(8,128)(2,1)} %get-tuple-element.47) | copy-start | bytes 2359300
  102.4 29.5 %collective-permute-start.9 = (bf16[256,1536]{1,0:T(8,128)(2,1)}, bf16[256,1536]{1,0:T(8,128)(2,1)S(1)}, u32[]{:S(2)}, u32[]{:S(2)}) collective-permute-start(bf16[256,1536]{1,0:T(8,128)(2,1)} %get-tuple-element.56), channel_id=1, source_target_pairs={{0,2},{1,3},{2,0},{3,1},{4,6},{5,7},{6,4},{7,5},{8,10},{9,11},{10,... | collective-permute-start | bytes 2359304 | tf_op jit(solution)/shard_map/ppermute | solution.py:23
  103.8 5.6 %collective-permute-start.12 = (f32[9,1536]{1,0:T(8,128)}, f32[9,1536]{1,0:T(8,128)S(1)}, u32[]{:S(2)}, u32[]{:S(2)}) collective-permute-start(f32[9,1536]{1,0:T(8,128)} %get-tuple-element.68), channel_id=1, source_target_pairs={{0,4},{4,0},{8,12},{12,8},{16,20},{20,16},{24,28},{28,24},{1,5},{5... | collective-permute-start | bytes 165896 | tf_op jit(solution)/shard_map/ppermute | solution.py:28
  110.4 5.2 %collective-permute-start.14 = (f32[9,1536]{1,0:T(8,128)S(1)}, f32[9,1536]{1,0:T(8,128)S(1)}, u32[]{:S(2)}, u32[]{:S(2)}) collective-permute-start(f32[9,1536]{1,0:T(8,128)S(1)} %add.33), channel_id=1, source_target_pairs={{0,8},{4,12},{8,0},{12,4},{16,24},{20,28},{24,16},{28,20},{1,9},{5... | collective-permute-start | bytes 165896 | tf_op jit(solution)/shard_map/ppermute | solution.py:28
  110.5 6.4 %collective-permute-start.15 = (f32[9,1536]{1,0:T(8,128)S(1)}, f32[9,1536]{1,0:T(8,128)S(1)}, u32[]{:S(2)}, u32[]{:S(2)}) collective-permute-start(f32[9,1536]{1,0:T(8,128)S(1)} %add.33), channel_id=1, source_target_pairs={{0,24},{4,28},{8,16},{12,20},{16,8},{20,12},{24,0},{28,4},{1,25},{... | collective-permute-start | bytes 165896 | tf_op jit(solution)/shard_map/ppermute | solution.py:28
  115.5 6.1 %collective-permute-start.13 = (f32[9,1536]{1,0:T(8,128)S(1)}, f32[9,1536]{1,0:T(8,128)S(1)}, u32[]{:S(2)}, u32[]{:S(2)}) collective-permute-start(f32[9,1536]{1,0:T(8,128)S(1)} %add.33), channel_id=1, source_target_pairs={{0,16},{4,20},{8,24},{12,28},{16,0},{20,4},{24,8},{28,12},{1,17},{... | collective-permute-start | bytes 165896 | tf_op jit(solution)/shard_map/ppermute | solution.py:28
  121.7 25.4 %collective-permute-start.17 = (f32[9,1536]{1,0:T(8,128)S(1)}, f32[9,1536]{1,0:T(8,128)S(1)}, u32[]{:S(2)}, u32[]{:S(2)}) collective-permute-start(f32[9,1536]{1,0:T(8,128)S(1)} %add_add_fusion.1), channel_id=1, source_target_pairs={{0,1},{1,0},{2,3},{3,2},{4,5},{5,4},{6,7},{7,6},{8,9},{9,8},{10,11... | collective-permute-start | bytes 165896 | tf_op jit(solution)/shard_map/ppermute | solution.py:28
  123.1 24.0 %collective-permute-start.18 = (f32[9,1536]{1,0:T(8,128)S(1)}, f32[9,1536]{1,0:T(8,128)S(1)}, u32[]{:S(2)}, u32[]{:S(2)}) collective-permute-start(f32[9,1536]{1,0:T(8,128)S(1)} %add_add_fusion.1), channel_id=1, source_target_pairs={{0,3},{1,2},{2,1},{3,0},{4,7},{5,6},{6,5},{7,4},{8,11},{9,10},{10,... | collective-permute-start | bytes 165896 | tf_op jit(solution)/shard_map/ppermute | solution.py:28
  124.5 22.7 %collective-permute-start.16 = (f32[9,1536]{1,0:T(8,128)S(1)}, f32[9,1536]{1,0:T(8,128)S(1)}, u32[]{:S(2)}, u32[]{:S(2)}) collective-permute-start(f32[9,1536]{1,0:T(8,128)S(1)} %add_add_fusion.1), channel_id=1, source_target_pairs={{0,2},{1,3},{2,0},{3,1},{4,6},{5,7},{6,4},{7,5},{8,10},{9,11},{10,... | collective-permute-start | bytes 165896 | tf_op jit(solution)/shard_map/ppermute | solution.py:28
  133.2 16.6 %all-to-all-start.2 = ((bf16[8,32,1536]{2,1,0:T(8,128)(2,1)}), bf16[8,32,1536]{2,1,0:T(8,128)(2,1)S(1)}, u32[]{:S(2)}, u32[]{:S(2)}) async-start(bf16[8,32,1536]{2,1,0:T(8,128)(2,1)} %bitcast.16), calls=%async_computation.2 | async-start | bytes 1572864 | tf_op jit(solution)/shard_map/all_to_all | solution.py:314
  136.7 10.4 %copy-start.10 = (f32[1,1536]{1,0:T(1,128)S(1)}, f32[1,1536]{1,0:T(1,128)}, u32[]{:S(2)}) copy-start(f32[1,1536]{1,0:T(1,128)} %gain_ref.3) | copy-start | bytes 18436
  149.8 0.9 copy-start.2

commit v5 on v4

--- a/solution.py
+++ b/solution.py
@@ -64,12 +64,17 @@
     )
 
 
-def seen_kernel(low_ref, high_ref, out_ref):
-    out_ref[...] = jnp.zeros_like(out_ref)
-
-
-def zeros_after(rows, low, high):
-    return call(seen_kernel, like((rows, low.shape[1]), f32), order_cost, 1)(low[:8], high[:8])
+def forward_kernel(low_ref, high_ref, zero_ref, from_low_ref, from_high_ref):
+    half = from_low_ref.shape[0]
+    zero_ref[...] = jnp.zeros_like(zero_ref)
+    from_low_ref[...] = low_ref[:half, :]
+    from_high_ref[...] = high_ref[half:, :]
+
+
+def forward_halves(rows, low, high):
+    piece = like((low.shape[0] // 2, low.shape[1]), bf16)
+    out = [like((rows, low.shape[1]), f32), piece, piece]
+    return call(forward_kernel, out, order_cost, 1)(low, high)
 
 
 def scalar():
@@ -325,11 +330,10 @@
     xn_own, c_slots = lax.optimization_barrier((xn_own, c_slots))
     xn_low, xn_high = shift(xn_own, "x", 1), shift(xn_own, "x", -1)
     c_own = exchange(c_slots)
-    c_own, seen = lax.optimization_barrier(
-        (c_own, zeros_after(experts + 1, xn_low, xn_high))
-    )
+    seen, from_low, from_high = forward_halves(experts + 1, xn_low, xn_high)
+    c_own, seen = lax.optimization_barrier((c_own, seen))
     c_low, c_high = shift(c_own, "x", 1), shift(c_own, "x", -1)
-    xn_far = [shift(xn_low[:half], "x", 1), shift(xn_high[half:], "x", -1)]
+    xn_far = [shift(from_low, "x", 1), shift(from_high, "x", -1)]
     h_own, d_own, part, (b_own,) = run_experts(
         mine, up, down, router, seen, [xn_own], [c_own], 1
     )

time: 155 us -> 156 us (level)
  the two profiles are of different devices: /device:TPU:64 before, /device:TPU:75 now
where the time goes in v5:
time: 156 us
  starting transfers between devices  55.3 us (35%)
  waiting for transfers between devices  49 us (31%)
  Pallas kernels  42.8 us (27%)
  local copies, waits for them, and re-layouts  4.98 us (3%)
  other arithmetic  2.85 us (2%)
    all_to_all x3, starting transfers between devices, exchange(): return lax.all_to_all(shaped, 'e', 0, 0, tiled=True).reshape(rows.shape)  29.7 us
    ppermute x11, waiting for transfers between devices, shift(): lax.ppermute(value, axis, [(i, (i + steps) % count) for i in range(count)])  29.4 us
    pallas_call x3, Pallas kernels, run_experts(): call(functools.partial(expert_kernel, len(xns)), [like((total, hid), bf16...  22.5 us
    ppermute x11, starting transfers between devices, shift(): lax.ppermute(value, axis, [(i, (i + steps) % count) for i in range(count)])  12.1 us
    pallas_call x1, Pallas kernels, run_grads(): call(functools.partial(grads_kernel, len(xns), len(cots), len(hs)), [like...  10.3 us
    ppermute x7, starting transfers between devices, swap(): return lax.ppermute(value, axis, [(i, i ^ mask) for i in range(count)])  10.3 us
    ppermute x7, waiting for transfers between devices, swap(): return lax.ppermute(value, axis, [(i, i ^ mask) for i in range(count)])  8.36 us
    ppermute x1, waiting for transfers between devices, shards(): lax.ppermute(upstream_grad[0], 'segment', [(i + 1, i) for i in range(n_se...  8.06 us
  transfers between devices with their start and end apart: 22, of which 13 were waited for; matrix products, arithmetic and copies ran while one was open for 3% of the time, Pallas kernels for 24%

profile of v5, /device:TPU:75, one launch (start us, length us, event | category | flops | bytes accessed | tf_op | source)
XLA Modules:
  0.0 155.7 jit_solution(3354410329356017664)
XLA Ops:
  0.7 2.5 %shard_map.128 = (bf16[256,1536]{1,0:T(8,128)(2,1)}, bf16[256,128]{1,0:T(8,128)(2,1)}, bf16[256,128]{1,0:T(8,128)(2,1)}, bf16[128,256]{1,0:T(8,128)(2,1)}) custom-call(bf16[128,1536]{1,0:T(8,128)(2,1)} %bitcast.35, f32[1,1536]{1,0:T(1,128)} %gain_ref.3, bf16[8,1536]{1,0:T(8,128)(2,1)} %bitcast.40, s32[2,128]{1,0:T(2,128)} %bitcast.44), custom_call_target="tpu_custom_call" | custom-call | flops 100663296 | bytes 1572864 | tf_op jit(solution)/shard_map/pallas_call | solution.py:303
  3.2 5.7 %all-to-all-start = ((bf16[8,32,1536]{2,1,0:T(8,128)(2,1)}), bf16[8,32,1536]{2,1,0:T(8,128)(2,1)S(1)}, u32[]{:S(2)}, u32[]{:S(2)}) async-start(bf16[8,32,1536]{2,1,0:T(8,128)(2,1)} %bitcast.38), calls=%async_computation | async-start | bytes 1572864 | tf_op jit(solution)/shard_map/all_to_all | solution.py:319
  8.9 3.1 %collective-permute-start = (bf16[128,1536]{1,0:T(8,128)(2,1)S(1)}, bf16[128,1536]{1,0:T(8,128)(2,1)S(1)}, u32[]{:S(2)}, u32[]{:S(2)}) collective-permute-start(bf16[128,1536]{1,0:T(8,128)(2,1)S(1)} %bitcast.54), channel_id=1, source_target_pairs={{32,0},{64,32},{96,64},{128,96},{160,128},{192,160},{224,192},{33,... | collective-permute-start | bytes 1179656 | tf_op jit(solution)/shard_map/ppermute | solution.py:314
  12.1 0.7 copy.14.rewards_ref
  12.8 8.1 %collective-permute-done.arrived_ref = bf16[128,1536]{1,0:T(8,128)(2,1)S(1)} collective-permute-done((bf16[128,1536]{1,0:T(8,128)(2,1)S(1)}, bf16[128,1536]{1,0:T(8,128)(2,1)S(1)}, u32[]{:S(2)}, u32[]{:S(2)}) %collective-permute-start) | collective-permute-done | bytes 393248 | tf_op jit(solution)/shard_map/ppermute | solution.py:314
  20.9 0.7 copy-done.11
  21.6 2.5 %shard_map.129 = (bf16[128,1536]{1,0:T(8,128)(2,1)}, bf16[256,1664]{1,0:T(8,128)(2,1)}) custom-call(s32[1]{0:T(128)} %bitcast.1.last_ref, bf16[128,1536]{1,0:T(8,128)(2,1)} %copy-done.11, bf16[128,1536]{1,0:T(8,128)(2,1)} %noise_ref.1, f32[128,1]{1,0:T(8,128)} %copy.14.rewards_ref, bf16[256,128]{1,0:T(8,128)(2,1)} %get-tuple-element.40.pick_ref, ...), custom_call_target="tpu_custom_call" | custom-call | flops 100663296 | bytes 1966080 | tf_op jit(solution)/shard_map/pallas_call | solution.py:322
  24.1 0.0 all-to-all-done
  24.1 1.2 collective-permute-start.1
  25.4 0.3 collective-permute-start.2
  25.6 14.5 %all-to-all-start.1 = ((bf16[8,32,1664]{2,1,0:T(8,128)(2,1)}), bf16[8,32,1664]{2,1,0:T(8,128)(2,1)S(1)}, u32[]{:S(2)}, u32[]{:S(2)}) async-start(bf16[8,32,1664]{2,1,0:T(8,128)(2,1)} %bitcast.37), calls=%async_computation.1 | async-start | bytes 1703936 | tf_op jit(solution)/shard_map/all_to_all | solution.py:319
  40.1 2.7 %collective-permute-done.1.low_ref.refs_0_.refs_1_ = bf16[256,1536]{1,0:T(8,128)(2,1)S(1)} collective-permute-done((bf16[256,1536]{1,0:T(8,128)(2,1)S(1)}, bf16[256,1536]{1,0:T(8,128)(2,1)S(1)}, u32[]{:S(2)}, u32[]{:S(2)}) %collective-permute-start.1) | collective-permute-done | bytes 786464 | tf_op jit(solution)/shard_map/ppermute | solution.py:23
  42.8 0.9 collective-permute-done.2.high_ref.refs_1_.refs_2_
  43.7 0.9 copy-done.6
  44.6 2.3 %shard_map.130 = (f32[9,1536]{1,0:T(8,128)}, bf16[128,1536]{1,0:T(8,128)(2,1)}, bf16[128,1536]{1,0:T(8,128)(2,1)}) custom-call(bf16[256,1536]{1,0:T(8,128)(2,1)} %copy-done.5, bf16[256,1536]{1,0:T(8,128)(2,1)} %copy-done.6), custom_call_target="tpu_custom_call" | custom-call | flops 10000000000 | bytes 1 | tf_op jit(solution)/shard_map/pallas_call | solution.py:77
  46.9 3.2 %all-to-all-done.1 = bf16[8,32,1664]{2,1,0:T(8,128)(2,1)S(1)} async-done(((bf16[8,32,1664]{2,1,0:T(8,128)(2,1)}), bf16[8,32,1664]{2,1,0:T(8,128)(2,1)S(1)}, u32[]{:S(2)}, u32[]{:S(2)}) %all-to-all-start.1) | async-done | bytes 852000 | tf_op jit(solution)/shard_map/all_to_all | solution.py:319
  50.1 1.2 collective-permute-start.3
  51.4 0.3 collective-permute-start.4
  51.6 1.2 collective-permute-start.5
  52.8 1.5 collective-permute-start.6
  54.3 0.0 copy-done
  54.3 6.5 %shard_map.131 = (bf16[256,768]{1,0:T(8,128)(2,1)}, bf16[256,768]{1,0:T(8,128)(2,1)}, f32[9,1536]{1,0:T(8,128)}, bf16[256,1536]{1,0:T(8,128)(2,1)}) custom-call(s32[1]{0:T(128)} %bitcast.12.mine_ref, bf16[1536,768]{1,0:T(8,128)(2,1)} %bitcast.46, bf16[768,1536]{1,0:T(8,128)(2,1)} %bitcast.49, bf16[8,1536]{1,0:T(8,128)(2,1)} %bitcast.41, ...), custom_call_target="tpu_custom_call" | custom-call | flops 1811939328 | bytes 7864320 | tf_op jit(solution)/shard_map/pallas_call | solution.py:219
  60.8 10.5 %collective-permute-done.3.refs_2_.refs_6_ = bf16[256,1664]{1,0:T(8,128)(2,1)S(1)} collective-permute-done((bf16[256,1664]{1,0:T(8,128)(2,1)S(1)}, bf16[256,1664]{1,0:T(8,128)(2,1)S(1)}, u32[]{:S(2)}, u32[]{:S(2)}) %collective-permute-start.3) | collective-permute-done | bytes 852000 | tf_op jit(solution)/shard_map/ppermute | solution.py:23
  71.2 1.2 collective-permute-done.4.refs_3_.refs_7_
  72.5 0.9 collective-permute-start.7
  73.4 0.9 collective-permute-start.8
  74.3 5.2 %collective-permute-done.5.refs_0_.refs_3_ = bf16[128,1536]{1,0:T(8,128)(2,1)S(1)} collective-permute-done((bf16[128,1536]{1,0:T(8,128)(2,1)}, bf16[128,1536]{1,0:T(8,128)(2,1)S(1)}, u32[]{:S(2)}, u32[]{:S(2)}) %collective-permute-start.5) | collective-permute-done | bytes 393248 | tf_op jit(solution)/shard_map/ppermute | solution.py:23
  79.6 1.2 collective-permute-done.6.refs_1_.refs_4_
  80.8 9.4 %shard_map.132 = (bf16[512,768]{1,0:T(8,128)(2,1)}, bf16[512,768]{1,0:T(8,128)(2,1)}, f32[9,1536]{1,0:T(8,128)}, bf16[256,1536]{1,0:T(8,128)(2,1)}, bf16[256,1536]{1,0:T(8,128)(2,1)}) custom-call(s32[1]{0:T(128)} %bitcast.12.mine_ref, bf16[1536,768]{1,0:T(8,128)(2,1)} %bitcast.47, bf16[768,1536]{1,0:T(8,128)(2,1)} %bitcast.50, bf16[8,1536]{1,0:T(8,128)(2,1)} %bitcast.42, ...), custom_call_target="tpu_custom_call" | custom-call | flops 3623878656 | bytes 11010048 | tf_op jit(solution)/shard_map/pallas_call | solution.py:219
  90.2 0.0 copy-done.10
  90.2 0.8 collective-permute-start.11
  91.0 0.9 collective-permute-start.10
  91.9 0.0 collective-permute-done.7.refs_2_.refs_8_
  91.9 0.0 collective-permute-done.8.refs_3_.refs_9_
  91.9 0.8 copy-done.8
  92.8 0.2 copy-done.9
  92.9 6.6 %shard_map.133 = (bf16[256,768]{1,0:T(8,128)(2,1)}, bf16[256,768]{1,0:T(8,128)(2,1)}, f32[9,1536]{1,0:T(8,128)}, bf16[256,1536]{1,0:T(8,128)(2,1)}) custom-call(s32[1]{0:T(128)} %bitcast.12.mine_ref, bf16[1536,768]{1,0:T(8,128)(2,1)} %bitcast.48, bf16[768,1536]{1,0:T(8,128)(2,1)} %bitcast.51, bf16[8,1536]{1,0:T(8,128)(2,1)} %bitcast.43, ...), custom_call_target="tpu_custom_call" | custom-call | flops 1811939328 | bytes 7864320 | tf_op jit(solution)/shard_map/pallas_call | solution.py:219
  99.6 3.0 %collective-permute-start.9 = (bf16[256,1536]{1,0:T(8,128)(2,1)}, bf16[256,1536]{1,0:T(8,128)(2,1)S(1)}, u32[]{:S(2)}, u32[]{:S(2)}) collective-permute-start(bf16[256,1536]{1,0:T(8,128)(2,1)} %get-tuple-element.62), channel_id=1, source_target_pairs={{0,2},{1,3},{2,0},{3,1},{4,6},{5,7},{6,4},{7,5},{8,10},{9,11},{10,... | collective-permute-start | bytes 2359304 | tf_op jit(solution)/shard_map/ppermute | solution.py:23
  102.6 5.1 %collective-permute-start.12 = (f32[9,1536]{1,0:T(8,128)}, f32[9,1536]{1,0:T(8,128)S(1)}, u32[]{:S(2)}, u32[]{:S(2)}) collective-permute-start(f32[9,1536]{1,0:T(8,128)} %get-tuple-element.74), channel_id=1, source_target_pairs={{0,4},{4,0},{8,12},{12,8},{16,20},{20,16},{24,28},{28,24},{1,5},{5... | collective-permute-start | bytes 165896 | tf_op jit(solution)/shard_map/ppermute | solution.py:28
  107.7 2.2 %collective-permute-done.12 = f32[9,1536]{1,0:T(8,128)S(1)} collective-permute-done((f32[9,1536]{1,0:T(8,128)}, f32[9,1536]{1,0:T(8,128)S(1)}, u32[]{:S(2)}, u32[]{:S(2)}) %collective-permute-start.12) | collective-permute-done | bytes 55328 | tf_op jit(solution)/shard_map/ppermute | solution.py:28
  109.9 0.9 add.33
  110.8 0.7 collective-permute-start.14
  111.5 1.8 %collective-permute-start.15 = (f32[9,1536]{1,0:T(8,128)S(1)}, f32[9,1536]{1,0:T(8,128)S(1)}, u32[]{:S(2)}, u32[]{:S(2)}) collective-permute-start(f32[9,1536]{1,0:T(8,128)S(1)} %add.33), channel_id=1, source_target_pairs={{0,24},{4,28},{8,16},{12,20},{16,8},{20,12},{24,0},{28,4},{1,25},{... | collective-permute-start | bytes 165896 | tf_op jit(solution)/shard_map/ppermute | solution.py:28
  113.3 1.9 %collective-permute-done.14 = f32[9,1536]{1,0:T(8,128)S(1)} collective-permute-done((f32[9,1536]{1,0:T(8,128)S(1)}, f32[9,1536]{1,0:T(8,128)S(1)}, u32[]{:S(2)}, u32[]{:S(2)}) %collective-permute-start.14) | collective-permute-done | bytes 55328 | tf_op jit(solution)/shard_map/ppermute | solution.py:28
  115.2 1.8 %collective-permute-start.13 = (f32[9,1536]{1,0:T(8,128)S(1)}, f32[9,1536]{1,0:T(8,128)S(1)}, u32[]{:S(2)}, u32[]{:S(2)}) collective-permute-start(f32[9,1536]{1,0:T(8,128)S(1)} %add.33), channel_id=1, source_target_pairs={{0,16},{4,20},{8,24},{12,28},{16,0},{20,4},{24,8},{28,12},{1,17},{... | collective-permute-start | bytes 165896 | tf_op jit(solution)/shard_map/ppermute | solution.py:28
  117.0 0.0 collective-permute-done.15
  117.0 4.2 %collective-permute-done.13 = f32[9,1536]{1,0:T(8,128)S(1)} collective-permute-done((f32[9,1536]{1,0:T(8,128)S(1)}, f32[9,1536]{1,0:T(8,128)S(1)}, u32[]{:S(2)}, u32[]{:S(2)}) %collective-permute-start.13) | collective-permute-done | bytes 55328 | tf_op jit(solution)/shard_map/ppermute | solution.py:28
  121.2 0.7 collective-permute-start.17
  121.9 0.3 collective-permute-start.18
  122.2 3.2 %collective-permute-done.11 = bf16[256,1536]{1,0:T(8,128)(2,1)S(1)} collective-permute-done((bf16[256,1536]{1,0:T(8,128)(2,1)}, bf16[256,1536]{1,0:T(8,128)(2,1)S(1)}, u32[]{:S(2)}, u32[]{:S(2)}) %collective-permute-start.11) | collective-permute-done | bytes 786464 | tf_op jit(solution)/shard_map/ppermute | solution.py:23
  125.4 0.0 collective-permute-start.16
  125.4 0.0 collective-permute-done.10
  125.4 4.4 %collective-permute-done.9 = bf16[256,1536]{1,0:T(8,128)(2,1)S(1)} collective-permute-done((bf16[256,1536]{1,0:T(8,128)(2,1)}, bf16[256,1536]{1,0:T(8,128)(2,1)S(1)}, u32[]{:S(2)}, u32[]{:S(2)}) %collective-permute-start.9) | collective-permute-done | bytes 786464 | tf_op jit(solution)/shard_map/ppermute | solution.py:23
  129.8 1.3 add_convert_fusion
  131.1 9.5 %all-to-all-start.2 = ((bf16[8,32,1536]{2,1,0:T(8,128)(2,1)}), bf16[8,32,1536]{2,1,0:T(8,128)(2,1)S(1)}, u32[]{:S(2)}, u32[]{:S(2)}) async-start(bf16[8,32,1536]{2,1,0:T(8,128)(2,1)} %bitcast.16), calls=%async_computation.2 | async-start | bytes 1572864 | tf_op jit(solution)/shard_map/all_to_all | solution.py:319
  140.5 10.3 %shard_map.135 = (bf16[1536,768]{1,0:T(8,128)(2,1)}, bf16[768,1536]{1,0:T(8,128)(2,1)}) custom-call(bf16[256,1536]{1,0:T(8,128)(2,1)} %bitcast.33, bf16[256,1536]{1,0:T(8,128)(2,1)} %copy-done.5, bf16[256,1536]{1,0:T(8,128)(2,1)} %copy-done.6, bf16[128,1536]{1,0:T(8,128)(2,1)} %copy-done.10, bf16[128,1536]{1,0:T(8,128)(2,1)} %collective-permute-done.6.refs_1_.refs_4_, ...), custom_call_target="tpu_custom_call" | custom-call | flops 48318384 | bytes 141557 | tf_op jit(solution)/shard_map/pallas_call | solution.py:250
  150.9 0.0 collective-permute-done.17
  150.9 0.0 collective-permute-done.18
  150.9 0.0 collective-permute-done.16
  151.0 0.6 slice_divide_fusion
  151.6 0.6 slice_bitcast_fusion
  152.2 0.0 all-to-all-done.2
  152.2 0.9 copy-done.2
  153.1 2.6 %shard_map.134 = bf16[128,1536]{1,0:T(8,128)(2,1)} custom-call(bf16[128,1536]{1,0:T(8,128)(2,1)} %bitcast.36, f32[1,1536]{1,0:T(1,128)} %gain_ref.3, bf16[128,1536]{1,0:T(8,128)(2,1)} %get-tuple-element.42.cot_ref, bf16[256,1536]{1,0:T(8,128)(2,1)} %bitcast.34, bf16[128,256]{1,0:T(8,128)(2,1)} %get-tuple-element.65.back_ref), custom_call_target="tpu_custom_call" | custom-call | flops 100663296 | bytes 2359296 | tf_op jit(solution)/shard_map/pallas_call | solution.py:366
  (27 shorter events, 0.2 us)
Async XLA Ops:
  0.6 8.3 %copy-start.14 = (bf16[1,128,1536]{2,1,0:T(8,128)(2,1)S(1)}, bf16[1,128,1536]{2,1,0:T(8,128)(2,1)}, u32[]{:S(2)}) copy-start(bf16[1,128,1536]{2,1,0:T(8,128)(2,1)} %param.10) | copy-start | bytes 1179652
  0.6 11.4 %copy-start.13 = (f32[128]{0:T(128)S(1)}, f32[128]{0:T(128)}, u32[]{:S(2)}) copy-start(f32[128]{0:T(128)} %param.12) | copy-start | bytes 1540
  3.2 20.9 %all-to-all-start = ((bf16[8,32,1536]{2,1,0:T(8,128)(2,1)}), bf16[8,32,1536]{2,1,0:T(8,128)(2,1)S(1)}, u32[]{:S(2)}, u32[]{:S(2)}) async-start(bf16[8,32,1536]{2,1,0:T(8,128)(2,1)} %bitcast.38), calls=%async_computation | async-start | bytes 1572864 | tf_op jit(solution)/shard_map/all_to_all | solution.py:319
  8.9 12.0 %collective-permute-start = (bf16[128,1536]{1,0:T(8,128)(2,1)S(1)}, bf16[128,1536]{1,0:T(8,128)(2,1)S(1)}, u32[]{:S(2)}, u32[]{:S(2)}) collective-permute-start(bf16[128,1536]{1,0:T(8,128)(2,1)S(1)} %bitcast.54), channel_id=1, source_target_pairs={{32,0},{64,32},{96,64},{128,96},{160,128},{192,160},{224,192},{33,... | collective-permute-start | bytes 1179656 | tf_op jit(solution)/shard_map/ppermute | solution.py:314
  20.9 0.7 copy-start.11
  24.1 22.8 %copy-start.1 = (bf16[8,32,1536]{2,1,0:T(8,128)(2,1)}, bf16[8,32,1536]{2,1,0:T(8,128)(2,1)S(1)}, u32[]{:S(2)}) copy-start(bf16[8,32,1536]{2,1,0:T(8,128)(2,1)S(1)} %all-to-all-done) | copy-start | bytes 2359300
  24.1 18.7 %collective-permute-start.1 = (bf16[256,1536]{1,0:T(8,128)(2,1)S(1)}, bf16[256,1536]{1,0:T(8,128)(2,1)S(1)}, u32[]{:S(2)}, u32[]{:S(2)}) collective-permute-start(bf16[256,1536]{1,0:T(8,128)(2,1)S(1)} %bitcast.30), channel_id=1, source_target_pairs={{0,1},{1,2},{2,3},{3,0},{4,5},{5,6},{6,7},{7,4},{8,9},{9,10},{10,1... | collective-permute-start | bytes 2359304 | tf_op jit(solution)/shard_map/ppermute | solution.py:23
  25.4 18.4 %collective-permute-start.2 = (bf16[256,1536]{1,0:T(8,128)(2,1)S(1)}, bf16[256,1536]{1,0:T(8,128)(2,1)S(1)}, u32[]{:S(2)}, u32[]{:S(2)}) collective-permute-start(bf16[256,1536]{1,0:T(8,128)(2,1)S(1)} %bitcast.31), channel_id=1, source_target_pairs={{0,3},{1,0},{2,1},{3,2},{4,7},{5,4},{6,5},{7,6},{8,11},{9,8},{10,9... | collective-permute-start | bytes 2359304 | tf_op jit(solution)/shard_map/ppermute | solution.py:23
  25.6 24.5 %all-to-all-start.1 = ((bf16[8,32,1664]{2,1,0:T(8,128)(2,1)}), bf16[8,32,1664]{2,1,0:T(8,128)(2,1)S(1)}, u32[]{:S(2)}, u32[]{:S(2)}) async-start(bf16[8,32,1664]{2,1,0:T(8,128)(2,1)} %bitcast.37), calls=%async_computation.1 | async-start | bytes 1703936 | tf_op jit(solution)/shard_map/all_to_all | solution.py:319
  42.8 0.9 copy-start.5
  43.7 0.9 copy-start.6
  50.1 4.2 %copy-start = (bf16[8,32,1664]{2,1,0:T(8,128)(2,1)}, bf16[8,32,1664]{2,1,0:T(8,128)(2,1)S(1)}, u32[]{:S(2)}) copy-start(bf16[8,32,1664]{2,1,0:T(8,128)(2,1)S(1)} %all-to-all-done.1) | copy-start | bytes 2555908
  50.1 21.1 %collective-permute-start.3 = (bf16[256,1664]{1,0:T(8,128)(2,1)S(1)}, bf16[256,1664]{1,0:T(8,128)(2,1)S(1)}, u32[]{:S(2)}, u32[]{:S(2)}) collective-permute-start(bf16[256,1664]{1,0:T(8,128)(2,1)S(1)} %bitcast.26), channel_id=1, source_target_pairs={{0,1},{1,2},{2,3},{3,0},{4,5},{5,6},{6,7},{7,4},{8,9},{9,10},{10,1... | collective-permute-start | bytes 2555912 | tf_op jit(solution)/shard_map/ppermute | solution.py:23
  51.4 21.1 %collective-permute-start.4 = (bf16[256,1664]{1,0:T(8,128)(2,1)S(1)}, bf16[256,1664]{1,0:T(8,128)(2,1)S(1)}, u32[]{:S(2)}, u32[]{:S(2)}) collective-permute-start(bf16[256,1664]{1,0:T(8,128)(2,1)S(1)} %bitcast.27), channel_id=1, source_target_pairs={{0,3},{1,0},{2,1},{3,2},{4,7},{5,4},{6,5},{7,6},{8,11},{9,8},{10,9... | collective-permute-start | bytes 2555912 | tf_op jit(solution)/shard_map/ppermute | solution.py:23
  51.6 27.9 %collective-permute-start.5 = (bf16[128,1536]{1,0:T(8,128)(2,1)}, bf16[128,1536]{1,0:T(8,128)(2,1)S(1)}, u32[]{:S(2)}, u32[]{:S(2)}) collective-permute-start(bf16[128,1536]{1,0:T(8,128)(2,1)} %get-tuple-element.53), channel_id=1, source_target_pairs={{0,1},{1,2},{2,3},{3,0},{4,5},{5,6},{6,7},{7,4},{8,9},{9,10},{10,1... | collective-permute-start | bytes 1179656 | tf_op jit(solution)/shard_map/ppermute | solution.py:23
  52.8 27.9 %collective-permute-start.6 = (bf16[128,1536]{1,0:T(8,128)(2,1)}, bf16[128,1536]{1,0:T(8,128)(2,1)}, u32[]{:S(2)}, u32[]{:S(2)}) collective-permute-start(bf16[128,1536]{1,0:T(8,128)(2,1)} %get-tuple-element.54), channel_id=1, source_target_pairs={{0,3},{1,0},{2,1},{3,2},{4,7},{5,4},{6,5},{7,6},{8,11},{9,8},{10,9... | collective-permute-start | bytes 1179656 | tf_op jit(solution)/shard_map/ppermute | solution.py:23
  71.2 9.5 %copy-start.3 = (bf16[256,1664]{1,0:T(8,128)(2,1)}, bf16[256,1664]{1,0:T(8,128)(2,1)S(1)}, u32[]{:S(2)}) copy-start(bf16[256,1664]{1,0:T(8,128)(2,1)S(1)} %collective-permute-done.3.refs_2_.refs_6_) | copy-start | bytes 2555908
  72.4 8.3 %copy-start.4 = (bf16[256,1664]{1,0:T(8,128)(2,1)}, bf16[256,1664]{1,0:T(8,128)(2,1)S(1)}, u32[]{:S(2)}) copy-start(bf16[256,1664]{1,0:T(8,128)(2,1)S(1)} %collective-permute-done.4.refs_3_.refs_7_) | copy-start | bytes 2555908
  72.5 19.5 %collective-permute-start.7 = (bf16[128,1664]{1,0:T(8,128)(2,1)S(1)}, bf16[128,1664]{1,0:T(8,128)(2,1)S(1)}, u32[]{:S(2)}, u32[]{:S(2)}) collective-permute-start(bf16[128,1664]{1,0:T(8,128)(2,1)S(1)} %slice.12), channel_id=1, source_target_pairs={{0,1},{1,2},{2,3},{3,0},{4,5},{5,6},{6,7},{7,4},{8,9},{9,10},{10,1... | collective-permute-start | bytes 1277960 | tf_op jit(solution)/shard_map/ppermute | solution.py:23
  73.4 18.5 %collective-permute-start.8 = (bf16[128,1664]{1,0:T(8,128)(2,1)S(1)}, bf16[128,1664]{1,0:T(8,128)(2,1)S(1)}, u32[]{:S(2)}, u32[]{:S(2)}) collective-permute-start(bf16[128,1664]{1,0:T(8,128)(2,1)S(1)} %slice.13), channel_id=1, source_target_pairs={{0,3},{1,0},{2,1},{3,2},{4,7},{5,4},{6,5},{7,6},{8,11},{9,8},{10,9... | collective-permute-start | bytes 1277960 | tf_op jit(solution)/shard_map/ppermute | solution.py:23
  79.5 10.6 %copy-start.10 = (bf16[128,1536]{1,0:T(8,128)(2,1)}, bf16[128,1536]{1,0:T(8,128)(2,1)S(1)}, u32[]{:S(2)}) copy-start(bf16[128,1536]{1,0:T(8,128)(2,1)S(1)} %collective-permute-done.5.refs_0_.refs_3_) | copy-start | bytes 1179652
  90.2 35.2 %collective-permute-start.11 = (bf16[256,1536]{1,0:T(8,128)(2,1)}, bf16[256,1536]{1,0:T(8,128)(2,1)S(1)}, u32[]{:S(2)}, u32[]{:S(2)}) collective-permute-start(bf16[256,1536]{1,0:T(8,128)(2,1)} %get-tuple-element.64), channel_id=1, source_target_pairs={{0,1},{1,2},{2,3},{3,0},{4,5},{5,6},{6,7},{7,4},{8,9},{9,10},{10,1... | collective-permute-start | bytes 2359304 | tf_op jit(solution)/shard_map/ppermute | solution.py:23
  91.0 34.4 %collective-permute-start.10 = (bf16[256,1536]{1,0:T(8,128)(2,1)}, bf16[256,1536]{1,0:T(8,128)(2,1)S(1)}, u32[]{:S(2)}, u32[]{:S(2)}) collective-permute-start(bf16[256,1536]{1,0:T(8,128)(2,1)} %get-tuple-element.63), channel_id=1, source_target_pairs={{0,3},{1,0},{2,1},{3,2},{4,7},{5,4},{6,5},{7,6},{8,11},{9,8},{10,9... | collective-permute-start | bytes 2359304 | tf_op jit(solution)/shard_map/ppermute | solution.py:23
  91.9 0.8 copy-start.8
  91.9 1.0 copy-start.9
  92.9 36.9 %copy-start.7 = (bf16[256,1536]{1,0:T(8,128)(2,1)S(1)}, bf16[256,1536]{1,0:T(8,128)(2,1)}, u32[]{:S(2)}) copy-start(bf16[256,1536]{1,0:T(8,128)(2,1)} %get-tuple-element.51) | copy-start | bytes 2359300
  99.6 30.2 %collective-permute-start.9 = (bf16[256,1536]{1,0:T(8,128)(2,1)}, bf16[256,1536]{1,0:T(8,128)(2,1)S(1)}, u32[]{:S(2)}, u32[]{:S(2)}) collective-permute-start(bf16[256,1536]{1,0:T(8,128)(2,1)} %get-tuple-element.62), channel_id=1, source_target_pairs={{0,2},{1,3},{2,0},{3,1},{4,6},{5,7},{6,4},{7,5},{8,10},{9,11},{10,... | collective-permute-start | bytes 2359304 | tf_op jit(solution)/shard_map/ppermute | solution.py:23
  102.6 7.3 %collective-permute-start.12 = (f32[9,1536]{1,0:T(8,128)}, f32[9,1536]{1,0:T(8,128)S(1)}, u32[]{:S(2)}, u32[]{:S(2)}) collective-permute-start(f32[9,1536]{1,0:T(8,128)} %get-tuple-element.74), channel_id=1, source_target_pairs={{0,4},{4,0},{8,12},{12,8},{16,20},{20,16},{24,28},{28,24},{1,5},{5... | collective-permute-start | bytes 165896 | tf_op jit(solution)/shard_map/ppermute | solution.py:28
  110.8 4.4 %collective-permute-start.14 = (f32[9,1536]{1,0:T(8,128)S(1)}, f32[9,1536]{1,0:T(8,128)S(1)}, u32[]{:S(2)}, u32[]{:S(2)}) collective-permute-start(f32[9,1536]{1,0:T(8,128)S(1)} %add.33), channel_id=1, source_target_pairs={{0,8},{4,12},{8,0},{12,4},{16,24},{20,28},{24,16},{28,20},{1,9},{5... | collective-permute-start | bytes 165896 | tf_op jit(solution)/shard_map/ppermute | solution.py:28
  111.5 5.5 %collective-permute-start.15 = (f32[9,1536]{1,0:T(8,128)S(1)}, f32[9,1536]{1,0:T(8,128)S(1)}, u32[]{:S(2)}, u32[]{:S(2)}) collective-permute-start(f32[9,1536]{1,0:T(8,128)S(1)} %add.33), channel_id=1, source_target_pairs={{0,24},{4,28},{8,16},{12,20},{16,8},{20,12},{24,0},{28,4},{1,25},{... | collective-permute-start | bytes 165896 | tf_op jit(solution)/shard_map/ppermute | solution.py:28
  115.2 6.0 %collective-permute-start.13 = (f32[9,1536]{1,0:T(8,128)S(1)}, f32[9,1536]{1,0:T(8,128)S(1)}, u32[]{:S(2)}, u32[]{:S(2)}) collective-permute-start(f32[9,1536]{1,0:T(8,128)S(1)} %add.33), channel_id=1, source_target_pairs={{0,16},{4,20},{8,24},{12,28},{16,0},{20,4},{24,8},{28,12},{1,17},{... | collective-permute-start | bytes 165896 | tf_op jit(solution)/shard_map/ppermute | solution.py:28
  121.2 29.7 %collective-permute-start.17 = (f32[9,1536]{1,0:T(8,128)S(1)}, f32[9,1536]{1,0:T(8,128)S(1)}, u32[]{:S(2)}, u32[]{:S(2)}) collective-permute-start(f32[9,1536]{1,0:T(8,128)S(1)} %add_add_fusion.1), channel_id=1, source_target_pairs={{0,1},{1,0},{2,3},{3,2},{4,5},{5,4},{6,7},{7,6},{8,9},{9,8},{10,11... | collective-permute-start | bytes 165896 | tf_op jit(solution)/shard_map/ppermute | solution.py:28
  121.9 29.0 %collective-permute-start.18 = (f32[9,1536]{1,0:T(8,128)S(1)}, f32[9,1536]{1,0:T(8,128)S(1)}, u32[]{:S(2)}, u32[]{:S(2)}) collective-permute-start(f32[9,1536]{1,0:T(8,128)S(1)} %add_add_fusion.1), channel_id=1, source_target_pairs={{0,3},{1,2},{2,1},{3,0},{4,7},{5,6},{6,5},{7,4},{8,11},{9,10},{10,... | collective-permute-start | bytes 165896 | tf_op jit(solution)/shard_map/ppermute | solution.py:28
  125.4 25.5 %collective-permute-start.16 = (f32[9,1536]{1,0:T(8,128)S(1)}, f32[9,1536]{1,0:T(8,128)S(1)}, u32[]{:S(2)}, u32[]{:S(2)}) collective-permute-start(f32[9,1536]{1,0:T(8,128)S(1)} %add_add_fusion.1), channel_id=1, source_target_pairs={{0,2},{1,3},{2,0},{3,1},{4,6},{5,7},{6,4},{7,5},{8,10},{9,11},{10,... | collective-permute-start | bytes 165896 | tf_op jit(solution)/shard_map/ppermute | solution.py:28
  131.1 21.1 %all-to-all-start.2 = ((bf16[8,32,1536]{2,1,0:T(8,128)(2,1)}), bf16[8,32,1536]{2,1,0:T(8,128)(2,1)S(1)}, u32[]{:S(2)}, u32[]{:S(2)}) async-start(bf16[8,32,1536]{2,1,0:T(8,128)(2,1)} %bitcast.16), calls=%async_computation.2 | async-start | bytes 1572864 | tf_op jit(solution)/shard_map/all_to_all | solution.py:319
  140.5 10.4 %copy-start.12 = (f32[1,1536]{1,0:T(1,128)S(1)}, f32[1,1536]{1,0:T(1,128)}, u32[]{:S(2)}) copy-start(f32[1,1536]{1,0:T(1,128)} %gain_ref.3) | copy-start | bytes 18436
  152.2 0.9 copy-start.2
